TPU v7x, 128 devices: a whole 4x4x4 slice. The times are simulated.
128 devices in a mesh: view: 16 (over x_hi, z, core), head: 8 (over y, x_lo).
Axes of the slice: x: 4 (x_hi: 2, x_lo: 2; x = x_hi * 2 + x_lo), y: 4, z: 4, core: 2. Of those that a mesh axis runs over, the one named last changes fastest.
Arguments:
- x_tokens: bfloat16 [8192, 3072], P('view'), may hold values from -14 to 14
- w_qkv: bfloat16 [3072, 3, 3072], P(None, None, 'head'), may hold values from -0.109375 to 0.109375
- w_out: bfloat16 [3072, 3072], P(None, 'head'), may hold values from -0.109375 to 0.109375
- grad_out: bfloat16 [8192, 3072], P('view'), may hold values from -1.5 to 1.5
Outputs:
- mixed_out: bfloat16 [8192, 3072], P('view')
- d_input: bfloat16 [8192, 3072], P('view')
- d_w_qkv: float32 [3072, 3, 3072], P('view', None, 'head')
- d_w_out: float32 [3072, 3072], P('view', 'head')
All inputs are finite; a program needn't handle non-finite values.
Results may differ from a plain program's by a relative error of at most 0.02.
The roundings to bfloat16 on the way count: a program that leaves them out, or rounds other values in their place, can miss the bound.
Values may be sent and summed in bfloat16 or wider, within the bound.
No kernel may reach another device: no remote copies, remote signals or barrier semaphores. Data moves between devices by JAX's collectives and lax.ppermute only.
A program may use at most 192 MiB of HBM per device.

v0:
```python
import math

import jax
import jax.numpy as jnp
from jax import lax
from jax.sharding import PartitionSpec as P

D = 3072
HEADS = 24
REACH = 2


def from_behind(block, axis, distance):
    devices = range(lax.axis_size(axis))
    route = [((i - distance) % len(devices), i) for i in devices]
    return lax.ppermute(block, axis, route)


def head_total(partial_term):
    return lax.psum(partial_term.astype(jnp.bfloat16), "head")


def local(x_tokens, w_qkv, w_out, grad_out):
    tokens = x_tokens.shape[0]
    model_width = w_qkv.shape[0]
    local_width = w_qkv.shape[2]
    head_dim = D // HEADS
    heads_here = local_width // head_dim
    score_scale = 1.0 / math.sqrt(head_dim)
    offsets = [offset for offset in range(-REACH, REACH + 1) if offset != 0]
    w_flat = w_qkv.reshape(model_width, 3 * local_width)
    projected = jnp.dot(x_tokens, w_flat, preferred_element_type=jnp.float32).astype(jnp.bfloat16)
    projected = projected.reshape(tokens, 3, local_width)
    queries = projected[:, 0].reshape(tokens, heads_here, head_dim)
    own_pair = projected[:, 1:]
    fetched = {0: own_pair}
    for offset in offsets:
        fetched[offset] = from_behind(own_pair, "view", -offset)
    ordered = jnp.concatenate([fetched[offset] for offset in range(-REACH, REACH + 1)], axis=0)
    key_rows = ordered[:, 0].reshape(-1, heads_here, head_dim)
    value_rows = ordered[:, 1].reshape(-1, heads_here, head_dim)
    scores = (
        jnp.einsum("qhe,khe->hqk", queries, key_rows, preferred_element_type=jnp.float32)
        * score_scale
    )
    soft_weights = jax.nn.softmax(scores, axis=-1)
    rounded = soft_weights.astype(jnp.bfloat16)
    attended = jnp.einsum(
        "hqk,khe->qhe", rounded, value_rows, preferred_element_type=jnp.float32
    ).astype(jnp.bfloat16)
    attended_flat = attended.reshape(tokens, local_width)
    mixed_out = head_total(jnp.dot(attended_flat, w_out.T, preferred_element_type=jnp.float32))
    d_att = jnp.dot(grad_out, w_out, preferred_element_type=jnp.float32).astype(jnp.bfloat16)
    d_rows = d_att.reshape(tokens, heads_here, head_dim)
    d_probs = jnp.einsum("qhe,khe->hqk", d_rows, value_rows, preferred_element_type=jnp.float32)
    row_delta = jnp.sum(soft_weights * d_probs, axis=-1, keepdims=True)
    d_scores = (soft_weights * (d_probs - row_delta) * score_scale).astype(jnp.bfloat16)
    d_query = jnp.einsum(
        "hqk,khe->qhe", d_scores, key_rows, preferred_element_type=jnp.float32
    ).astype(jnp.bfloat16)
    key_span = 2 * REACH + 1
    d_keys = jnp.einsum(
        "hqk,qhe->khe", d_scores, queries, preferred_element_type=jnp.float32
    ).reshape(key_span, tokens, local_width)
    d_values = jnp.einsum(
        "hqk,qhe->khe", rounded, d_rows, preferred_element_type=jnp.float32
    ).reshape(key_span, tokens, local_width)
    pairs = jnp.stack([d_keys, d_values], axis=2)
    summed = pairs[REACH]
    for offset in offsets:
        summed = summed + from_behind(
            pairs[REACH + offset].astype(jnp.bfloat16), "view", offset
        ).astype(jnp.float32)
    d_projected = jnp.stack(
        [
            d_query.reshape(tokens, local_width),
            summed[:, 0].astype(jnp.bfloat16),
            summed[:, 1].astype(jnp.bfloat16),
        ],
        axis=1,
    ).reshape(tokens, 3 * local_width)
    d_input = head_total(jnp.dot(d_projected, w_flat.T, preferred_element_type=jnp.float32))
    row_count = model_width // lax.axis_size("view")
    part_qkv = jnp.dot(x_tokens.T, d_projected, preferred_element_type=jnp.float32).reshape(
        lax.axis_size("view") * row_count, 3, local_width
    )
    part_out = jnp.dot(grad_out.T, attended_flat, preferred_element_type=jnp.float32).reshape(
        lax.axis_size("view") * row_count, 1, local_width
    )
    grads = lax.psum_scatter(
        jnp.concatenate([part_qkv, part_out], axis=1).astype(jnp.bfloat16),
        "view",
        scatter_dimension=0,
        tiled=True,
    ).astype(jnp.float32)
    return (mixed_out, d_input, grads[:, :3], grads[:, 3])


def solution(mesh):
    placed = (P("view", None), P(None, None, "head"), P(None, "head"), P("view", None))
    return jax.shard_map(
        local,
        mesh=mesh,
        in_specs=placed,
        out_specs=(P("view", None), P("view", None), P("view", None, "head"), P("view", "head")),
        check_vma=False,
    )
```

profile of v0, /device:TPU:0, one launch (start us, length us, event | category | flops | bytes accessed | tf_op | source)
XLA Modules:
  0.0 555.1 jit_solution(14087318069062382906)
XLA Ops:
  8.1 10.4 %copy.18 = bf16[3072,3,384]{0,2,1:T(8,128)(2,1)} copy(bf16[3072,3,384]{2,0,1:T(8,128)(2,1)} %param.5) | data formatting | bytes 14155776 | tf_op args[1]
  18.5 8.3 %convolution_convert_fusion.3 = bf16[512,1152]{1,0:T(8,128)(2,1)} fusion(bf16[512,3072]{1,0:T(8,128)(2,1)S(1)} %copy-done, bf16[3072,1152]{0,1:T(8,128)(2,1)} %bitcast.79), kind=kOutput, calls=%fused_computation.27 | convolution fusion | flops 3624468480 | bytes 11403264 | tf_op jit(solution)/shard_map/dot_general | solution.py:32
  32.4 4.7 collective-permute-start.3
  42.7 12.7 %collective-permute-done = bf16[512,2,384]{0,2,1:T(8,128)(2,1)S(1)} collective-permute-done((bf16[512,2,384]{0,2,1:T(8,128)(2,1)S(1)}, bf16[512,2,384]{0,2,1:T(8,128)(2,1)S(1)}, u32[]{:S(2)}, u32[]{:S(2)}) %collective-permute-start) | collective-permute-done | bytes 786464 | tf_op jit(solution)/shard_map/ppermute | solution.py:16
  55.4 7.5 %collective-permute-done.1 = bf16[512,2,384]{0,2,1:T(8,128)(2,1)S(1)} collective-permute-done((bf16[512,2,384]{0,2,1:T(8,128)(2,1)S(1)}, bf16[512,2,384]{0,2,1:T(8,128)(2,1)S(1)}, u32[]{:S(2)}, u32[]{:S(2)}) %collective-permute-start.1) | collective-permute-done | bytes 786464 | tf_op jit(solution)/shard_map/ppermute | solution.py:16
  65.2 7.8 %fusion.45 = f32[3,512,2560]{2,1,0:T(8,128)} fusion(bf16[512,3,128]{0,2,1:T(8,128)(2,1)S(1)} %bitcast.86, bf16[2560,3,128]{0,2,1:T(8,128)(2,1)S(1)} %bitcast.76), kind=kOutput, calls=%fused_computation.57 | convolution fusion | flops 1006632960 | bytes 18087936 | tf_op jit(solution)/shard_map/qhe,khe->hqk/dot_general | solution.py:55
  72.9 11.9 %fusion.44 = (f32[3,512]{1,0:T(4,128)S(1)}, f32[3,512,2560]{2,1,0:T(8,128)}) fusion(bf16[512,3,128]{0,2,1:T(8,128)(2,1)S(1)} %bitcast.83, bf16[2560,3,128]{0,2,1:T(8,128)(2,1)} %bitcast.80), kind=kOutput, calls=%fused_computation.56 | convolution fusion | flops 1018432000 | bytes 18094080 | tf_op jit(solution)/shard_map/sub | solution.py:46
  84.8 8.8 %convolution_bitcast_fusion = f32[2560,3,128]{0,2,1:T(8,128)} fusion(bf16[512,3,128]{0,2,1:T(8,128)(2,1)} %bitcast.87, f32[3,512,2560]{2,1,0:T(8,128)} %get-tuple-element.13, f32[3,512]{1,0:T(4,128)S(1)} %get-tuple-element.12), kind=kOutput, calls=%fused_computation.20 | convolution fusion | flops 1014497280 | bytes 20060160 | tf_op jit(solution)/shard_map/hqk,qhe->khe/dot_general | solution.py:65
  93.6 27.2 %fusion.16 = f32[2560,3,128]{0,2,1:T(8,128)} fusion(bf16[512,3,128]{0,2,1:T(8,128)(2,1)S(1)} %bitcast.84, f32[3,512,2560]{2,1,0:T(8,128)} %fusion.45, f32[3,512,2560]{2,1,0:T(8,128)} %get-tuple-element.13, f32[3,512]{1,0:T(4,128)S(1)} %get-tuple-element.12), kind=kOutput, calls=%fused_computation.19 | convolution fusion | flops 1034162176 | bytes 35788800 | tf_op jit(solution)/shard_map/hqk,qhe->khe/dot_general | solution.py:62
  120.8 6.8 %reshape.47 = f32[5,512,1,384]{1,0,3,2:T(8,128)} reshape(f32[2560,3,128]{0,2,1:T(8,128)} %convolution_bitcast_fusion) | data formatting | bytes 7864320 | tf_op jit(solution)/shard_map/stack;reshape | solution.py:68
  127.6 5.7 %copy.27 = f32[5,512,1,384]{3,1,2,0:T(8,128)} copy(f32[5,512,1,384]{1,0,3,2:T(8,128)} %reshape.47) | data formatting | bytes 7864320 | tf_op jit(solution)/shard_map/stack;reshape | solution.py:68
  133.3 6.8 %reshape.46 = f32[5,512,1,384]{1,0,3,2:T(8,128)} reshape(f32[2560,3,128]{0,2,1:T(8,128)} %fusion.16) | data formatting | bytes 7864320 | tf_op jit(solution)/shard_map/stack;reshape | solution.py:68
  140.1 5.7 %copy.26 = f32[5,512,1,384]{3,1,2,0:T(8,128)} copy(f32[5,512,1,384]{1,0,3,2:T(8,128)} %reshape.46) | data formatting | bytes 7864320 | tf_op jit(solution)/shard_map/stack;reshape | solution.py:68
  157.1 5.0 collective-permute-start.5
  162.0 9.0 %fusion.32 = bf16[3,128,512]{2,1,0:T(8,128)(2,1)} fusion(bf16[2560,3,128]{0,2,1:T(8,128)(2,1)S(1)} %bitcast.77, f32[3,512,2560]{2,1,0:T(8,128)} %get-tuple-element.13, f32[3,512]{1,0:T(4,128)S(1)} %get-tuple-element.12), kind=kOutput, calls=%fused_computation.36 | convolution fusion | flops 1014693888 | bytes 18094080 | tf_op jit(solution)/shard_map/hqk,khe->qhe/dot_general | solution.py:48
  171.1 21.9 %fusion.35 = bf16[3,128,512]{2,1,0:T(8,128)(2,1)} fusion(bf16[2560,3,128]{0,2,1:T(8,128)(2,1)} %bitcast.81, f32[3,512,2560]{2,1,0:T(8,128)} %fusion.45, f32[3,512,2560]{2,1,0:T(8,128)} %get-tuple-element.13, f32[3,512]{1,0:T(4,128)S(1)} %get-tuple-element.12), kind=kOutput, calls=%fused_computation.37 | convolution fusion | flops 1034358784 | bytes 33822720 | tf_op jit(solution)/shard_map/hqk,khe->qhe/dot_general | solution.py:58
  194.2 4.8 fusion.22
  210.6 7.2 %convolution_convert_fusion = bf16[1152,3072]{1,0:T(8,128)(2,1)} fusion(bf16[512,1152]{0,1:T(8,128)(2,1)} %bitcast.82, bf16[512,3072]{1,0:T(8,128)(2,1)S(1)} %copy-done), kind=kOutput, calls=%fused_computation.8 | convolution fusion | flops 3627417600 | bytes 11403264 | tf_op jit(solution)/shard_map/dot_general | solution.py:84
  217.8 10.3 %copy.30 = bf16[3072,3,384]{2,0,1:T(8,128)(2,1)} copy(bf16[3072,3,384]{0,2,1:T(8,128)(2,1)} %bitcast.78) | data formatting | bytes 14155776 | tf_op jit(solution)/shard_map/reshape | solution.py:84
  228.1 8.4 %pad_maximum_fusion = bf16[3072,4,384]{2,0,1:T(8,128)(2,1)} fusion(bf16[3072,1,384]{2,0,1:T(8,128)(2,1)} %copy.31, bf16[3072,3,384]{2,0,1:T(8,128)(2,1)} %copy.30), kind=kLoop, calls=%fused_computation.9 | loop fusion | flops 4718592 | bytes 18874368 | tf_op jit(solution)/shard_map/concatenate | solution.py:91
  236.6 5.4 convolution_convert_fusion.1
  241.9 9.3 %bitcast_convert_fusion = bf16[512,3072]{1,0:T(8,128)(2,1)} fusion(bf16[3072,3,384]{2,0,1:T(8,128)(2,1)} %param.5, bf16[512,2,384]{2,0,1:T(8,128)(2,1)S(1)} %copy-done.6, bf16[512,1,384]{2,0,1:T(8,128)(2,1)S(1)} %copy.28), kind=kOutput, calls=%fused_computation.18 | convolution fusion | flops 3626041344 | bytes 11403264 | tf_op jit(solution)/shard_map/dot_general | solution.py:82
  251.2 131.5 %reduce-scatter.2.cloned.1.call-done = bf16[192,4,384]{2,0,1:T(8,128)(2,1)} async-done(((bf16[3072,4,384]{2,0,1:T(8,128)(2,1)}), bf16[192,4,384]{2,0,1:T(8,128)(2,1)}) %reduce-scatter.2.cloned.1.call-update) | async-done | bytes 589840 | tf_op jit(solution)/shard_map/reduce_scatter | solution.py:90
  386.6 155.5 %all-reduce.3.cloned.1.call-done = (bf16[512,3072]{1,0:T(8,128)(2,1)}, bf16[512,3072]{1,0:T(8,128)(2,1)}) async-done(((bf16[512,3072]{1,0:T(8,128)(2,1)}, bf16[512,3072]{1,0:T(8,128)(2,1)}), (bf16[512,3072]{1,0:T(8,128)(2,1)}, bf16[512,3072]{1,0:T(8,128)(2,1)})) %all-reduce.3.cloned.1.call-update) | async-done | bytes 6291472 | tf_op jit(solution)/shard_map/psum | solution.py:20
  (54 shorter events, 46.9 us)
Async XLA Ops:
  8.0 10.5 %copy-start = (bf16[512,3072]{1,0:T(8,128)(2,1)S(1)}, bf16[512,3072]{1,0:T(8,128)(2,1)}, u32[]{:S(2)}) copy-start(bf16[512,3072]{1,0:T(8,128)(2,1)} %param.4) | copy-start | bytes 9437188
  8.0 374.7 %reduce-scatter.2.cloned.1.call-start = ((), (), s32[]{:S(2)}) async-start(), calls=%async_computation.1 | async-start | bytes 10027008 | tf_op jit(solution)/shard_map/reduce_scatter | solution.py:90
  30.3 12.3 %copy-start.1 = (bf16[512,1152]{0,1:T(8,128)(2,1)S(1)}, bf16[512,1152]{0,1:T(8,128)(2,1)}, u32[]{:S(2)}) copy-start(bf16[512,1152]{0,1:T(8,128)(2,1)} %copy.19) | copy-start | bytes 3538948
  30.3 25.0 %collective-permute-start = (bf16[512,2,384]{0,2,1:T(8,128)(2,1)S(1)}, bf16[512,2,384]{0,2,1:T(8,128)(2,1)S(1)}, u32[]{:S(2)}, u32[]{:S(2)}) collective-permute-start(bf16[512,2,384]{0,2,1:T(8,128)(2,1)S(1)} %slice.59), channel_id=1, source_target_pairs={{112,0},{120,8},{0,16},{8,24},{16,32},{24,40},{32,48},{40,56},{48,... | collective-permute-start | bytes 2359304 | tf_op jit(solution)/shard_map/ppermute | solution.py:16
  32.4 30.5 %collective-permute-start.1 = (bf16[512,2,384]{0,2,1:T(8,128)(2,1)S(1)}, bf16[512,2,384]{0,2,1:T(8,128)(2,1)S(1)}, u32[]{:S(2)}, u32[]{:S(2)}) collective-permute-start(bf16[512,2,384]{0,2,1:T(8,128)(2,1)S(1)} %slice.59), channel_id=1, source_target_pairs={{120,0},{0,8},{8,16},{16,24},{24,32},{32,40},{40,48},{48,56},{56,6... | collective-permute-start | bytes 2359304 | tf_op jit(solution)/shard_map/ppermute | solution.py:16
  32.4 31.2 %collective-permute-start.3 = (bf16[512,2,384]{0,2,1:T(8,128)(2,1)S(1)}, bf16[512,2,384]{0,2,1:T(8,128)(2,1)S(1)}, u32[]{:S(2)}, u32[]{:S(2)}) collective-permute-start(bf16[512,2,384]{0,2,1:T(8,128)(2,1)S(1)} %slice.59), channel_id=1, source_target_pairs={{16,0},{24,8},{32,16},{40,24},{48,32},{56,40},{64,48},{72,56},{80,... | collective-permute-start | bytes 2359304 | tf_op jit(solution)/shard_map/ppermute | solution.py:16
  37.2 26.4 %collective-permute-start.2 = (bf16[512,2,384]{0,2,1:T(8,128)(2,1)S(1)}, bf16[512,2,384]{0,2,1:T(8,128)(2,1)S(1)}, u32[]{:S(2)}, u32[]{:S(2)}) collective-permute-start(bf16[512,2,384]{0,2,1:T(8,128)(2,1)S(1)} %slice.59), channel_id=1, source_target_pairs={{8,0},{16,8},{24,16},{32,24},{40,32},{48,40},{56,48},{64,56},{72,6... | collective-permute-start | bytes 2359304 | tf_op jit(solution)/shard_map/ppermute | solution.py:16
  42.6 22.6 %copy-start.7 = (bf16[512,384]{0,1:T(8,128)(2,1)}, bf16[512,384]{0,1:T(8,128)(2,1)S(1)}, u32[]{:S(2)}) copy-start(bf16[512,384]{0,1:T(8,128)(2,1)S(1)} %convolution_convert_fusion.4) | copy-start | bytes 1179652
  65.2 7.8 %copy-start.2 = (bf16[2560,1,384]{0,2,1:T(8,128)(2,1)}, bf16[2560,1,384]{0,2,1:T(8,128)(2,1)S(1)}, u32[]{:S(2)}) copy-start(bf16[2560,1,384]{0,2,1:T(8,128)(2,1)S(1)} %get-tuple-element.11) | copy-start | bytes 5898244
  149.7 12.4 %copy-start.3 = (bf16[2560,1,384]{0,2,1:T(8,128)(2,1)S(1)}, bf16[2560,1,384]{0,2,1:T(8,128)(2,1)}, u32[]{:S(2)}) copy-start(bf16[2560,1,384]{0,2,1:T(8,128)(2,1)} %copy-done.2) | copy-start | bytes 5898244
  151.4 51.8 %collective-permute-start.4 = (bf16[512,2,384]{2,0,1:T(8,128)(2,1)}, bf16[512,2,384]{2,0,1:T(8,128)(2,1)}, u32[]{:S(2)}, u32[]{:S(2)}) collective-permute-start(bf16[512,2,384]{2,0,1:T(8,128)(2,1)} %get-tuple-element.6), channel_id=1, source_target_pairs={{16,0},{24,8},{32,16},{40,24},{48,32},{56,40},{64,48},{72,56},{80,... | collective-permute-start | bytes 2359304 | tf_op jit(solution)/shard_map/ppermute | solution.py:16
  152.8 50.5 %collective-permute-start.7 = (bf16[512,2,384]{2,0,1:T(8,128)(2,1)}, bf16[512,2,384]{2,0,1:T(8,128)(2,1)}, u32[]{:S(2)}, u32[]{:S(2)}) collective-permute-start(bf16[512,2,384]{2,0,1:T(8,128)(2,1)} %get-tuple-element.7), channel_id=1, source_target_pairs={{112,0},{120,8},{0,16},{8,24},{16,32},{24,40},{32,48},{40,56},{48,... | collective-permute-start | bytes 2359304 | tf_op jit(solution)/shard_map/ppermute | solution.py:16
  153.5 49.8 %collective-permute-start.6 = (bf16[512,2,384]{2,0,1:T(8,128)(2,1)}, bf16[512,2,384]{2,0,1:T(8,128)(2,1)}, u32[]{:S(2)}, u32[]{:S(2)}) collective-permute-start(bf16[512,2,384]{2,0,1:T(8,128)(2,1)} %get-tuple-element.8), channel_id=1, source_target_pairs={{120,0},{0,8},{8,16},{16,24},{24,32},{32,40},{40,48},{48,56},{56,6... | collective-permute-start | bytes 2359304 | tf_op jit(solution)/shard_map/ppermute | solution.py:16
  157.1 46.2 %collective-permute-start.5 = (bf16[512,2,384]{2,0,1:T(8,128)(2,1)}, bf16[512,2,384]{2,0,1:T(8,128)(2,1)}, u32[]{:S(2)}, u32[]{:S(2)}) collective-permute-start(bf16[512,2,384]{2,0,1:T(8,128)(2,1)} %get-tuple-element.9), channel_id=1, source_target_pairs={{8,0},{16,8},{24,16},{32,24},{40,32},{48,40},{56,48},{64,56},{72,6... | collective-permute-start | bytes 2359304 | tf_op jit(solution)/shard_map/ppermute | solution.py:16
  206.1 0.9 copy-start.5
  236.5 305.6 %all-reduce.3.cloned.1.call-start = ((), (), s32[]{:S(2)}) async-start(), calls=%async_computation.2 | async-start | bytes 12582912 | tf_op jit(solution)/shard_map/psum | solution.py:20
  236.6 5.4 copy-start.6
  542.1 3.9 copy-start.4
Sparse Core Ops, SparseCore 0:
  236.6 146.0 reduce-scatter.1
Sparse Core Ops, SparseCore 1:
  251.3 290.7 all-reduce.2
where the time goes:
time: 557 us; the launch traced here: 555 us
  waiting for transfers between devices  308 us (55%)
  matrix products  126 us (23%)
  local copies, waits for them, and re-layouts  70 us (13%)
  starting transfers between devices  18.9 us (3%)
  other arithmetic  17.3 us (3%)
  between operations  15.6 us (3%)
    psum x1, waiting for transfers between devices, head_total(): return lax.psum(partial_term.astype(jnp.bfloat16), 'head')  156 us
    reduce_scatter x1, waiting for transfers between devices, local(): lax.psum_scatter(jnp.concatenate([part_qkv, part_out], axis=1).astype(jnp...  131 us
    dot_general x1, matrix products, local(): jnp.einsum('hqk,qhe->khe', d_scores, queries, preferred_element_type=jnp....  27.2 us
    another operation x4, local copies, waits for them, and re-layouts, local(): pairs = jnp.stack([d_keys, d_values], axis=2)  25 us
    dot_general x1, matrix products, local(): jnp.einsum('hqk,khe->qhe', d_scores, key_rows, preferred_element_type=jnp...  21.9 us
    ppermute x8, waiting for transfers between devices, from_behind(): return lax.ppermute(block, axis, route)  20.7 us
    ppermute x8, starting transfers between devices, from_behind(): return lax.ppermute(block, axis, route)  18.8 us
    unnamed x23, local copies, waits for them, and re-layouts  17.1 us
  transfers between devices with their start and end apart: 10, of which 5 were waited for; matrix products, arithmetic and copies ran while one was open for 12% of the time, Pallas kernels for 0%

commit v1 on v0

v1 whole, which is shorter than its diff:
```python
import functools
import math

import jax
import jax.numpy as jnp
from jax import lax
from jax.experimental import pallas as pl
from jax.experimental.pallas import tpu as pltpu
from jax.sharding import PartitionSpec as P

D = 3072
HEADS = 24
E = 128
TOK = 512
LH = 3
LW = LH * E
ROWS = D // 16
SCALE = 1.0 / math.sqrt(E)
EXP2_SCALE = SCALE * math.log2(math.e)
BF = jnp.bfloat16
F32 = jnp.float32
VMEM_LIMIT = 56 << 20


def sds(shape, dtype):
    return jax.ShapeDtypeStruct(shape, dtype)


def dot(a, b, dims=((1,), (0,))):
    return lax.dot_general(a, b, (dims, ((), ())), preferred_element_type=F32)


def params():
    return pltpu.CompilerParams(vmem_limit_bytes=VMEM_LIMIT)


def cost(flops, moved, exps=0):
    return pl.CostEstimate(flops=int(flops), bytes_accessed=int(moved), transcendentals=int(exps))


def view_route(step):
    return [(v, step(v) % 16) for v in range(16)]


SWAP = view_route(lambda v: v ^ 1)
NEAR = view_route(lambda v: v + 2 if v % 2 == 0 else v - 2)
FAR = view_route(lambda v: v - 2 if v % 2 == 0 else v + 2)
BACK_ONE = view_route(lambda v: v - 1 if v % 2 == 0 else v + 1)


def z_route(dz):
    return [(v, (v // 8) * 8 + ((v // 2 + dz) % 4) * 2 + v % 2) for v in range(16)]


X_HI = view_route(lambda v: v + 8)
HEAD_STEPS = [(dy, dx) for dy in range(4) for dx in range(2)]


def head_route(dy, dx):
    return [(h, ((h // 2 + dy) % 4) * 2 + (h % 2 ^ dx)) for h in range(8)]


def over_view(block, route):
    return lax.ppermute(block, "view", route)


def over_head(block, step):
    return lax.ppermute(block, "head", head_route(*step))


def kv_kernel(x_ref, wk_ref, wv_ref, *refs):
    kv_refs = refs[:LH]
    acc = refs[LH]
    step = pl.program_id(0)
    x = x_ref[...]
    k = dot(x, wk_ref[...])
    v = dot(x, wv_ref[...])

    @pl.when(step == 0)
    def _():
        acc[:, :LW] = k
        acc[:, LW:] = v

    @pl.when((step > 0) & (step < 3))
    def _():
        acc[:, :LW] += k
        acc[:, LW:] += v

    @pl.when(step == 3)
    def _():
        for h in range(LH):
            cols = slice(h * E, (h + 1) * E)
            kv_refs[h][:, :E] = (acc[:, cols] + k[:, cols]).astype(BF)
            kv_refs[h][:, E:] = (acc[:, LW + h * E : LW + (h + 1) * E] + v[:, cols]).astype(BF)


def project_kv(x, w3):
    depth = D // 4
    return pl.pallas_call(
        kv_kernel,
        grid=(4,),
        in_specs=[
            pl.BlockSpec((TOK, depth), lambda i: (0, i)),
            pl.BlockSpec((None, depth, LW), lambda i: (1, i, 0)),
            pl.BlockSpec((None, depth, LW), lambda i: (2, i, 0)),
        ],
        out_specs=[pl.BlockSpec((TOK, 2 * E), lambda i: (0, 0))] * LH,
        out_shape=[sds((TOK, 2 * E), BF)] * LH,
        scratch_shapes=[pltpu.VMEM((TOK, 2 * LW), F32)],
        compiler_params=params(),
        cost_estimate=cost(2 * TOK * D * 2 * LW, 9 << 20),
    )(x, w3, w3)


def attention_kernel(q_ref, g_ref, o_ref, a_ref, b_ref, c_ref, r_ref, _x, _g, att_dq_ref, d_o, d_a, d_bc, d_r, s_scr, dp_scr):
    n = TOK
    kvs = (o_ref, a_ref, b_ref, c_ref, r_ref)
    outs = (d_o, d_a, d_bc.at[0], d_bc.at[1], d_r)
    q = q_ref[...]
    g = g_ref[...]
    q_t = q.T
    g_t = g.T
    top = None
    for j, kv in enumerate(kvs):
        s = dot(kv[:, :E], q_t)
        s_scr[j * n : (j + 1) * n] = s
        here = jnp.max(s, axis=0, keepdims=True)
        top = here if top is None else jnp.maximum(top, here)
    top = top * EXP2_SCALE
    total = None
    for j in range(5):
        e = jnp.exp2(s_scr[j * n : (j + 1) * n] * EXP2_SCALE - top)
        s_scr[j * n : (j + 1) * n] = e
        here = jnp.sum(e, axis=0, keepdims=True)
        total = here if total is None else total + here
    inverse = 1.0 / total
    delta = None
    acc = None
    for j, kv in enumerate(kvs):
        p = s_scr[j * n : (j + 1) * n] * inverse
        s_scr[j * n : (j + 1) * n] = p
        p_bf = p.astype(BF)
        v = kv[:, E:]
        dp = dot(v, g_t)
        dp_scr[j * n : (j + 1) * n] = dp
        here = jnp.sum(p * dp, axis=0, keepdims=True)
        delta = here if delta is None else delta + here
        term = dot(v.T, p_bf)
        acc = term if acc is None else acc + term
        outs[j][:, E:] = dot(p_bf, g).astype(outs[j].dtype)
    att_dq_ref[0] = acc.T.astype(BF)
    acc = None
    for j, kv in enumerate(kvs):
        ds = (s_scr[j * n : (j + 1) * n] * (dp_scr[j * n : (j + 1) * n] - delta) * SCALE).astype(BF)
        k = kv[:, :E]
        term = dot(k.T, ds)
        acc = term if acc is None else acc + term
        outs[j][:, :E] = dot(ds, q).astype(outs[j].dtype)
    att_dq_ref[1] = acc.T.astype(BF)


def attention(h, queries, d_att, kvs, before):
    head_block = pl.BlockSpec((TOK, E), lambda i: (0, h))
    pair = pl.BlockSpec((TOK, 2 * E), lambda i: (0, 0))
    return pl.pallas_call(
        attention_kernel,
        grid=(1,),
        in_specs=[head_block, head_block] + [pair] * 5 + [pl.BlockSpec(memory_space=pl.ANY)] * 2,
        out_specs=[
            pl.BlockSpec((2, TOK, E), lambda i: (0, 0, 0)),
            pair,
            pair,
            pl.BlockSpec((2, TOK, 2 * E), lambda i: (0, 0, 0)),
            pair,
        ],
        out_shape=[
            sds((2, TOK, E), BF),
            sds((TOK, 2 * E), F32),
            sds((TOK, 2 * E), BF),
            sds((2, TOK, 2 * E), BF),
            sds((TOK, 2 * E), F32),
        ],
        scratch_shapes=[pltpu.VMEM((5 * TOK, TOK), F32)] * 2,
        compiler_params=params(),
        cost_estimate=cost(6 * 2 * TOK * 5 * TOK * E * 2, 4 << 20, 5 * TOK * TOK),
    )(queries, d_att, *kvs, *before)


def rows_kernel(k_of, dest_ref, *refs):
    parts = refs[: len(k_of)]
    w_ref = refs[len(k_of)]
    outs = refs[len(k_of) + 2 : len(k_of) + 10]
    a_scr = refs[-1]

    @pl.when(pl.program_id(0) == 0)
    def _():
        for i in range(8):
            rows = pl.ds(pl.multiple_of(dest_ref[i] * 64, 64), 64)
            for part, places in zip(parts, k_of):
                piece = part[rows, :] if len(part.shape) == 2 else part[0, rows, :]
                for src, dst in places:
                    a_scr[i * 64 : (i + 1) * 64, dst : dst + E] = piece[:, src : src + E]

    a = a_scr[...]
    if len(w_ref.shape) == 2:
        out = dot(a, w_ref[...], ((1,), (1,)))
    else:
        out = None
        for i in range(w_ref.shape[0]):
            term = dot(a[:, i * LW : (i + 1) * LW], w_ref[i], ((1,), (1,)))
            out = term if out is None else out + term
    out = out.astype(BF)
    for i in range(8):
        outs[i][...] = out[i * 64 : (i + 1) * 64]


def rows_product(dest, parts, k_of, weights, tiles, before):
    cols = D // tiles
    part_specs = []
    for part in parts:
        if part.ndim == 2:
            part_specs.append(pl.BlockSpec(part.shape, lambda t, s: (0, 0)))
        else:
            part_specs.append(pl.BlockSpec((1,) + part.shape[1:], lambda t, s: (part_index[0], 0, 0)))
    part_index = [1] if weights.ndim == 3 else [0]
    if weights.ndim == 2:
        w_spec = pl.BlockSpec((cols, LW), lambda t, s: (t, 0))
        depth = LW
    else:
        w_spec = pl.BlockSpec((3, cols, LW), lambda t, s: (0, t, 0))
        depth = 3 * LW
    return pl.pallas_call(
        functools.partial(rows_kernel, k_of),
        grid_spec=pltpu.PrefetchScalarGridSpec(
            num_scalar_prefetch=1,
            grid=(tiles,),
            in_specs=part_specs + [w_spec, pl.BlockSpec(memory_space=pl.ANY)],
            out_specs=[pl.BlockSpec((64, cols), lambda t, s: (0, t))] * 8,
            scratch_shapes=[pltpu.VMEM((TOK, depth), BF)],
        ),
        out_shape=[sds((64, D), BF)] * 8,
        compiler_params=params(),
        cost_estimate=cost(2 * TOK * D * depth, (depth * D + 2 * TOK * D) * 2),
    )(dest, *parts, weights, before)


def place_kernel(src_ref, *refs):
    out_ref = refs[8]
    for i in range(8):
        rows = pl.ds(pl.multiple_of(src_ref[i] * 64, 64), 64)
        out_ref[rows, :] = refs[i][...]


def place(source, chunks):
    cols = D // 4
    return pl.pallas_call(
        place_kernel,
        grid_spec=pltpu.PrefetchScalarGridSpec(
            num_scalar_prefetch=1,
            grid=(4,),
            in_specs=[pl.BlockSpec((64, cols), lambda t, s: (0, t))] * 8,
            out_specs=pl.BlockSpec((TOK, cols), lambda t, s: (0, t)),
        ),
        out_shape=sds((TOK, D), BF),
        compiler_params=params(),
        cost_estimate=cost(0, 4 * TOK * D),
    )(source, *chunks)


def head_sum(chunks):
    got = [chunks[0]] + [over_head(chunks[i], HEAD_STEPS[i]) for i in range(1, 8)]
    total = got[0].astype(F32)
    for chunk in got[1:]:
        total = total + chunk.astype(F32)
    return total.astype(BF)


def head_gather(source, chunk):
    return place(source, [chunk] + [over_head(chunk, HEAD_STEPS[i]) for i in range(1, 8)])


def turn_kernel(core_ref, x_ref, mine_ref, other_ref, scr):
    scr[...] = x_ref[...].T
    core = core_ref[0]
    mine_ref[...] = scr[pl.ds(pl.multiple_of(core * ROWS, ROWS), ROWS), :]
    other_ref[...] = scr[pl.ds(pl.multiple_of((1 - core) * ROWS, ROWS), ROWS), :]


def turn(core, x):
    block = pl.BlockSpec((None, ROWS, TOK), lambda c, s: (c, 0, 0))
    return pl.pallas_call(
        turn_kernel,
        grid_spec=pltpu.PrefetchScalarGridSpec(
            num_scalar_prefetch=1,
            grid=(8,),
            in_specs=[pl.BlockSpec((TOK, 2 * ROWS), lambda c, s: (0, c))],
            out_specs=[block, block],
            scratch_shapes=[pltpu.VMEM((2 * ROWS, TOK), BF)],
        ),
        out_shape=[sds((8, ROWS, TOK), BF)] * 2,
        compiler_params=params(),
        cost_estimate=cost(TOK * D * 64, 4 * TOK * D),
    )(core, x)


def weight_kernel(plan, n_lhs, n_rhs, at_ref, *refs):
    lhs = refs[: 4 * n_lhs]
    rhs = refs[4 * n_lhs : 4 * n_lhs + n_rhs]
    outs = refs[4 * n_lhs + n_rhs :]
    step = pl.program_id(0)
    for i in range(4):
        @pl.when(step == i)
        def _():
            for pick, mine, theirs, dst in plan:
                top_m, low_m, top_t, low_t = lhs[4 * pick : 4 * pick + 4]
                left = jnp.concatenate([top_m[...], low_m[...]], axis=0)
                right = jnp.concatenate([top_t[...], low_t[...]], axis=0)
                out = dot(left, mine(rhs)) + dot(right, theirs(rhs))
                out = out.astype(BF)
                width = out.shape[1]
                outs[i][0, :, dst : dst + width] = out[:ROWS]
                outs[i][1, :, dst : dst + width] = out[ROWS:]


def weight_terms(at, lhs_pairs, rhs, plan):
    own = pl.BlockSpec((None, None, ROWS, TOK), lambda i, s: (s[4], s[i], 0, 0))
    far = pl.BlockSpec((None, None, ROWS, TOK), lambda i, s: (1 - s[4], s[i], 0, 0))
    lhs = []
    for mine, theirs in lhs_pairs:
        mine = mine.reshape(2, 4, ROWS, TOK)
        theirs = theirs.reshape(2, 4, ROWS, TOK)
        lhs += [mine, mine, theirs, theirs]
    rhs_specs = [
        pl.BlockSpec(r.shape, functools.partial(lambda nd, i, s: (0,) * nd, r.ndim)) for r in rhs
    ]
    out_block = pl.BlockSpec((2, ROWS, 2 * LW), lambda i, s: (0, 0, 0))
    return pl.pallas_call(
        functools.partial(weight_kernel, plan, len(lhs_pairs), len(rhs)),
        grid_spec=pltpu.PrefetchScalarGridSpec(
            num_scalar_prefetch=1,
            grid=(4,),
            in_specs=[own, far] * (2 * len(lhs_pairs)) + rhs_specs,
            out_specs=[out_block] * 4,
        ),
        out_shape=[sds((2, ROWS, 2 * LW), BF)] * 4,
        compiler_params=params(),
        cost_estimate=cost(2 * 8 * ROWS * 2 * TOK * 2 * LW, 10 << 20),
    )(at, *lhs, *rhs)


def weight_sum(terms):
    total = terms[0].astype(F32)
    for dz in range(1, 4):
        total = total + over_view(terms[dz], z_route(dz)).astype(F32)
    return total[0] + over_view(total[1].astype(BF), X_HI).astype(F32)


def local(x_tokens, w_qkv, w_out, grad_out):
    view = lax.axis_index("view")
    head = lax.axis_index("head")
    core = (view % 2).astype(jnp.int32)
    chip_z = view // 2 % 4
    x_hi = view // 8
    dest = jnp.stack([((head // 2 + dy) % 4) * 2 + (head % 2 ^ dx) for dy, dx in HEAD_STEPS]).astype(jnp.int32)
    source = jnp.stack([((head // 2 - dy) % 4) * 2 + (head % 2 ^ dx) for dy, dx in HEAD_STEPS]).astype(jnp.int32)
    at = jnp.stack([(chip_z + dz) % 4 for dz in range(4)] + [x_hi]).astype(jnp.int32)
    core = core.reshape(1)
    w3 = jnp.transpose(w_qkv, (1, 0, 2))

    own = project_kv(x_tokens, w3)
    near = [over_view(kv, NEAR) for kv in own]
    far = [over_view(kv, FAR) for kv in own]
    beside = [over_view(kv, SWAP) for kv in own]
    relayed = [over_view(kv, SWAP) for kv in far]

    queries = jnp.dot(x_tokens, w3[0], preferred_element_type=F32).astype(BF)
    d_att = jnp.dot(grad_out, w_out, preferred_element_type=F32).astype(BF)

    x_mine, x_other = turn(core, x_tokens)
    x_theirs = over_view(x_other, SWAP)
    g_mine, g_other = turn(core, grad_out)
    g_theirs = over_view(g_other, SWAP)

    att_dq = []
    d_kv = []
    for h in range(LH):
        pair, d_own, d_near, d_swap, d_relay = attention(
            h, queries, d_att, (own[h], near[h], far[h], beside[h], relayed[h]), (x_other, g_other)
        )
        att_dq.append(pair)
        back = over_view(d_swap, SWAP)
        relay = (d_relay + back[0].astype(F32)).astype(BF)
        two = over_view(d_near, FAR)
        one = over_view(relay, BACK_ONE)
        d_kv.append((d_own + back[1].astype(F32) + two.astype(F32) + one.astype(F32)).astype(BF))

    mixed_chunks = rows_product(dest, att_dq, [[(0, E * h)] for h in range(LH)], w_out, 4, relay)
    mixed_part = head_sum(mixed_chunks)

    att_dq_theirs = [over_view(pair, SWAP) for pair in att_dq]

    def joined(which, base):
        return lambda rhs: jnp.concatenate([rhs[base + h][which] for h in range(LH)], axis=1)

    early = weight_terms(
        at,
        [(x_mine, x_theirs), (g_mine, g_theirs)],
        att_dq + att_dq_theirs,
        [(0, joined(1, 0), joined(1, LH), 0), (1, joined(0, 0), joined(0, LH), LW)],
    )
    early_sum = weight_sum(early)

    d_in_chunks = rows_product(
        dest,
        att_dq + d_kv,
        [[(0, E * h)] for h in range(LH)] + [[(0, LW + E * h), (E, 2 * LW + E * h)] for h in range(LH)],
        w3,
        4,
        early[0],
    )
    d_in_part = head_sum(d_in_chunks)

    d_kv_theirs = [over_view(pair, SWAP) for pair in d_kv]

    def columns(first, base):
        return lambda rhs: jnp.concatenate([rhs[base + h][:, first : first + E] for h in range(LH)], axis=1)

    late = weight_terms(
        at,
        [(x_mine, x_theirs)],
        d_kv + d_kv_theirs,
        [(0, columns(0, 0), columns(0, LH), 0), (0, columns(E, 0), columns(E, LH), LW)],
    )
    late_sum = weight_sum(late)

    mixed_out = head_gather(source, mixed_part)
    d_input = head_gather(source, d_in_part)
    d_w = jnp.stack([early_sum[:, :LW], late_sum[:, :LW], late_sum[:, LW:]], axis=1)
    return (mixed_out, d_input, d_w, early_sum[:, LW:])


def solution(mesh):
    placed = (P("view", None), P(None, None, "head"), P(None, "head"), P("view", None))
    return jax.shard_map(
        local,
        mesh=mesh,
        in_specs=placed,
        out_specs=(P("view", None), P("view", None), P("view", None, "head"), P("view", "head")),
        check_vma=False,
    )
```

time: 557 us -> 334 us (0.60)
  waiting for transfers between devices: 308 us -> 119 us
  matrix products: 126 us -> 6.89 us
  Pallas kernels: 0 us -> 86.3 us
  starting transfers between devices: 18.9 us -> 100 us
  local copies, waits for them, and re-layouts: 70 us -> 6.49 us
  between operations: 15.6 us -> 1.77 us
  other arithmetic: 17.3 us -> 7.02 us
    psum x1 -> x0, waiting for transfers between devices: 156 us -> none  [head_total(): return lax.psum(partial_term.astype(jnp.bfloat16), 'head')]
    reduce_scatter x1 -> x0, waiting for transfers between devices: 131 us -> none  [local(): lax.psum_scatter(jnp.concatenate([part_qkv, part_out], axis=1).astype(jnp...]
    dot_general x11 -> x2, matrix products: 114 us -> 6.89 us  [the longest x1 4.35 us: local(): queries = jnp.dot(x_tokens, w3[0], preferred_element_type=F32).astype(BF)]
    ppermute x8 -> x65, waiting for transfers between devices: 20.7 us -> 119 us  [the longest x28 64.8 us: over_head(): return lax.ppermute(block, 'head', head_route(*step))]
    pallas_call x0 -> x12, Pallas kernels: none -> 86.3 us  [the longest x3 23.1 us: attention(): pl.pallas_call(attention_kernel, grid=(1,), in_specs=[head_block, head_bl...]
    ppermute x8 -> x65, starting transfers between devices: 18.8 us -> 100 us  [the longest x28 52.1 us: over_head(): return lax.ppermute(block, 'head', head_route(*step))]
    another operation x6 -> x4, local copies, waits for them, and re-layouts: 28.7 us -> 1.98 us  [the longest x1 0.65 us: local(): jnp.stack([(head // 2 + dy) % 4 * 2 + (head % 2 ^ dx) for dy, dx in HEAD_...]
    reshape x2 -> x0, local copies, waits for them, and re-layouts: 14.6 us -> none  [the longest x1 10.3 us: local(): jnp.dot(x_tokens.T, d_projected, preferred_element_type=jnp.float32)]
  transfers between devices with their start and end apart: 10 -> 65, of which waited for: 5 -> 19; matrix products, arithmetic and copies ran while one was open for 12% -> 5% of each run, Pallas kernels for 0% -> 24%
where the time goes in v1:
time: 334 us; the launch traced here: 328 us
  waiting for transfers between devices  119 us (36%)
  starting transfers between devices  100 us (30%)
  Pallas kernels  86.3 us (26%)
  other arithmetic  7.02 us (2%)
  matrix products  6.89 us (2%)
  local copies, waits for them, and re-layouts  6.49 us (2%)
    ppermute x28, waiting for transfers between devices, over_head(): return lax.ppermute(block, 'head', head_route(*step))  64.8 us
    ppermute x37, waiting for transfers between devices, over_view(): return lax.ppermute(block, 'view', route)  54.5 us
    ppermute x28, starting transfers between devices, over_head(): return lax.ppermute(block, 'head', head_route(*step))  52.1 us
    ppermute x37, starting transfers between devices, over_view(): return lax.ppermute(block, 'view', route)  48.1 us
    pallas_call x3, Pallas kernels, attention(): pl.pallas_call(attention_kernel, grid=(1,), in_specs=[head_block, head_bl...  23.1 us
    pallas_call x2, Pallas kernels, weight_terms(): pl.pallas_call(functools.partial(weight_kernel, plan, len(lhs_pairs), len...  16.9 us
    pallas_call x2, Pallas kernels, rows_product(): pl.pallas_call(functools.partial(rows_kernel, k_of), grid_spec=pltpu.Pref...  15.5 us
    pallas_call x2, Pallas kernels, turn(): pl.pallas_call(turn_kernel, grid_spec=pltpu.PrefetchScalarGridSpec(num_sc...  13.5 us
  transfers between devices with their start and end apart: 65, of which 19 were waited for; matrix products, arithmetic and copies ran while one was open for 5% of the time, Pallas kernels for 24%

profile of v1, /device:TPU:0, one launch (start us, length us, event | category | flops | bytes accessed | tf_op | source)
XLA Modules:
  0.0 328.1 jit_solution(10534570861978090249)
XLA Ops:
  0.6 7.3 %shard_map.75 = (bf16[512,256]{1,0:T(8,128)(2,1)}, bf16[512,256]{1,0:T(8,128)(2,1)}, bf16[512,256]{1,0:T(8,128)(2,1)}) custom-call(bf16[512,3072]{1,0:T(8,128)(2,1)} %x_ref.4, bf16[3,3072,384]{2,1,0:T(8,128)(2,1)} %bitcast.81, bf16[3,3072,384]{2,1,0:T(8,128)(2,1)} %bitcast.82), custom_call_target="tpu_custom_call" | custom-call | flops 2415919104 | bytes 9437184 | tf_op jit(solution)/shard_map/pallas_call | solution.py:99
  8.0 6.6 %collective-permute-start.9 = (bf16[512,256]{1,0:T(8,128)(2,1)}, bf16[512,256]{1,0:T(8,128)(2,1)}, u32[]{:S(2)}, u32[]{:S(2)}) collective-permute-start(bf16[512,256]{1,0:T(8,128)(2,1)} %get-tuple-element.56.o_ref), channel_id=1, source_target_pairs={{0,112},{8,24},{16,0},{24,40},{32,16},{40,56},{48,32},{56,72},{64,... | collective-permute-start | bytes 786440 | tf_op jit(solution)/shard_map/ppermute | solution.py:64
  20.2 6.7 %shard_map.76 = (bf16[8,192,512]{2,1,0:T(8,128)(2,1)}, bf16[8,192,512]{2,1,0:T(8,128)(2,1)}) custom-call(s32[1]{0:T(128)} %bitcast.16.core_ref, bf16[512,3072]{1,0:T(8,128)(2,1)} %x_ref.4), custom_call_target="tpu_custom_call" | custom-call | flops 100663296 | bytes 6291456 | tf_op jit(solution)/shard_map/pallas_call | solution.py:291
  26.9 6.8 %shard_map.77 = (bf16[8,192,512]{2,1,0:T(8,128)(2,1)}, bf16[8,192,512]{2,1,0:T(8,128)(2,1)}) custom-call(s32[1]{0:T(128)} %bitcast.16.core_ref, bf16[512,3072]{1,0:T(8,128)(2,1)} %x_ref.5), custom_call_target="tpu_custom_call" | custom-call | flops 100663296 | bytes 6291456 | tf_op jit(solution)/shard_map/pallas_call | solution.py:291
  47.6 7.7 %shard_map.80 = (bf16[2,512,128]{2,1,0:T(8,128)(2,1)}, f32[512,256]{1,0:T(8,128)}, bf16[512,256]{1,0:T(8,128)(2,1)}, bf16[2,512,256]{2,1,0:T(8,128)(2,1)}, f32[512,256]{1,0:T(8,128)}) custom-call(bf16[512,384]{1,0:T(8,128)(2,1)} %fusion.1.q_ref, bf16[512,384]{1,0:T(8,128)(2,1)} %convolution_convert_fusion.g_ref, bf16[512,256]{1,0:T(8,128)(2,1)} %get-tuple-element.56.o_ref, ...), custom_call_target="tpu_custom_call" | custom-call | flops 4026531840 | bytes 4194304 | tf_op jit(solution)/shard_map/pallas_call | solution.py:165
  61.8 7.7 %shard_map.79 = (bf16[2,512,128]{2,1,0:T(8,128)(2,1)}, f32[512,256]{1,0:T(8,128)}, bf16[512,256]{1,0:T(8,128)(2,1)}, bf16[2,512,256]{2,1,0:T(8,128)(2,1)}, f32[512,256]{1,0:T(8,128)}) custom-call(bf16[512,384]{1,0:T(8,128)(2,1)} %fusion.1.q_ref, bf16[512,384]{1,0:T(8,128)(2,1)} %convolution_convert_fusion.g_ref, bf16[512,256]{1,0:T(8,128)(2,1)} %get-tuple-element.54.o_ref, ...), custom_call_target="tpu_custom_call" | custom-call | flops 4026531840 | bytes 4194304 | tf_op jit(solution)/shard_map/pallas_call | solution.py:165
  71.1 7.6 %shard_map.78 = (bf16[2,512,128]{2,1,0:T(8,128)(2,1)}, f32[512,256]{1,0:T(8,128)}, bf16[512,256]{1,0:T(8,128)(2,1)}, bf16[2,512,256]{2,1,0:T(8,128)(2,1)}, f32[512,256]{1,0:T(8,128)}) custom-call(bf16[512,384]{1,0:T(8,128)(2,1)} %fusion.1.q_ref, bf16[512,384]{1,0:T(8,128)(2,1)} %convolution_convert_fusion.g_ref, bf16[512,256]{1,0:T(8,128)(2,1)} %get-tuple-element.50.o_ref, ...), custom_call_target="tpu_custom_call" | custom-call | flops 4026531840 | bytes 4194304 | tf_op jit(solution)/shard_map/pallas_call | solution.py:165
  85.1 6.1 %shard_map.81 = (bf16[64,3072]{1,0:T(8,128)(2,1)}, bf16[64,3072]{1,0:T(8,128)(2,1)}, bf16[64,3072]{1,0:T(8,128)(2,1)}, bf16[64,3072]{1,0:T(8,128)(2,1)}, bf16[64...) custom-call(s32[8]{0:T(128)} %stack.95.dest_ref, ...), custom_call_target="tpu_custom_call" | custom-call | flops 1207959552 | bytes 8650752 | tf_op jit(solution)/shard_map/pallas_call | solution.py:232
  112.9 6.3 %collective-permute-done.29 = bf16[512,256]{1,0:T(8,128)(2,1)S(1)} collective-permute-done((bf16[512,256]{1,0:T(8,128)(2,1)S(1)}, bf16[512,256]{1,0:T(8,128)(2,1)S(1)}, u32[]{:S(2)}, u32[]{:S(2)}) %collective-permute-start.29) | collective-permute-done | bytes 262176 | tf_op jit(solution)/shard_map/ppermute | solution.py:64
  120.5 6.5 %collective-permute-start.17 = (bf16[64,3072]{1,0:T(8,128)(2,1)S(1)}, bf16[64,3072]{1,0:T(8,128)(2,1)S(1)}, u32[]{:S(2)}, u32[]{:S(2)}) collective-permute-start(bf16[64,3072]{1,0:T(8,128)(2,1)S(1)} %copy-done.45), channel_id=1, source_target_pairs={{0,5},{1,4},{2,7},{3,6},{4,1},{5,0},{6,3},{7,2},{8,13},{9,12},{10,... | collective-permute-start | bytes 1179656 | tf_op jit(solution)/shard_map/ppermute | solution.py:68
  137.4 13.7 %collective-permute-done.18 = bf16[64,3072]{1,0:T(8,128)(2,1)S(1)} collective-permute-done((bf16[64,3072]{1,0:T(8,128)(2,1)S(1)}, bf16[64,3072]{1,0:T(8,128)(2,1)S(1)}, u32[]{:S(2)}, u32[]{:S(2)}) %collective-permute-start.18) | collective-permute-done | bytes 393248 | tf_op jit(solution)/shard_map/ppermute | solution.py:68
  161.8 8.8 %shard_map.83 = (bf16[2,192,768]{2,1,0:T(8,128)(2,1)}, bf16[2,192,768]{2,1,0:T(8,128)(2,1)}, bf16[2,192,768]{2,1,0:T(8,128)(2,1)}, bf16[2,192,768]{2,1,0:T(8,128)(2,1)}) custom-call(s32[5]{0:T(128)} %stack.101.at_ref, bf16[2,4,192,512]{3,2,1,0:T(8,128)(2,1)} %bitcast.85, bf16[2,4,192,512]{3,2,1,0:T(8,128)(2,1)} %bitcast.86, ...), custom_call_target="tpu_custom_call" | custom-call | flops 2415919104 | bytes 10485760 | tf_op jit(solution)/shard_map/pallas_call | solution.py:337
  171.5 9.4 %shard_map.84 = (bf16[64,3072]{1,0:T(8,128)(2,1)}, bf16[64,3072]{1,0:T(8,128)(2,1)}, bf16[64,3072]{1,0:T(8,128)(2,1)}, bf16[64,3072]{1,0:T(8,128)(2,1)}, bf16[64...) custom-call(s32[8]{0:T(128)} %stack.95.dest_ref, ...), custom_call_target="tpu_custom_call" | custom-call | flops 3623878656 | bytes 13369344 | tf_op jit(solution)/shard_map/pallas_call | solution.py:232
  181.0 8.2 %collective-permute-done.25.refs_6_ = bf16[64,3072]{1,0:T(8,128)(2,1)S(1)} collective-permute-done((bf16[64,3072]{1,0:T(8,128)(2,1)S(1)}, bf16[64,3072]{1,0:T(8,128)(2,1)S(1)}, u32[]{:S(2)}, u32[]{:S(2)}) %collective-permute-start.25) | collective-permute-done | bytes 393248 | tf_op jit(solution)/shard_map/ppermute | solution.py:68
  194.8 6.4 %collective-permute-done.20.refs_1_ = bf16[64,3072]{1,0:T(8,128)(2,1)S(1)} collective-permute-done((bf16[64,3072]{1,0:T(8,128)(2,1)S(1)}, bf16[64,3072]{1,0:T(8,128)(2,1)S(1)}, u32[]{:S(2)}, u32[]{:S(2)}) %collective-permute-start.20) | collective-permute-done | bytes 393248 | tf_op jit(solution)/shard_map/ppermute | solution.py:68
  202.0 7.7 %collective-permute-done.40 = bf16[64,3072]{1,0:T(8,128)(2,1)S(1)} collective-permute-done((bf16[64,3072]{1,0:T(8,128)(2,1)}, bf16[64,3072]{1,0:T(8,128)(2,1)S(1)}, u32[]{:S(2)}, u32[]{:S(2)}) %collective-permute-start.40) | collective-permute-done | bytes 393248 | tf_op jit(solution)/shard_map/ppermute | solution.py:68
  209.7 20.5 %collective-permute-start.45 = (bf16[64,3072]{1,0:T(8,128)(2,1)}, bf16[64,3072]{1,0:T(8,128)(2,1)S(1)}, u32[]{:S(2)}, u32[]{:S(2)}) collective-permute-start(bf16[64,3072]{1,0:T(8,128)(2,1)} %get-tuple-element.87), channel_id=1, source_target_pairs={{0,6},{1,7},{2,0},{3,1},{4,2},{5,3},{6,4},{7,5},{8,14},{9,15},{10,... | collective-permute-start | bytes 1179656 | tf_op jit(solution)/shard_map/ppermute | solution.py:68
  231.3 8.2 %shard_map.86 = (bf16[2,192,768]{2,1,0:T(8,128)(2,1)}, bf16[2,192,768]{2,1,0:T(8,128)(2,1)}, bf16[2,192,768]{2,1,0:T(8,128)(2,1)}, bf16[2,192,768]{2,1,0:T(8,128)(2,1)}) custom-call(s32[5]{0:T(128)} %stack.101.at_ref, bf16[2,4,192,512]{3,2,1,0:T(8,128)(2,1)} %bitcast.87, bf16[2,4,192,512]{3,2,1,0:T(8,128)(2,1)} %bitcast.88, ...), custom_call_target="tpu_custom_call" | custom-call | flops 2415919104 | bytes 10485760 | tf_op jit(solution)/shard_map/pallas_call | solution.py:337
  252.5 9.9 %collective-permute-done.55 = bf16[2,192,768]{2,1,0:T(8,128)(2,1)S(1)} collective-permute-done((bf16[2,192,768]{2,1,0:T(8,128)(2,1)S(1)}, bf16[2,192,768]{2,1,0:T(8,128)(2,1)S(1)}, u32[]{:S(2)}, u32[]{:S(2)}) %collective-permute-start.55) | collective-permute-done | bytes 589856 | tf_op jit(solution)/shard_map/ppermute | solution.py:64
  262.8 9.4 %collective-permute-done.56 = bf16[2,192,768]{2,1,0:T(8,128)(2,1)S(1)} collective-permute-done((bf16[2,192,768]{2,1,0:T(8,128)(2,1)S(1)}, bf16[2,192,768]{2,1,0:T(8,128)(2,1)S(1)}, u32[]{:S(2)}, u32[]{:S(2)}) %collective-permute-start.56) | collective-permute-done | bytes 589856 | tf_op jit(solution)/shard_map/ppermute | solution.py:64
  277.3 6.0 %collective-permute-done.62 = bf16[2,192,768]{2,1,0:T(8,128)(2,1)S(1)} collective-permute-done((bf16[2,192,768]{2,1,0:T(8,128)(2,1)}, bf16[2,192,768]{2,1,0:T(8,128)(2,1)S(1)}, u32[]{:S(2)}, u32[]{:S(2)}) %collective-permute-start.62) | collective-permute-done | bytes 589856 | tf_op jit(solution)/shard_map/ppermute | solution.py:64
  283.3 9.8 %collective-permute-done.63 = bf16[2,192,768]{2,1,0:T(8,128)(2,1)S(1)} collective-permute-done((bf16[2,192,768]{2,1,0:T(8,128)(2,1)}, bf16[2,192,768]{2,1,0:T(8,128)(2,1)S(1)}, u32[]{:S(2)}, u32[]{:S(2)}) %collective-permute-start.63) | collective-permute-done | bytes 589856 | tf_op jit(solution)/shard_map/ppermute | solution.py:64
  299.5 8.2 %collective-permute-done.50.refs_4_ = bf16[64,3072]{1,0:T(8,128)(2,1)S(1)} collective-permute-done((bf16[64,3072]{1,0:T(8,128)(2,1)S(1)}, bf16[64,3072]{1,0:T(8,128)(2,1)S(1)}, u32[]{:S(2)}, u32[]{:S(2)}) %collective-permute-start.50) | collective-permute-done | bytes 393248 | tf_op jit(solution)/shard_map/ppermute | solution.py:68
  309.1 8.2 %collective-permute-done.48.refs_2_ = bf16[64,3072]{1,0:T(8,128)(2,1)S(1)} collective-permute-done((bf16[64,3072]{1,0:T(8,128)(2,1)S(1)}, bf16[64,3072]{1,0:T(8,128)(2,1)S(1)}, u32[]{:S(2)}, u32[]{:S(2)}) %collective-permute-start.48) | collective-permute-done | bytes 393248 | tf_op jit(solution)/shard_map/ppermute | solution.py:68
  (252 shorter events, 122.6 us)
Async XLA Ops:
  8.0 33.9 %collective-permute-start.10 = (bf16[512,256]{1,0:T(8,128)(2,1)}, bf16[512,256]{1,0:T(8,128)(2,1)S(1)}, u32[]{:S(2)}, u32[]{:S(2)}) collective-permute-start(bf16[512,256]{1,0:T(8,128)(2,1)} %get-tuple-element.56.o_ref), channel_id=1, source_target_pairs={{0,8},{8,0},{16,24},{24,16},{32,40},{40,32},{48,56},{56,48},{64,72... | collective-permute-start | bytes 786440 | tf_op jit(solution)/shard_map/ppermute | solution.py:64
  8.0 30.7 %collective-permute-start.9 = (bf16[512,256]{1,0:T(8,128)(2,1)}, bf16[512,256]{1,0:T(8,128)(2,1)}, u32[]{:S(2)}, u32[]{:S(2)}) collective-permute-start(bf16[512,256]{1,0:T(8,128)(2,1)} %get-tuple-element.56.o_ref), channel_id=1, source_target_pairs={{0,112},{8,24},{16,0},{24,40},{32,16},{40,56},{48,32},{56,72},{64,... | collective-permute-start | bytes 786440 | tf_op jit(solution)/shard_map/ppermute | solution.py:64
  14.6 27.4 %collective-permute-start.8 = (bf16[512,256]{1,0:T(8,128)(2,1)}, bf16[512,256]{1,0:T(8,128)(2,1)}, u32[]{:S(2)}, u32[]{:S(2)}) collective-permute-start(bf16[512,256]{1,0:T(8,128)(2,1)} %get-tuple-element.56.o_ref), channel_id=1, source_target_pairs={{0,16},{8,120},{16,32},{24,8},{32,48},{40,24},{48,64},{56,40},{64,... | collective-permute-start | bytes 786440 | tf_op jit(solution)/shard_map/ppermute | solution.py:64
  14.6 55.0 %collective-permute-start.2 = (bf16[512,256]{1,0:T(8,128)(2,1)}, bf16[512,256]{1,0:T(8,128)(2,1)}, u32[]{:S(2)}, u32[]{:S(2)}) collective-permute-start(bf16[512,256]{1,0:T(8,128)(2,1)} %get-tuple-element.50.o_ref), channel_id=1, source_target_pairs={{0,8},{8,0},{16,24},{24,16},{32,40},{40,32},{48,56},{56,48},{64,72... | collective-permute-start | bytes 786440 | tf_op jit(solution)/shard_map/ppermute | solution.py:64
  14.8 26.6 %collective-permute-start.5 = (bf16[512,256]{1,0:T(8,128)(2,1)}, bf16[512,256]{1,0:T(8,128)(2,1)}, u32[]{:S(2)}, u32[]{:S(2)}) collective-permute-start(bf16[512,256]{1,0:T(8,128)(2,1)} %get-tuple-element.54.o_ref), channel_id=1, source_target_pairs={{0,112},{8,24},{16,0},{24,40},{32,16},{40,56},{48,32},{56,72},{64,... | collective-permute-start | bytes 786440 | tf_op jit(solution)/shard_map/ppermute | solution.py:64
  56.2 28.8 %collective-permute-start.33 = (bf16[512,256]{1,0:T(8,128)(2,1)}, bf16[512,256]{1,0:T(8,128)(2,1)S(1)}, u32[]{:S(2)}, u32[]{:S(2)}) collective-permute-start(bf16[512,256]{1,0:T(8,128)(2,1)} %get-tuple-element.77), channel_id=1, source_target_pairs={{0,112},{8,24},{16,0},{24,40},{32,16},{40,56},{48,32},{56,72},{64,... | collective-permute-start | bytes 786440 | tf_op jit(solution)/shard_map/ppermute | solution.py:64
  119.2 32.9 %collective-permute-start.36 = (bf16[8,192,512]{2,1,0:T(8,128)(2,1)}, bf16[8,192,512]{2,1,0:T(8,128)(2,1)S(1)}, u32[]{:S(2)}, u32[]{:S(2)}) collective-permute-start(bf16[8,192,512]{2,1,0:T(8,128)(2,1)} %get-tuple-element.52._g), channel_id=1, source_target_pairs={{0,8},{8,0},{16,24},{24,16},{32,40},{40,32},{48,56},{56,48},{64,72... | collective-permute-start | bytes 4718600 | tf_op jit(solution)/shard_map/ppermute | solution.py:64
  119.2 40.4 %collective-permute-start.35 = (bf16[8,192,512]{2,1,0:T(8,128)(2,1)}, bf16[8,192,512]{2,1,0:T(8,128)(2,1)S(1)}, u32[]{:S(2)}, u32[]{:S(2)}) collective-permute-start(bf16[8,192,512]{2,1,0:T(8,128)(2,1)} %get-tuple-element.51._x), channel_id=1, source_target_pairs={{0,8},{8,0},{16,24},{24,16},{32,40},{40,32},{48,56},{56,48},{64,72... | collective-permute-start | bytes 4718600 | tf_op jit(solution)/shard_map/ppermute | solution.py:64
  155.3 33.9 %collective-permute-start.25 = (bf16[64,3072]{1,0:T(8,128)(2,1)S(1)}, bf16[64,3072]{1,0:T(8,128)(2,1)S(1)}, u32[]{:S(2)}, u32[]{:S(2)}) collective-permute-start(bf16[64,3072]{1,0:T(8,128)(2,1)S(1)} %add_convert_fusion.1.refs_0_), channel_id=1, source_target_pairs={{0,6},{1,7},{2,0},{3,1},{4,2},{5,3},{6,4},{7,5},{8,14},{9,15},{10,... | collective-permute-start | bytes 1179656 | tf_op jit(solution)/shard_map/ppermute | solution.py:68
  155.4 34.6 %collective-permute-start.24 = (bf16[64,3072]{1,0:T(8,128)(2,1)S(1)}, bf16[64,3072]{1,0:T(8,128)(2,1)S(1)}, u32[]{:S(2)}, u32[]{:S(2)}) collective-permute-start(bf16[64,3072]{1,0:T(8,128)(2,1)S(1)} %add_convert_fusion.1.refs_0_), channel_id=1, source_target_pairs={{0,5},{1,4},{2,7},{3,6},{4,1},{5,0},{6,3},{7,2},{8,13},{9,12},{10,... | collective-permute-start | bytes 1179656 | tf_op jit(solution)/shard_map/ppermute | solution.py:68
  157.8 33.4 %collective-permute-start.23 = (bf16[64,3072]{1,0:T(8,128)(2,1)S(1)}, bf16[64,3072]{1,0:T(8,128)(2,1)S(1)}, u32[]{:S(2)}, u32[]{:S(2)}) collective-permute-start(bf16[64,3072]{1,0:T(8,128)(2,1)S(1)} %add_convert_fusion.1.refs_0_), channel_id=1, source_target_pairs={{0,4},{1,5},{2,6},{3,7},{4,0},{5,1},{6,2},{7,3},{8,12},{9,13},{10,... | collective-permute-start | bytes 1179656 | tf_op jit(solution)/shard_map/ppermute | solution.py:68
  159.6 31.7 %collective-permute-start.22 = (bf16[64,3072]{1,0:T(8,128)(2,1)S(1)}, bf16[64,3072]{1,0:T(8,128)(2,1)S(1)}, u32[]{:S(2)}, u32[]{:S(2)}) collective-permute-start(bf16[64,3072]{1,0:T(8,128)(2,1)S(1)} %add_convert_fusion.1.refs_0_), channel_id=1, source_target_pairs={{0,3},{1,2},{2,5},{3,4},{4,7},{5,6},{6,1},{7,0},{8,11},{9,10},{10,... | collective-permute-start | bytes 1179656 | tf_op jit(solution)/shard_map/ppermute | solution.py:68
  191.3 38.9 %collective-permute-start.42 = (bf16[64,3072]{1,0:T(8,128)(2,1)}, bf16[64,3072]{1,0:T(8,128)(2,1)S(1)}, u32[]{:S(2)}, u32[]{:S(2)}) collective-permute-start(bf16[64,3072]{1,0:T(8,128)(2,1)} %get-tuple-element.84), channel_id=1, source_target_pairs={{0,3},{1,2},{2,5},{3,4},{4,7},{5,6},{6,1},{7,0},{8,11},{9,10},{10,... | collective-permute-start | bytes 1179656 | tf_op jit(solution)/shard_map/ppermute | solution.py:68
  194.8 55.5 %collective-permute-start.54 = (bf16[2,192,768]{2,1,0:T(8,128)(2,1)}, bf16[2,192,768]{2,1,0:T(8,128)(2,1)S(1)}, u32[]{:S(2)}, u32[]{:S(2)}) collective-permute-start(bf16[2,192,768]{2,1,0:T(8,128)(2,1)} %get-tuple-element.89), channel_id=1, source_target_pairs={{0,16},{8,24},{16,32},{24,40},{32,48},{40,56},{48,0},{56,8},{64,80... | collective-permute-start | bytes 1769480 | tf_op jit(solution)/shard_map/ppermute | solution.py:64
  202.0 42.7 %collective-permute-start.43 = (bf16[64,3072]{1,0:T(8,128)(2,1)}, bf16[64,3072]{1,0:T(8,128)(2,1)S(1)}, u32[]{:S(2)}, u32[]{:S(2)}) collective-permute-start(bf16[64,3072]{1,0:T(8,128)(2,1)} %get-tuple-element.85), channel_id=1, source_target_pairs={{0,4},{1,5},{2,6},{3,7},{4,0},{5,1},{6,2},{7,3},{8,12},{9,13},{10,... | collective-permute-start | bytes 1179656 | tf_op jit(solution)/shard_map/ppermute | solution.py:68
  209.6 35.1 %collective-permute-start.44 = (bf16[64,3072]{1,0:T(8,128)(2,1)}, bf16[64,3072]{1,0:T(8,128)(2,1)S(1)}, u32[]{:S(2)}, u32[]{:S(2)}) collective-permute-start(bf16[64,3072]{1,0:T(8,128)(2,1)} %get-tuple-element.86), channel_id=1, source_target_pairs={{0,5},{1,4},{2,7},{3,6},{4,1},{5,0},{6,3},{7,2},{8,13},{9,12},{10,... | collective-permute-start | bytes 1179656 | tf_op jit(solution)/shard_map/ppermute | solution.py:68
  209.7 35.2 %collective-permute-start.45 = (bf16[64,3072]{1,0:T(8,128)(2,1)}, bf16[64,3072]{1,0:T(8,128)(2,1)S(1)}, u32[]{:S(2)}, u32[]{:S(2)}) collective-permute-start(bf16[64,3072]{1,0:T(8,128)(2,1)} %get-tuple-element.87), channel_id=1, source_target_pairs={{0,6},{1,7},{2,0},{3,1},{4,2},{5,3},{6,4},{7,5},{8,14},{9,15},{10,... | collective-permute-start | bytes 1179656 | tf_op jit(solution)/shard_map/ppermute | solution.py:68
  244.7 27.4 %collective-permute-start.56 = (bf16[2,192,768]{2,1,0:T(8,128)(2,1)S(1)}, bf16[2,192,768]{2,1,0:T(8,128)(2,1)S(1)}, u32[]{:S(2)}, u32[]{:S(2)}) collective-permute-start(bf16[2,192,768]{2,1,0:T(8,128)(2,1)S(1)} %copy-done.41), channel_id=1, source_target_pairs={{0,48},{8,56},{16,0},{24,8},{32,16},{40,24},{48,32},{56,40},{64,11... | collective-permute-start | bytes 1769480 | tf_op jit(solution)/shard_map/ppermute | solution.py:64
  244.8 30.2 %collective-permute-start.61 = (bf16[2,192,768]{2,1,0:T(8,128)(2,1)}, bf16[2,192,768]{2,1,0:T(8,128)(2,1)S(1)}, u32[]{:S(2)}, u32[]{:S(2)}) collective-permute-start(bf16[2,192,768]{2,1,0:T(8,128)(2,1)} %get-tuple-element.93), channel_id=1, source_target_pairs={{0,16},{8,24},{16,32},{24,40},{32,48},{40,56},{48,0},{56,8},{64,80... | collective-permute-start | bytes 1769480 | tf_op jit(solution)/shard_map/ppermute | solution.py:64
  246.9 36.4 %collective-permute-start.62 = (bf16[2,192,768]{2,1,0:T(8,128)(2,1)}, bf16[2,192,768]{2,1,0:T(8,128)(2,1)S(1)}, u32[]{:S(2)}, u32[]{:S(2)}) collective-permute-start(bf16[2,192,768]{2,1,0:T(8,128)(2,1)} %get-tuple-element.94), channel_id=1, source_target_pairs={{0,32},{8,40},{16,48},{24,56},{32,0},{40,8},{48,16},{56,24},{64,96... | collective-permute-start | bytes 1769480 | tf_op jit(solution)/shard_map/ppermute | solution.py:64
  250.3 42.8 %collective-permute-start.63 = (bf16[2,192,768]{2,1,0:T(8,128)(2,1)}, bf16[2,192,768]{2,1,0:T(8,128)(2,1)S(1)}, u32[]{:S(2)}, u32[]{:S(2)}) collective-permute-start(bf16[2,192,768]{2,1,0:T(8,128)(2,1)} %get-tuple-element.95), channel_id=1, source_target_pairs={{0,48},{8,56},{16,0},{24,8},{32,16},{40,24},{48,32},{56,40},{64,11... | collective-permute-start | bytes 1769480 | tf_op jit(solution)/shard_map/ppermute | solution.py:64
  262.5 33.1 %collective-permute-start.53 = (bf16[64,3072]{1,0:T(8,128)(2,1)S(1)}, bf16[64,3072]{1,0:T(8,128)(2,1)S(1)}, u32[]{:S(2)}, u32[]{:S(2)}) collective-permute-start(bf16[64,3072]{1,0:T(8,128)(2,1)S(1)} %add_convert_fusion.refs_0_), channel_id=1, source_target_pairs={{0,7},{1,6},{2,1},{3,0},{4,3},{5,2},{6,5},{7,4},{8,15},{9,14},{10,... | collective-permute-start | bytes 1179656 | tf_op jit(solution)/shard_map/ppermute | solution.py:68
  283.3 24.4 %collective-permute-start.50 = (bf16[64,3072]{1,0:T(8,128)(2,1)S(1)}, bf16[64,3072]{1,0:T(8,128)(2,1)S(1)}, u32[]{:S(2)}, u32[]{:S(2)}) collective-permute-start(bf16[64,3072]{1,0:T(8,128)(2,1)S(1)} %add_convert_fusion.refs_0_), channel_id=1, source_target_pairs={{0,4},{1,5},{2,6},{3,7},{4,0},{5,1},{6,2},{7,3},{8,12},{9,13},{10,... | collective-permute-start | bytes 1179656 | tf_op jit(solution)/shard_map/ppermute | solution.py:68
  296.5 27.1 %collective-permute-start.57 = (bf16[192,768]{1,0:T(8,128)(2,1)S(1)}, bf16[192,768]{1,0:T(8,128)(2,1)S(1)}, u32[]{:S(2)}, u32[]{:S(2)}) collective-permute-start(bf16[192,768]{1,0:T(8,128)(2,1)S(1)} %fusion.16), channel_id=1, source_target_pairs={{0,64},{8,72},{16,80},{24,88},{32,96},{40,104},{48,112},{56,120},{... | collective-permute-start | bytes 884744 | tf_op jit(solution)/shard_map/ppermute | solution.py:64
  (97 other events, 1469.6 us)

commit v2 on v1

v2 whole, which is shorter than its diff:
```python
import functools
import math

import jax
import jax.numpy as jnp
from jax import lax
from jax.experimental import pallas as pl
from jax.experimental.pallas import tpu as pltpu
from jax.sharding import PartitionSpec as P

D = 3072
HEADS = 24
E = 128
TOK = 512
LH = 3
LW = LH * E
ROWS = D // 16
SCALE = 1.0 / math.sqrt(E)
EXP2_SCALE = SCALE * math.log2(math.e)
BF = jnp.bfloat16
F32 = jnp.float32
VMEM_LIMIT = 56 << 20


def sds(shape, dtype):
    return jax.ShapeDtypeStruct(shape, dtype)


def dot(a, b, dims=((1,), (0,))):
    return lax.dot_general(a, b, (dims, ((), ())), preferred_element_type=F32)


def params():
    return pltpu.CompilerParams(vmem_limit_bytes=VMEM_LIMIT)


def cost(flops, moved, exps=0):
    return pl.CostEstimate(flops=int(flops), bytes_accessed=int(moved), transcendentals=int(exps))


def view_route(step):
    return [(v, step(v) % 16) for v in range(16)]


SWAP = view_route(lambda v: v ^ 1)
NEAR = view_route(lambda v: v + 2 if v % 2 == 0 else v - 2)
FAR = view_route(lambda v: v - 2 if v % 2 == 0 else v + 2)


BACK_ONE = view_route(lambda v: v - 1 if v % 2 == 0 else v + 1)
HEAD_STEPS = [(dy, dx) for dx in range(2) for dy in range(4)]
HALF = D // 2
X_LO = (0, 1)


def head_route(dy, dx):
    return [(h, ((h // 2 + dy) % 4) * 2 + (h % 2 ^ dx)) for h in range(8)]


def over_view(block, route):
    return lax.ppermute(block, "view", route)


def over_head(block, step):
    return lax.ppermute(block, "head", head_route(*step))


def kv_kernel(x_ref, wk_ref, wv_ref, kv_ref, acc):
    step = pl.program_id(0)
    x = x_ref[...]
    k = dot(x, wk_ref[...])
    v = dot(x, wv_ref[...])

    @pl.when(step == 0)
    def _():
        acc[:, :LW] = k
        acc[:, LW:] = v

    @pl.when((step > 0) & (step < 3))
    def _():
        acc[:, :LW] += k
        acc[:, LW:] += v

    @pl.when(step == 3)
    def _():
        for h in range(LH):
            cols = slice(h * E, (h + 1) * E)
            kv_ref[h, :, :E] = (acc[:, cols] + k[:, cols]).astype(BF)
            kv_ref[h, :, E:] = (acc[:, LW + h * E : LW + (h + 1) * E] + v[:, cols]).astype(BF)


def project_kv(x, w3):
    depth = D // 4
    return pl.pallas_call(
        kv_kernel,
        grid=(4,),
        in_specs=[
            pl.BlockSpec((TOK, depth), lambda i: (0, i)),
            pl.BlockSpec((None, depth, LW), lambda i: (1, i, 0)),
            pl.BlockSpec((None, depth, LW), lambda i: (2, i, 0)),
        ],
        out_specs=pl.BlockSpec((LH, TOK, 2 * E), lambda i: (0, 0, 0)),
        out_shape=sds((LH, TOK, 2 * E), BF),
        scratch_shapes=[pltpu.VMEM((TOK, 2 * LW), F32)],
        compiler_params=params(),
        cost_estimate=cost(2 * TOK * D * 2 * LW, 9 << 20),
    )(x, w3, w3)


def attention_kernel(q_ref, g_ref, o_ref, a_ref, b_ref, c_ref, r_ref, *refs):
    att_dq_ref, d_o, d_a, d_bc, d_r, s_scr, dp_scr = refs[-7:]
    n = TOK
    kvs = (o_ref, a_ref, b_ref, c_ref, r_ref)
    outs = (d_o, d_a, d_bc.at[0], d_bc.at[1], d_r)
    q = q_ref[...]
    g = g_ref[...]
    q_t = q.T
    g_t = g.T
    top = None
    for j, kv in enumerate(kvs):
        s = dot(kv[:, :E], q_t)
        s_scr[j * n : (j + 1) * n] = s
        here = jnp.max(s, axis=0, keepdims=True)
        top = here if top is None else jnp.maximum(top, here)
    top = top * EXP2_SCALE
    total = None
    for j in range(5):
        e = jnp.exp2(s_scr[j * n : (j + 1) * n] * EXP2_SCALE - top)
        s_scr[j * n : (j + 1) * n] = e
        here = jnp.sum(e, axis=0, keepdims=True)
        total = here if total is None else total + here
    inverse = 1.0 / total
    delta = None
    acc = None
    for j, kv in enumerate(kvs):
        p = s_scr[j * n : (j + 1) * n] * inverse
        s_scr[j * n : (j + 1) * n] = p
        p_bf = p.astype(BF)
        v = kv[:, E:]
        dp = dot(v, g_t)
        dp_scr[j * n : (j + 1) * n] = dp
        here = jnp.sum(p * dp, axis=0, keepdims=True)
        delta = here if delta is None else delta + here
        term = dot(v.T, p_bf)
        acc = term if acc is None else acc + term
        outs[j][:, E:] = dot(p_bf, g).astype(outs[j].dtype)
    att_dq_ref[0] = acc.T.astype(BF)
    acc = None
    for j, kv in enumerate(kvs):
        ds = (s_scr[j * n : (j + 1) * n] * (dp_scr[j * n : (j + 1) * n] - delta) * SCALE).astype(BF)
        k = kv[:, :E]
        term = dot(k.T, ds)
        acc = term if acc is None else acc + term
        outs[j][:, :E] = dot(ds, q).astype(outs[j].dtype)
    att_dq_ref[1] = acc.T.astype(BF)


def attention(queries, d_att, kvs):
    head_block = pl.BlockSpec((TOK, E), lambda h: (0, h))
    pair = pl.BlockSpec((None, TOK, 2 * E), lambda h: (h, 0, 0))
    return pl.pallas_call(
        attention_kernel,
        grid=(LH,),
        in_specs=[head_block, head_block] + [pair] * 5,
        out_specs=[
            pl.BlockSpec((2, TOK, E), lambda h: (0, 0, h)),
            pair,
            pair,
            pl.BlockSpec((2, None, TOK, 2 * E), lambda h: (0, h, 0, 0)),
            pair,
        ],
        out_shape=[
            sds((2, TOK, LW), BF),
            sds((LH, TOK, 2 * E), F32),
            sds((LH, TOK, 2 * E), BF),
            sds((2, LH, TOK, 2 * E), BF),
            sds((LH, TOK, 2 * E), F32),
        ],
        scratch_shapes=[pltpu.VMEM((5 * TOK, TOK), F32)] * 2,
        compiler_params=params(),
        cost_estimate=cost(LH * 6 * 2 * TOK * 5 * TOK * E * 2, 12 << 20, LH * 5 * TOK * TOK),
    )(queries, d_att, *kvs)


COLS = D // 4


def left_tile(rows):
    return pl.BlockSpec((rows, COLS), lambda t, *s: (0, jnp.minimum(t, 1)))


def right_tile(rows):
    return pl.BlockSpec((rows, COLS), lambda t, *s: (0, jnp.maximum(t - 2, 0)))


def gather_rows(dest_ref, a_scr, pieces):
    for i in range(8):
        rows = pl.ds(pl.multiple_of(dest_ref[i] * 64, 64), 64)
        for at, part in pieces:
            a_scr[i * 64 : (i + 1) * 64, at : at + part.shape[1]] = part[rows, :]


def y_rows(out, dy):
    return out[dy * 64 : (dy + 1) * 64], out[256 + dy * 64 : 256 + (dy + 1) * 64]


def mixed_kernel(dest_ref, att_ref, w_ref, near_ref, far_ref, y0_ref, y1_ref, y2_ref, y3_ref, a_scr):
    tile = pl.program_id(0)

    @pl.when(tile == 0)
    def _():
        gather_rows(dest_ref, a_scr, [(0, att_ref)])

    out = dot(a_scr[...], w_ref[...], ((1,), (1,))).astype(BF)

    @pl.when(tile < 2)
    def _():
        near_ref[...] = out[:256]
        far_ref[...] = out[256:]

    @pl.when(tile >= 2)
    def _():
        for dy, ref in enumerate((y0_ref, y1_ref, y2_ref, y3_ref)):
            ref[:64], ref[64:] = y_rows(out, dy)


def mixed_product(dest, att_dq, w_out):
    return pl.pallas_call(
        mixed_kernel,
        grid_spec=pltpu.PrefetchScalarGridSpec(
            num_scalar_prefetch=1,
            grid=(4,),
            in_specs=[
                pl.BlockSpec((None, TOK, LW), lambda t, s: (0, 0, 0)),
                pl.BlockSpec((COLS, LW), lambda t, s: (t, 0)),
            ],
            out_specs=[left_tile(256)] * 2 + [right_tile(128)] * 4,
            scratch_shapes=[pltpu.VMEM((TOK, LW), BF)],
        ),
        out_shape=[sds((256, HALF), BF)] * 2 + [sds((128, HALF), BF)] * 4,
        compiler_params=params(),
        cost_estimate=cost(2 * TOK * D * LW, (LW * D + TOK * D) * 2),
    )(dest, att_dq, w_out)


def input_kernel(dest_ref, *refs):
    dq_ref, d_kv_ref, w_ref, near_in, far_in, y0_in, y1_in, y2_in, y3_in = refs[:9]
    near_ref, y0_ref, left_ref, right_ref, x_ref, y1_ref, y2_ref, y3_ref, a_scr = refs[9:]
    tile = pl.program_id(0)

    @pl.when(tile == 0)
    def _():
        pieces = [(0, dq_ref)]
        for h in range(LH):
            pieces += [(LW + E * h, d_kv_ref.at[h, :, :E]), (2 * LW + E * h, d_kv_ref.at[h, :, E:])]
        gather_rows(dest_ref, a_scr, pieces)

    a = a_scr[...]
    out = None
    for i in range(3):
        term = dot(a[:, i * LW : (i + 1) * LW], w_ref[i], ((1,), (1,)))
        out = term if out is None else out + term
    out = out.astype(BF)

    @pl.when(tile < 2)
    def _():
        near_ref[...] = out[:256]
        x_ref[:256] = out[256:]
        total = y0_in[...].astype(F32)
        for ref in (y1_in, y2_in, y3_in):
            total = total + ref[...].astype(F32)
        right_ref[...] = total[:64]
        x_ref[256:] = total[64:].astype(BF)

    @pl.when(tile >= 2)
    def _():
        total = near_in[...].astype(F32) + far_in[...].astype(F32)
        left_ref[...] = total[:64]
        y0_ref[:64], y0_ref[64:] = y_rows(out, 0)
        for dy, ref in ((1, y1_ref), (2, y2_ref), (3, y3_ref)):
            ref[:64], ref[64:128] = y_rows(out, dy)
            ref[128:] = total[dy * 64 : (dy + 1) * 64].astype(BF)


def input_product(dest, att_dq, d_kv, w3, mixed):
    return pl.pallas_call(
        input_kernel,
        grid_spec=pltpu.PrefetchScalarGridSpec(
            num_scalar_prefetch=1,
            grid=(4,),
            in_specs=[
                pl.BlockSpec((None, TOK, LW), lambda t, s: (1, 0, 0)),
                pl.BlockSpec((LH, TOK, 2 * E), lambda t, s: (0, 0, 0)),
                pl.BlockSpec((3, COLS, LW), lambda t, s: (0, t, 0)),
            ]
            + [right_tile(256)] * 2
            + [left_tile(128)] * 4,
            out_specs=[left_tile(256), right_tile(128), right_tile(64), left_tile(64), left_tile(320)]
            + [right_tile(192)] * 3,
            scratch_shapes=[pltpu.VMEM((TOK, 3 * LW), BF)],
        ),
        out_shape=[
            sds((256, HALF), BF),
            sds((128, HALF), BF),
            sds((64, HALF), F32),
            sds((64, HALF), F32),
            sds((320, HALF), BF),
        ]
        + [sds((192, HALF), BF)] * 3,
        compiler_params=params(),
        cost_estimate=cost(2 * TOK * D * 3 * LW, (3 * LW * D + 2 * TOK * D) * 2),
    )(dest, att_dq, d_kv, w3, *mixed)


def third_kernel(near_in, y0_in, left_in, right_in, x_in, y1_in, y2_in, y3_in, *refs):
    left_ref, right_ref, x_ref, y1_ref, y2_ref, y3_ref = refs
    y_in = (y1_in, y2_in, y3_in)
    mixed_left = left_in[...]
    for ref in y_in:
        mixed_left = mixed_left + ref[128:].astype(F32)
    mixed_left = mixed_left.astype(BF)
    x_ref[64:] = (right_in[...] + x_in[256:].astype(F32)).astype(BF)
    total = near_in[...].astype(F32) + x_in[:256].astype(F32)
    left_ref[...] = total[:64]
    for dy, ref in ((1, y1_ref), (2, y2_ref), (3, y3_ref)):
        ref[:64] = total[dy * 64 : (dy + 1) * 64].astype(BF)
        ref[64:] = mixed_left
    total = y0_in[...].astype(F32)
    for ref in y_in:
        total = total + ref[:128].astype(F32)
    right_ref[...] = total[:64]
    x_ref[:64] = total[64:].astype(BF)


def fourth_kernel(left_in, right_in, x_own, x_in, y_own, y1_in, y2_in, y3_in, x_ref, y_ref):
    y_in = (y1_in, y2_in, y3_in)
    left = left_in[...]
    for ref in y_in:
        left = left + ref[:64].astype(F32)
    y_ref[:64] = left.astype(BF)
    y_ref[64:128] = x_own[64:]
    y_ref[128:] = x_in[64:]
    x_ref[:64] = (right_in[...] + x_in[:64].astype(F32)).astype(BF)
    x_ref[64:128] = y_own[64:]
    for dy, ref in enumerate(y_in):
        x_ref[128 + dy * 64 : 192 + dy * 64] = ref[64:]


def fifth_kernel(x_own, x_in, y_own, y1_in, y2_in, y3_in, x_ref, y_ref):
    x_ref[:64] = y_own[:64]
    for dy, ref in enumerate((y1_in, y2_in, y3_in)):
        x_ref[64 + dy * 64 : 128 + dy * 64] = ref[:64]
    y_ref[:64] = x_own[:64]
    y_ref[64:] = x_in[:64]


def by_columns(kernel, inputs, outputs):
    def tile(rows):
        return pl.BlockSpec((rows, COLS), lambda t: (0, t))

    return pl.pallas_call(
        kernel,
        grid=(2,),
        in_specs=[tile(a.shape[0]) for a in inputs],
        out_specs=[tile(rows) for rows, _ in outputs],
        out_shape=[sds((rows, HALF), dtype) for rows, dtype in outputs],
        compiler_params=params(),
        cost_estimate=cost(5e10, 4 << 20),
    )(*inputs)


def exchange(x, ys):
    return over_head(x, X_LO), [over_head(y, (dy, 0)) for dy, y in zip((1, 2, 3), ys)]


def place_kernel(first, src_ref, own_ref, beside_ref, y0_ref, y1_ref, y2_ref, y3_ref, out_ref):
    half = pl.program_id(0)

    def rows(i):
        return pl.ds(pl.multiple_of(src_ref[i] * 64, 64), 64)

    @pl.when(half == 0)
    def _():
        for dy, ref in enumerate((y0_ref, y1_ref, y2_ref, y3_ref)):
            out_ref[rows(dy), :] = ref[first : first + 64]
            out_ref[rows(4 + dy), :] = ref[first + 64 : first + 128]

    @pl.when(half == 1)
    def _():
        for dy in range(4):
            out_ref[rows(dy), :] = own_ref[first + dy * 64 : first + (dy + 1) * 64]
            out_ref[rows(4 + dy), :] = beside_ref[first + dy * 64 : first + (dy + 1) * 64]


def place(source, first, own, beside, ys):
    def whole(rows):
        return pl.BlockSpec((rows, HALF), lambda t, s: (0, 0))

    return pl.pallas_call(
        functools.partial(place_kernel, first),
        grid_spec=pltpu.PrefetchScalarGridSpec(
            num_scalar_prefetch=1,
            grid=(2,),
            in_specs=[whole(first + 256)] * 2 + [whole(first + 128)] * 4,
            out_specs=pl.BlockSpec((TOK, HALF), lambda t, s: (0, 1 - t)),
        ),
        out_shape=sds((TOK, D), BF),
        compiler_params=params(),
        cost_estimate=cost(5e10, 4 * TOK * D),
    )(source, own, beside, *ys)


def turn_kernel(core_ref, x_ref, _, mine_ref, other_ref, scr):
    scr[...] = x_ref[...].T
    core = core_ref[0]
    for c in range(4):
        first = c * 2 * ROWS
        mine_ref[c] = scr[pl.ds(pl.multiple_of(first + core * ROWS, ROWS), ROWS), :]
        other_ref[c] = scr[pl.ds(pl.multiple_of(first + (1 - core) * ROWS, ROWS), ROWS), :]


def turn(core, x, before):
    block = pl.BlockSpec((4, ROWS, TOK), lambda c, s: (c, 0, 0))
    return pl.pallas_call(
        turn_kernel,
        grid_spec=pltpu.PrefetchScalarGridSpec(
            num_scalar_prefetch=1,
            grid=(2,),
            in_specs=[pl.BlockSpec((TOK, HALF), lambda c, s: (0, c)), pl.BlockSpec(memory_space=pl.ANY)],
            out_specs=[block, block],
            scratch_shapes=[pltpu.VMEM((HALF, TOK), BF)],
        ),
        out_shape=[sds((8, ROWS, TOK), BF)] * 2,
        compiler_params=params(),
        cost_estimate=cost(TOK * D * 64, 4 * TOK * D),
    )(core, x, before)


def weight_kernel(plan, n_lhs, n_rhs, *refs):
    lhs = refs[: 2 * n_lhs]
    rhs = refs[2 * n_lhs : 2 * n_lhs + n_rhs]
    out_ref = refs[-1]
    for pick, mine, theirs, dst in plan:
        left, right = (
            jnp.concatenate([ref[x_hi, z] for z in range(2) for x_hi in range(2)], axis=0)
            for ref in lhs[2 * pick : 2 * pick + 2]
        )
        out = dot(left, mine(rhs)) + dot(right, theirs(rhs))
        out_ref[:, dst : dst + out.shape[1]] = out.astype(BF)


def weight_terms(lhs_pairs, rhs, plan):
    lhs = [side.reshape(2, 4, ROWS, TOK) for pair in lhs_pairs for side in pair]
    rhs_specs = [pl.BlockSpec(r.shape, functools.partial(lambda nd, i: (0,) * nd, r.ndim)) for r in rhs]
    return pl.pallas_call(
        functools.partial(weight_kernel, plan, len(lhs_pairs), len(rhs)),
        grid=(2,),
        in_specs=[pl.BlockSpec((2, 2, ROWS, TOK), lambda i: (0, i, 0, 0))] * len(lhs) + rhs_specs,
        out_specs=pl.BlockSpec((4 * ROWS, 2 * LW), lambda i: (i, 0)),
        out_shape=sds((8 * ROWS, 2 * LW), BF),
        compiler_params=params(),
        cost_estimate=cost(2 * 8 * ROWS * 2 * TOK * 2 * LW, 10 << 20),
    )(*lhs, *rhs)


Z_GROUPS = [[x_hi * 8 + z * 2 + core for z in range(4)] for x_hi in range(2) for core in range(2)]
X_HI = view_route(lambda v: v + 8)


def weight_sum(x_hi, terms):
    total = lax.psum_scatter(terms, "view", scatter_dimension=0, axis_index_groups=Z_GROUPS, tiled=True)
    own = lax.dynamic_slice_in_dim(total, x_hi * ROWS, ROWS)
    other = lax.dynamic_slice_in_dim(total, (1 - x_hi) * ROWS, ROWS)
    return own, other


def with_x_hi(own, other):
    return own.astype(F32) + over_view(other, X_HI).astype(F32)


def local(x_tokens, w_qkv, w_out, grad_out):
    view = lax.axis_index("view")
    head = lax.axis_index("head")
    core = (view % 2).astype(jnp.int32)
    dest = jnp.stack([((head // 2 + dy) % 4) * 2 + (head % 2 ^ dx) for dy, dx in HEAD_STEPS]).astype(jnp.int32)
    source = jnp.stack([((head // 2 - dy) % 4) * 2 + (head % 2 ^ dx) for dy, dx in HEAD_STEPS]).astype(jnp.int32)
    core = core.reshape(1)
    w3 = jnp.transpose(w_qkv, (1, 0, 2))

    own = project_kv(x_tokens, w3)
    far = over_view(own, FAR)
    near = over_view(own, NEAR)
    beside = over_view(own, SWAP)

    queries = jnp.dot(x_tokens, w3[0], preferred_element_type=F32).astype(BF)
    d_att = jnp.dot(grad_out, w_out, preferred_element_type=F32).astype(BF)
    x_mine, x_other = turn(core, x_tokens, d_att)
    far, near, queries, d_att, x_mine, x_other = lax.optimization_barrier(
        (far, near, queries, d_att, x_mine, x_other)
    )
    relayed = over_view(far, SWAP)

    att_dq, d_own, d_near, d_swap, d_relay = attention(queries, d_att, (own, near, far, beside, relayed))

    back = over_view(d_swap, SWAP)
    mixed_near, mixed_far, mixed_y0, *mixed_y = mixed_product(dest, att_dq, w_out)
    mixed_x, mixed_y = exchange(mixed_far, mixed_y)

    relay = (d_relay + back[0].astype(F32)).astype(BF)
    two = over_view(d_near, FAR)
    one = over_view(relay, BACK_ONE)
    d_kv = (d_own + back[1].astype(F32) + two.astype(F32) + one.astype(F32)).astype(BF)

    near2, y02, left2, right2, x2, *y2 = input_product(
        dest, att_dq, d_kv, w3, (mixed_near, mixed_x, mixed_y0, *mixed_y)
    )
    from_x2, from_y2 = exchange(x2, y2)

    x_other, _ = lax.optimization_barrier((x_other, x2))
    x_theirs = over_view(x_other, SWAP)
    g_mine, g_other = turn(core, grad_out, x2)
    g_theirs = over_view(g_other, SWAP)
    att_dq_late, _ = lax.optimization_barrier((att_dq, x2))
    att_dq_theirs = over_view(att_dq_late, SWAP)
    early = weight_terms(
        [(x_mine, x_theirs), (g_mine, g_theirs)],
        [att_dq, att_dq_theirs],
        [(0, lambda r: r[0][1], lambda r: r[1][1], 0), (1, lambda r: r[0][0], lambda r: r[1][0], LW)],
    )
    early_own, early_other = weight_sum(view // 8, early)

    d_kv_late, _ = lax.optimization_barrier((d_kv, x2))
    d_kv_theirs = over_view(d_kv_late, SWAP)

    def columns(which, first):
        return lambda r: jnp.concatenate([r[which][h, :, first : first + E] for h in range(LH)], axis=1)

    late = weight_terms(
        [(x_mine, x_theirs)],
        [d_kv_late, d_kv_theirs],
        [(0, columns(0, 0), columns(1, 0), 0), (0, columns(0, E), columns(1, E), LW)],
    )
    late_sum = with_x_hi(*weight_sum(view // 8, late))

    near2, _, _ = lax.optimization_barrier((near2, late, g_mine))
    left3, right3, x3, *y3 = by_columns(
        third_kernel,
        (near2, y02, left2, right2, from_x2, *from_y2),
        [(64, F32), (64, F32), (128, BF), (128, BF), (128, BF), (128, BF)],
    )
    from_x3, from_y3 = exchange(x3, y3)
    left3, _ = lax.optimization_barrier((left3, early))
    x4, y4 = by_columns(
        fourth_kernel, (left3, right3, x3, from_x3, y3[0], *from_y3), [(320, BF), (192, BF)]
    )
    from_x4, from_y4 = exchange(x4, [y4] * 3)
    x4, late_sum = lax.optimization_barrier((x4, late_sum))
    x5, y5 = by_columns(fifth_kernel, (x4, from_x4, y4, *from_y4), [(256, BF), (128, BF)])
    early_other, _ = lax.optimization_barrier((early_other, x5))
    early_sum = with_x_hi(early_own, early_other)
    from_x5, from_y5 = exchange(x5, [y5] * 3)
    mixed_out = place(source, 64, x4, from_x4, (y4, *from_y4))
    d_input = place(source, 0, x5, from_x5, (y5, *from_y5))

    d_w = jnp.stack([early_sum[:, :LW], late_sum[:, :LW], late_sum[:, LW:]], axis=1)
    return (mixed_out, d_input, d_w, early_sum[:, LW:])


def solution(mesh):
    placed = (P("view", None), P(None, None, "head"), P(None, "head"), P("view", None))
    return jax.shard_map(
        local,
        mesh=mesh,
        in_specs=placed,
        out_specs=(P("view", None), P("view", None), P("view", None, "head"), P("view", "head")),
        check_vma=False,
    )
```

time: 334 us -> 260 us (0.78); the launches traced: 328 us -> 259 us
  starting transfers between devices: 100 us -> 49.9 us
  waiting for transfers between devices: 119 us -> 82.2 us
  between operations: 1.77 us -> 14.3 us
  local copies, waits for them, and re-layouts: 6.49 us -> 14 us
    ppermute x28 -> x20, waiting for transfers between devices: 64.8 us -> 28.4 us  [over_head(): return lax.ppermute(block, 'head', head_route(*step))]
    ppermute x37 -> x13, starting transfers between devices: 48.1 us -> 21.9 us  [over_view(): return lax.ppermute(block, 'view', route)]
    ppermute x28 -> x20, starting transfers between devices: 52.1 us -> 28 us  [over_head(): return lax.ppermute(block, 'head', head_route(*step))]
    ppermute x37 -> x13, waiting for transfers between devices: 54.5 us -> 41.1 us  [over_view(): return lax.ppermute(block, 'view', route)]
    reduce_scatter x0 -> x2, waiting for transfers between devices: none -> 12.7 us  [weight_sum(): lax.psum_scatter(terms, 'view', scatter_dimension=0, axis_index_groups=Z_...]
    pallas_call x7 -> x8, Pallas kernels: 48.5 us -> 55.8 us  [the longest x1 18.5 us: attention(): pl.pallas_call(attention_kernel, grid=(LH,), in_specs=[head_block, head_b...]
    unnamed x112 -> x54, local copies, waits for them, and re-layouts: 3.69 us -> 10 us
    pallas_call x2, Pallas kernels: 13.5 us -> 7.49 us  [turn(): pl.pallas_call(turn_kernel, grid_spec=pltpu.PrefetchScalarGridSpec(num_sc...]
  transfers between devices with their start and end apart: 65 -> 35, of which waited for: 19 -> 13; matrix products, arithmetic and copies ran while one was open for 5% -> 7% of each run, Pallas kernels for 24% -> 15%
where the time goes in v2:
time: 260 us; the launch traced here: 259 us
  Pallas kernels  84.2 us (32%)
  waiting for transfers between devices  82.2 us (32%)
  starting transfers between devices  49.9 us (19%)
  between operations  14.3 us (6%)
  local copies, waits for them, and re-layouts  14 us (5%)
  matrix products  8.41 us (3%)
  other arithmetic  5.73 us (2%)
    ppermute x13, waiting for transfers between devices, over_view(): return lax.ppermute(block, 'view', route)  41.1 us
    ppermute x20, waiting for transfers between devices, over_head(): return lax.ppermute(block, 'head', head_route(*step))  28.4 us
    ppermute x20, starting transfers between devices, over_head(): return lax.ppermute(block, 'head', head_route(*step))  28 us
    ppermute x13, starting transfers between devices, over_view(): return lax.ppermute(block, 'view', route)  21.9 us
    pallas_call x1, Pallas kernels, attention(): pl.pallas_call(attention_kernel, grid=(LH,), in_specs=[head_block, head_b...  18.5 us
    pallas_call x2, Pallas kernels, weight_terms(): pl.pallas_call(functools.partial(weight_kernel, plan, len(lhs_pairs), len...  13.4 us
    reduce_scatter x2, waiting for transfers between devices, weight_sum(): lax.psum_scatter(terms, 'view', scatter_dimension=0, axis_index_groups=Z_...  12.7 us
    pallas_call x1, Pallas kernels, input_product(): pl.pallas_call(input_kernel, grid_spec=pltpu.PrefetchScalarGridSpec(num_s...  12 us
  transfers between devices with their start and end apart: 35, of which 13 were waited for; matrix products, arithmetic and copies ran while one was open for 7% of the time, Pallas kernels for 15%

profile of v2, /device:TPU:0, one launch (start us, length us, event | category | flops | bytes accessed | tf_op | source)
XLA Modules:
  0.0 258.8 jit_solution(8350058579055245776)
XLA Ops:
  7.2 7.5 %shard_map.75.o_ref = bf16[3,512,256]{2,1,0:T(8,128)(2,1)} custom-call(bf16[512,3072]{1,0:T(8,128)(2,1)} %x_ref.4, bf16[3,3072,384]{2,1,0:T(8,128)(2,1)} %bitcast.44, bf16[3,3072,384]{2,1,0:T(8,128)(2,1)} %bitcast.45), custom_call_target="tpu_custom_call" | custom-call | flops 2415919104 | bytes 9437184 | tf_op jit(solution)/shard_map/pallas_call | solution.py:94
  16.7 4.7 %collective-permute-start = (bf16[3,512,256]{2,1,0:T(8,128)(2,1)}, bf16[3,512,256]{2,1,0:T(8,128)(2,1)}, u32[]{:S(2)}, u32[]{:S(2)}) collective-permute-start(bf16[3,512,256]{2,1,0:T(8,128)(2,1)} %shard_map.75.o_ref), channel_id=1, source_target_pairs={{0,112},{8,24},{16,0},{24,40},{32,16},{40,56},{48,32},{56,72},{64,... | collective-permute-start | bytes 2359304 | tf_op jit(solution)/shard_map/ppermute | solution.py:61
  21.4 4.2 %convolution_convert_fusion._.g_ref = bf16[512,384]{1,0:T(8,128)(2,1)} fusion(bf16[512,3072]{1,0:T(8,128)(2,1)S(1)} %copy-done.1, bf16[3072,384]{1,0:T(8,128)(2,1)} %w_ref.1), kind=kOutput, calls=%fused_computation.9 | convolution fusion | flops 1208156160 | bytes 5898240 | tf_op jit(solution)/shard_map/dot_general | solution.py:496
  25.6 3.8 %shard_map.76 = (bf16[8,192,512]{2,1,0:T(8,128)(2,1)}, bf16[8,192,512]{2,1,0:T(8,128)(2,1)}) custom-call(s32[1]{0:T(128)} %bitcast.16.core_ref, bf16[512,3072]{1,0:T(8,128)(2,1)} %x_ref.4, bf16[512,384]{1,0:T(8,128)(2,1)} %convolution_convert_fusion._.g_ref), custom_call_target="tpu_custom_call" | custom-call | flops 100663296 | bytes 6291456 | tf_op jit(solution)/shard_map/pallas_call | solution.py:424
  29.4 4.2 %fusion.5.q_ref = bf16[512,384]{1,0:T(8,128)(2,1)} fusion(bf16[512,3072]{1,0:T(8,128)(2,1)S(1)} %copy-done, bf16[3,3072,384]{2,1,0:T(8,128)(2,1)} %bitcast.46), kind=kOutput, calls=%fused_computation.8 | convolution fusion | flops 1208156160 | bytes 5898240 | tf_op jit(solution)/shard_map/dot_general | solution.py:495
  35.0 4.1 %collective-permute-done.b_ref = bf16[3,512,256]{2,1,0:T(8,128)(2,1)} collective-permute-done((bf16[3,512,256]{2,1,0:T(8,128)(2,1)}, bf16[3,512,256]{2,1,0:T(8,128)(2,1)}, u32[]{:S(2)}, u32[]{:S(2)}) %collective-permute-start) | collective-permute-done | bytes 786464 | tf_op jit(solution)/shard_map/ppermute | solution.py:61
  42.9 18.5 %shard_map.77 = (bf16[2,512,384]{2,1,0:T(8,128)(2,1)}, f32[3,512,256]{2,1,0:T(8,128)}, bf16[3,512,256]{2,1,0:T(8,128)(2,1)}, bf16[2,3,512,256]{3,2,1,0:T(8,128)(2,1)}, f32[3,512,256]{2,1,0:T(8,128)}) custom-call(bf16[512,384]{1,0:T(8,128)(2,1)} %fusion.5.q_ref, bf16[512,384]{1,0:T(8,128)(2,1)} %convolution_convert_fusion._.g_ref, ...), custom_call_target="tpu_custom_call" | custom-call | flops 12079595520 | bytes 12582912 | tf_op jit(solution)/shard_map/pallas_call | solution.py:161
  61.7 5.5 %collective-permute-start.5 = (bf16[3,512,256]{2,1,0:T(8,128)(2,1)}, bf16[3,512,256]{2,1,0:T(8,128)(2,1)S(1)}, u32[]{:S(2)}, u32[]{:S(2)}) collective-permute-start(bf16[3,512,256]{2,1,0:T(8,128)(2,1)} %get-tuple-element.60), channel_id=1, source_target_pairs={{0,112},{8,24},{16,0},{24,40},{32,16},{40,56},{48,32},{56,72},{64,... | collective-permute-start | bytes 2359304 | tf_op jit(solution)/shard_map/ppermute | solution.py:61
  73.6 6.6 %shard_map.78 = (bf16[256,1536]{1,0:T(8,128)(2,1)}, bf16[256,1536]{1,0:T(8,128)(2,1)}, bf16[128,1536]{1,0:T(8,128)(2,1)}, bf16[128,1536]{1,0:T(8,128)(2,1)}, bf1...) custom-call(s32[8]{0:T(128)} %stack.77.dest_ref, bf16[2,512,384]{2,1,0:T(8,128)(2,1)} %get-tuple-element.84.att_ref.refs_0_.refs_4_, ...), custom_call_target="tpu_custom_call" | custom-call | flops 1207959552 | bytes 5505024 | tf_op jit(solution)/shard_map/pallas_call | solution.py:228
  86.6 7.2 %collective-permute-done.6 = bf16[3,512,256]{2,1,0:T(8,128)(2,1)S(1)} collective-permute-done((bf16[3,512,256]{2,1,0:T(8,128)(2,1)}, bf16[3,512,256]{2,1,0:T(8,128)(2,1)S(1)}, u32[]{:S(2)}, u32[]{:S(2)}) %collective-permute-start.6) | collective-permute-done | bytes 786464 | tf_op jit(solution)/shard_map/ppermute | solution.py:61
  97.6 5.7 %collective-permute-done.7.refs_4_ = bf16[256,1536]{1,0:T(8,128)(2,1)S(1)} collective-permute-done((bf16[256,1536]{1,0:T(8,128)(2,1)}, bf16[256,1536]{1,0:T(8,128)(2,1)S(1)}, u32[]{:S(2)}, u32[]{:S(2)}) %collective-permute-start.7) | collective-permute-done | bytes 786464 | tf_op jit(solution)/shard_map/ppermute | solution.py:65
  104.2 12.0 %shard_map.79 = (bf16[256,1536]{1,0:T(8,128)(2,1)}, bf16[128,1536]{1,0:T(8,128)(2,1)}, f32[64,1536]{1,0:T(8,128)}, f32[64,1536]{1,0:T(8,128)}, bf16[320,1536]{1,...) custom-call(s32[8]{0:T(128)} %stack.77.dest_ref, ...), custom_call_target="tpu_custom_call" | custom-call | flops 3623878656 | bytes 13369344 | tf_op jit(solution)/shard_map/pallas_call | solution.py:286
  124.0 3.6 %shard_map.81 = (bf16[8,192,512]{2,1,0:T(8,128)(2,1)}, bf16[8,192,512]{2,1,0:T(8,128)(2,1)}) custom-call(s32[1]{0:T(128)} %bitcast.16.core_ref, bf16[512,3072]{1,0:T(8,128)(2,1)} %x_ref.5, bf16[320,1536]{1,0:T(8,128)(2,1)} %get-tuple-element.71._), custom_call_target="tpu_custom_call" | custom-call | flops 100663296 | bytes 6291456 | tf_op jit(solution)/shard_map/pallas_call | solution.py:424
  128.8 6.5 %shard_map.80 = bf16[1536,768]{1,0:T(8,128)(2,1)} custom-call(bf16[2,4,192,512]{3,2,1,0:T(8,128)(2,1)} %bitcast.48, bf16[2,4,192,512]{3,2,1,0:T(8,128)(2,1)} %bitcast.50, bf16[3,512,256]{2,1,0:T(8,128)(2,1)} %fusion.4.refs_1_.refs_2_, bf16[3,512,256]{2,1,0:T(8,128)(2,1)} %copy-done.14), custom_call_target="tpu_custom_call" | custom-call | flops 2415919104 | bytes 10485760 | tf_op jit(solution)/shard_map/pallas_call | solution.py:455
  136.7 11.9 %collective-permute-done.15.y2_in = bf16[192,1536]{1,0:T(8,128)(2,1)} collective-permute-done((bf16[192,1536]{1,0:T(8,128)(2,1)}, bf16[192,1536]{1,0:T(8,128)(2,1)}, u32[]{:S(2)}, u32[]{:S(2)}) %collective-permute-start.15) | collective-permute-done | bytes 589856 | tf_op jit(solution)/shard_map/ppermute | solution.py:65
  148.6 3.7 %shard_map.82 = (f32[64,1536]{1,0:T(8,128)}, f32[64,1536]{1,0:T(8,128)}, bf16[128,1536]{1,0:T(8,128)(2,1)}, bf16[128,1536]{1,0:T(8,128)(2,1)}, bf16[128,1536]{1,0:T(8,128)(2,1)}, /*index=5*/bf16[128,1536]{1,0:T(8,128)(2,1)}) custom-call(bf16[256,1536]{1,0:T(8,128)(2,1)} %get-tuple-element.75.near_in, bf16[128,1536]{1,0:T(8,128)(2,1)} %get-tuple-element.76.y0_in, ...), custom_call_target="tpu_custom_call" | custom-call | flops 49999998976 | bytes 4194304 | tf_op jit(solution)/shard_map/pallas_call | solution.py:361
  159.0 7.0 %shard_map.83 = bf16[1536,768]{1,0:T(8,128)(2,1)} custom-call(bf16[2,4,192,512]{3,2,1,0:T(8,128)(2,1)} %bitcast.49, bf16[2,4,192,512]{3,2,1,0:T(8,128)(2,1)} %bitcast.51, bf16[2,4,192,512]{3,2,1,0:T(8,128)(2,1)} %bitcast.52, bf16[2,4,192,512]{3,2,1,0:T(8,128)(2,1)} %bitcast.53, bf16[2,512,384]{2,1,0:T(8,128)(2,1)} %get-tuple-element.84.att_ref.refs_0_.refs_4_, ...), custom_call_target="tpu_custom_call" | custom-call | flops 2415919104 | bytes 10485760 | tf_op jit(solution)/shard_map/pallas_call | solution.py:455
  166.2 6.9 %collective-permute-done.22.y3_in = bf16[128,1536]{1,0:T(8,128)(2,1)} collective-permute-done((bf16[128,1536]{1,0:T(8,128)(2,1)}, bf16[128,1536]{1,0:T(8,128)(2,1)}, u32[]{:S(2)}, u32[]{:S(2)}) %collective-permute-start.22) | collective-permute-done | bytes 393248 | tf_op jit(solution)/shard_map/ppermute | solution.py:65
  184.7 12.7 %reduce-scatter.5.cloned.1.call-done = bf16[384,768]{1,0:T(8,128)(2,1)} async-done(((bf16[1536,768]{1,0:T(8,128)(2,1)}), bf16[384,768]{1,0:T(8,128)(2,1)}) %reduce-scatter.5.cloned.1.call-update) | async-done | bytes 589840 | tf_op jit(solution)/shard_map/reduce_scatter | solution.py:471
  198.3 8.6 %collective-permute-done.23 = bf16[192,768]{1,0:T(8,128)(2,1)S(1)} collective-permute-done((bf16[192,768]{1,0:T(8,128)(2,1)S(1)}, bf16[192,768]{1,0:T(8,128)(2,1)S(1)}, u32[]{:S(2)}, u32[]{:S(2)}) %collective-permute-start.23) | collective-permute-done | bytes 294944 | tf_op jit(solution)/shard_map/ppermute | solution.py:61
  217.5 4.1 %collective-permute-start.32 = (bf16[192,768]{1,0:T(8,128)(2,1)S(1)}, bf16[192,768]{1,0:T(8,128)(2,1)S(1)}, u32[]{:S(2)}, u32[]{:S(2)}) collective-permute-start(bf16[192,768]{1,0:T(8,128)(2,1)S(1)} %constant_dynamic-slice_fusion), channel_id=1, source_target_pairs={{0,64},{8,72},{16,80},{24,88},{32,96},{40,104},{48,112},{56,120},{... | collective-permute-start | bytes 884744 | tf_op jit(solution)/shard_map/ppermute | solution.py:61
  221.6 4.7 %shard_map.85 = bf16[512,3072]{1,0:T(8,128)(2,1)} custom-call(s32[8]{0:T(128)} %stack.70.src_ref, bf16[320,1536]{1,0:T(8,128)(2,1)} %get-tuple-element.92.own_ref.x_own, bf16[320,1536]{1,0:T(8,128)(2,1)} %copy-done.11, bf16[192,1536]{1,0:T(8,128)(2,1)} %get-tuple-element.93.y0_ref.y_own, bf16[192,1536]{1,0:T(8,128)(2,1)} %copy-done.18, ...), custom_call_target="tpu_custom_call" | custom-call | flops 49999998976 | bytes 6291456 | tf_op jit(solution)/shard_map/pallas_call | solution.py:399
  226.3 17.6 %collective-permute-done.32 = bf16[192,768]{1,0:T(8,128)(2,1)S(1)} collective-permute-done((bf16[192,768]{1,0:T(8,128)(2,1)S(1)}, bf16[192,768]{1,0:T(8,128)(2,1)S(1)}, u32[]{:S(2)}, u32[]{:S(2)}) %collective-permute-start.32) | collective-permute-done | bytes 294944 | tf_op jit(solution)/shard_map/ppermute | solution.py:61
  247.7 4.3 %shard_map.87 = bf16[512,3072]{1,0:T(8,128)(2,1)} custom-call(s32[8]{0:T(128)} %stack.70.src_ref, bf16[256,1536]{1,0:T(8,128)(2,1)} %get-tuple-element.94.own_ref, bf16[256,1536]{1,0:T(8,128)(2,1)} %copy-done.13, bf16[128,1536]{1,0:T(8,128)(2,1)} %get-tuple-element.95.y0_ref, bf16[128,1536]{1,0:T(8,128)(2,1)} %copy-done.22, bf16[128,1536]{1,0:T(8,128)(2,1)} %copy-done.20, ...), custom_call_target="tpu_custom_call" | custom-call | flops 49999998976 | bytes 6291456 | tf_op jit(solution)/shard_map/pallas_call | solution.py:399
  (128 shorter events, 68.9 us)
Async XLA Ops:
  7.2 175.3 %reduce-scatter.3.cloned.1.call-start = ((), (), s32[]{:S(2)}) async-start(), calls=%async_computation.2 | async-start | bytes 2949120 | tf_op jit(solution)/shard_map/reduce_scatter | solution.py:471
  14.7 25.1 %collective-permute-start.2 = (bf16[3,512,256]{2,1,0:T(8,128)(2,1)}, bf16[3,512,256]{2,1,0:T(8,128)(2,1)}, u32[]{:S(2)}, u32[]{:S(2)}) collective-permute-start(bf16[3,512,256]{2,1,0:T(8,128)(2,1)} %shard_map.75.o_ref), channel_id=1, source_target_pairs={{0,8},{8,0},{16,24},{24,16},{32,40},{40,32},{48,56},{56,48},{64,72... | collective-permute-start | bytes 2359304 | tf_op jit(solution)/shard_map/ppermute | solution.py:61
  14.7 20.3 %collective-permute-start.1 = (bf16[3,512,256]{2,1,0:T(8,128)(2,1)}, bf16[3,512,256]{2,1,0:T(8,128)(2,1)}, u32[]{:S(2)}, u32[]{:S(2)}) collective-permute-start(bf16[3,512,256]{2,1,0:T(8,128)(2,1)} %shard_map.75.o_ref), channel_id=1, source_target_pairs={{0,16},{8,120},{16,32},{24,8},{32,48},{40,24},{48,64},{56,40},{64,... | collective-permute-start | bytes 2359304 | tf_op jit(solution)/shard_map/ppermute | solution.py:61
  16.7 22.4 %collective-permute-start = (bf16[3,512,256]{2,1,0:T(8,128)(2,1)}, bf16[3,512,256]{2,1,0:T(8,128)(2,1)}, u32[]{:S(2)}, u32[]{:S(2)}) collective-permute-start(bf16[3,512,256]{2,1,0:T(8,128)(2,1)} %shard_map.75.o_ref), channel_id=1, source_target_pairs={{0,112},{8,24},{16,0},{24,40},{32,16},{40,56},{48,32},{56,72},{64,... | collective-permute-start | bytes 2359304 | tf_op jit(solution)/shard_map/ppermute | solution.py:61
  61.7 23.6 %collective-permute-start.5 = (bf16[3,512,256]{2,1,0:T(8,128)(2,1)}, bf16[3,512,256]{2,1,0:T(8,128)(2,1)S(1)}, u32[]{:S(2)}, u32[]{:S(2)}) collective-permute-start(bf16[3,512,256]{2,1,0:T(8,128)(2,1)} %get-tuple-element.60), channel_id=1, source_target_pairs={{0,112},{8,24},{16,0},{24,40},{32,16},{40,56},{48,32},{56,72},{64,... | collective-permute-start | bytes 2359304 | tf_op jit(solution)/shard_map/ppermute | solution.py:61
  69.7 24.2 %collective-permute-start.6 = (bf16[3,512,256]{2,1,0:T(8,128)(2,1)}, bf16[3,512,256]{2,1,0:T(8,128)(2,1)S(1)}, u32[]{:S(2)}, u32[]{:S(2)}) collective-permute-start(bf16[3,512,256]{2,1,0:T(8,128)(2,1)} %fusion.1), channel_id=1, source_target_pairs={{0,120},{8,16},{16,8},{24,32},{32,24},{40,48},{48,40},{56,64},{64,... | collective-permute-start | bytes 2359304 | tf_op jit(solution)/shard_map/ppermute | solution.py:61
  80.2 23.0 %collective-permute-start.7 = (bf16[256,1536]{1,0:T(8,128)(2,1)}, bf16[256,1536]{1,0:T(8,128)(2,1)S(1)}, u32[]{:S(2)}, u32[]{:S(2)}) collective-permute-start(bf16[256,1536]{1,0:T(8,128)(2,1)} %get-tuple-element.63), channel_id=1, source_target_pairs={{0,1},{1,0},{2,3},{3,2},{4,5},{5,4},{6,7},{7,6},{8,9},{9,8},{10,11... | collective-permute-start | bytes 2359304 | tf_op jit(solution)/shard_map/ppermute | solution.py:65
  116.7 31.9 %collective-permute-start.13 = (bf16[320,1536]{1,0:T(8,128)(2,1)}, bf16[320,1536]{1,0:T(8,128)(2,1)}, u32[]{:S(2)}, u32[]{:S(2)}) collective-permute-start(bf16[320,1536]{1,0:T(8,128)(2,1)} %get-tuple-element.71._), channel_id=1, source_target_pairs={{0,1},{1,0},{2,3},{3,2},{4,5},{5,4},{6,7},{7,6},{8,9},{9,8},{10,11... | collective-permute-start | bytes 2949128 | tf_op jit(solution)/shard_map/ppermute | solution.py:65
  119.7 28.9 %collective-permute-start.15 = (bf16[192,1536]{1,0:T(8,128)(2,1)}, bf16[192,1536]{1,0:T(8,128)(2,1)}, u32[]{:S(2)}, u32[]{:S(2)}) collective-permute-start(bf16[192,1536]{1,0:T(8,128)(2,1)} %get-tuple-element.80), channel_id=1, source_target_pairs={{0,4},{1,5},{2,6},{3,7},{4,0},{5,1},{6,2},{7,3},{8,12},{9,13},{10,... | collective-permute-start | bytes 1769480 | tf_op jit(solution)/shard_map/ppermute | solution.py:65
  122.7 26.0 %collective-permute-start.16 = (bf16[192,1536]{1,0:T(8,128)(2,1)}, bf16[192,1536]{1,0:T(8,128)(2,1)}, u32[]{:S(2)}, u32[]{:S(2)}) collective-permute-start(bf16[192,1536]{1,0:T(8,128)(2,1)} %get-tuple-element.81), channel_id=1, source_target_pairs={{0,6},{1,7},{2,0},{3,1},{4,2},{5,3},{6,4},{7,5},{8,14},{9,15},{10,... | collective-permute-start | bytes 1769480 | tf_op jit(solution)/shard_map/ppermute | solution.py:65
  127.7 29.9 %collective-permute-start.18 = (bf16[2,512,384]{2,1,0:T(8,128)(2,1)S(1)}, bf16[2,512,384]{2,1,0:T(8,128)(2,1)S(1)}, u32[]{:S(2)}, u32[]{:S(2)}) collective-permute-start(bf16[2,512,384]{2,1,0:T(8,128)(2,1)S(1)} %copy-done.5), channel_id=1, source_target_pairs={{0,8},{8,0},{16,24},{24,16},{32,40},{40,32},{48,56},{56,48},{64,72... | collective-permute-start | bytes 2359304 | tf_op jit(solution)/shard_map/ppermute | solution.py:61
  135.3 62.0 %reduce-scatter.5.cloned.1.call-start = ((), (), s32[]{:S(2)}) async-start(), calls=%async_computation.3 | async-start | bytes 2949120 | tf_op jit(solution)/shard_map/reduce_scatter | solution.py:471
  136.7 20.9 %collective-permute-start.17 = (bf16[8,192,512]{2,1,0:T(8,128)(2,1)S(1)}, bf16[8,192,512]{2,1,0:T(8,128)(2,1)S(1)}, u32[]{:S(2)}, u32[]{:S(2)}) collective-permute-start(bf16[8,192,512]{2,1,0:T(8,128)(2,1)S(1)} %copy-done.10), channel_id=1, source_target_pairs={{0,8},{8,0},{16,24},{24,16},{32,40},{40,32},{48,56},{56,48},{64,72... | collective-permute-start | bytes 4718600 | tf_op jit(solution)/shard_map/ppermute | solution.py:61
  155.0 18.1 %collective-permute-start.22 = (bf16[128,1536]{1,0:T(8,128)(2,1)}, bf16[128,1536]{1,0:T(8,128)(2,1)}, u32[]{:S(2)}, u32[]{:S(2)}) collective-permute-start(bf16[128,1536]{1,0:T(8,128)(2,1)} %get-tuple-element.90), channel_id=1, source_target_pairs={{0,6},{1,7},{2,0},{3,1},{4,2},{5,3},{6,4},{7,5},{8,14},{9,15},{10,... | collective-permute-start | bytes 1179656 | tf_op jit(solution)/shard_map/ppermute | solution.py:65
  176.9 32.4 %collective-permute-start.24 = (bf16[320,1536]{1,0:T(8,128)(2,1)}, bf16[320,1536]{1,0:T(8,128)(2,1)S(1)}, u32[]{:S(2)}, u32[]{:S(2)}) collective-permute-start(bf16[320,1536]{1,0:T(8,128)(2,1)} %get-tuple-element.92.own_ref.x_own), channel_id=1, source_target_pairs={{0,1},{1,0},{2,3},{3,2},{4,5},{5,4},{6,7},{7,6},{8,9},{9,8},{10,11... | collective-permute-start | bytes 2949128 | tf_op jit(solution)/shard_map/ppermute | solution.py:65
  177.9 30.1 %collective-permute-start.27 = (bf16[192,1536]{1,0:T(8,128)(2,1)}, bf16[192,1536]{1,0:T(8,128)(2,1)S(1)}, u32[]{:S(2)}, u32[]{:S(2)}) collective-permute-start(bf16[192,1536]{1,0:T(8,128)(2,1)} %get-tuple-element.93.y0_ref.y_own), channel_id=1, source_target_pairs={{0,6},{1,7},{2,0},{3,1},{4,2},{5,3},{6,4},{7,5},{8,14},{9,15},{10,... | collective-permute-start | bytes 1769480 | tf_op jit(solution)/shard_map/ppermute | solution.py:65
  180.5 27.5 %collective-permute-start.26 = (bf16[192,1536]{1,0:T(8,128)(2,1)}, bf16[192,1536]{1,0:T(8,128)(2,1)S(1)}, u32[]{:S(2)}, u32[]{:S(2)}) collective-permute-start(bf16[192,1536]{1,0:T(8,128)(2,1)} %get-tuple-element.93.y0_ref.y_own), channel_id=1, source_target_pairs={{0,4},{1,5},{2,6},{3,7},{4,0},{5,1},{6,2},{7,3},{8,12},{9,13},{10,... | collective-permute-start | bytes 1769480 | tf_op jit(solution)/shard_map/ppermute | solution.py:65
  181.6 27.6 %collective-permute-start.25 = (bf16[192,1536]{1,0:T(8,128)(2,1)}, bf16[192,1536]{1,0:T(8,128)(2,1)S(1)}, u32[]{:S(2)}, u32[]{:S(2)}) collective-permute-start(bf16[192,1536]{1,0:T(8,128)(2,1)} %get-tuple-element.93.y0_ref.y_own), channel_id=1, source_target_pairs={{0,2},{1,3},{2,4},{3,5},{4,6},{5,7},{6,0},{7,1},{8,10},{9,11},{10,... | collective-permute-start | bytes 1769480 | tf_op jit(solution)/shard_map/ppermute | solution.py:65
  183.4 23.5 %collective-permute-start.23 = (bf16[192,768]{1,0:T(8,128)(2,1)S(1)}, bf16[192,768]{1,0:T(8,128)(2,1)S(1)}, u32[]{:S(2)}, u32[]{:S(2)}) collective-permute-start(bf16[192,768]{1,0:T(8,128)(2,1)S(1)} %constant_dynamic-slice_fusion.1), channel_id=1, source_target_pairs={{0,64},{8,72},{16,80},{24,88},{32,96},{40,104},{48,112},{56,120},{... | collective-permute-start | bytes 884744 | tf_op jit(solution)/shard_map/ppermute | solution.py:61
  214.1 31.7 %collective-permute-start.31 = (bf16[128,1536]{1,0:T(8,128)(2,1)}, bf16[128,1536]{1,0:T(8,128)(2,1)S(1)}, u32[]{:S(2)}, u32[]{:S(2)}) collective-permute-start(bf16[128,1536]{1,0:T(8,128)(2,1)} %get-tuple-element.95.y0_ref), channel_id=1, source_target_pairs={{0,6},{1,7},{2,0},{3,1},{4,2},{5,3},{6,4},{7,5},{8,14},{9,15},{10,... | collective-permute-start | bytes 1179656 | tf_op jit(solution)/shard_map/ppermute | solution.py:65
  216.5 29.2 %collective-permute-start.30 = (bf16[128,1536]{1,0:T(8,128)(2,1)}, bf16[128,1536]{1,0:T(8,128)(2,1)S(1)}, u32[]{:S(2)}, u32[]{:S(2)}) collective-permute-start(bf16[128,1536]{1,0:T(8,128)(2,1)} %get-tuple-element.95.y0_ref), channel_id=1, source_target_pairs={{0,4},{1,5},{2,6},{3,7},{4,0},{5,1},{6,2},{7,3},{8,12},{9,13},{10,... | collective-permute-start | bytes 1179656 | tf_op jit(solution)/shard_map/ppermute | solution.py:65
  217.3 28.5 %collective-permute-start.29 = (bf16[128,1536]{1,0:T(8,128)(2,1)}, bf16[128,1536]{1,0:T(8,128)(2,1)S(1)}, u32[]{:S(2)}, u32[]{:S(2)}) collective-permute-start(bf16[128,1536]{1,0:T(8,128)(2,1)} %get-tuple-element.95.y0_ref), channel_id=1, source_target_pairs={{0,2},{1,3},{2,4},{3,5},{4,6},{5,7},{6,0},{7,1},{8,10},{9,11},{10,... | collective-permute-start | bytes 1179656 | tf_op jit(solution)/shard_map/ppermute | solution.py:65
  217.5 28.3 %collective-permute-start.28 = (bf16[256,1536]{1,0:T(8,128)(2,1)}, bf16[256,1536]{1,0:T(8,128)(2,1)S(1)}, u32[]{:S(2)}, u32[]{:S(2)}) collective-permute-start(bf16[256,1536]{1,0:T(8,128)(2,1)} %get-tuple-element.94.own_ref), channel_id=1, source_target_pairs={{0,1},{1,0},{2,3},{3,2},{4,5},{5,4},{6,7},{7,6},{8,9},{9,8},{10,11... | collective-permute-start | bytes 2359304 | tf_op jit(solution)/shard_map/ppermute | solution.py:65
  217.5 26.4 %collective-permute-start.32 = (bf16[192,768]{1,0:T(8,128)(2,1)S(1)}, bf16[192,768]{1,0:T(8,128)(2,1)S(1)}, u32[]{:S(2)}, u32[]{:S(2)}) collective-permute-start(bf16[192,768]{1,0:T(8,128)(2,1)S(1)} %constant_dynamic-slice_fusion), channel_id=1, source_target_pairs={{0,64},{8,72},{16,80},{24,88},{32,96},{40,104},{48,112},{56,120},{... | collective-permute-start | bytes 884744 | tf_op jit(solution)/shard_map/ppermute | solution.py:61
  (38 other events, 271.7 us)
Sparse Core Ops, SparseCore 0:
  135.4 27.2 reduce-scatter.2
  166.2 31.1 reduce-scatter.4

commit v3 on v2

--- a/solution.py
+++ b/solution.py
@@ -19,7 +19,6 @@
 EXP2_SCALE = SCALE * math.log2(math.e)
 BF = jnp.bfloat16
 F32 = jnp.float32
-VMEM_LIMIT = 56 << 20
 
 
 def sds(shape, dtype):
@@ -30,8 +29,8 @@
     return lax.dot_general(a, b, (dims, ((), ())), preferred_element_type=F32)
 
 
-def params():
-    return pltpu.CompilerParams(vmem_limit_bytes=VMEM_LIMIT)
+def params(mib=56):
+    return pltpu.CompilerParams(vmem_limit_bytes=mib << 20)
 
 
 def cost(flops, moved, exps=0):
@@ -76,12 +75,7 @@
         acc[:, :LW] = k
         acc[:, LW:] = v
 
-    @pl.when((step > 0) & (step < 3))
-    def _():
-        acc[:, :LW] += k
-        acc[:, LW:] += v
-
-    @pl.when(step == 3)
+    @pl.when(step == 1)
     def _():
         for h in range(LH):
             cols = slice(h * E, (h + 1) * E)
@@ -90,10 +84,10 @@
 
 
 def project_kv(x, w3):
-    depth = D // 4
+    depth = D // 2
     return pl.pallas_call(
         kv_kernel,
-        grid=(4,),
+        grid=(2,),
         in_specs=[
             pl.BlockSpec((TOK, depth), lambda i: (0, i)),
             pl.BlockSpec((None, depth, LW), lambda i: (1, i, 0)),
@@ -213,12 +207,12 @@
 
     out = dot(a_scr[...], w_ref[...], ((1,), (1,))).astype(BF)
 
-    @pl.when(tile < 2)
+    @pl.when(tile == 0)
     def _():
         near_ref[...] = out[:256]
         far_ref[...] = out[256:]
 
-    @pl.when(tile >= 2)
+    @pl.when(tile > 0)
     def _():
         for dy, ref in enumerate((y0_ref, y1_ref, y2_ref, y3_ref)):
             ref[:64], ref[64:] = y_rows(out, dy)
@@ -234,18 +228,20 @@
                 pl.BlockSpec((None, TOK, LW), lambda t, s: (0, 0, 0)),
                 pl.BlockSpec((COLS, LW), lambda t, s: (t, 0)),
             ],
-            out_specs=[left_tile(256)] * 2 + [right_tile(128)] * 4,
+            out_specs=[pl.BlockSpec((256, COLS), lambda t, s: (0, 0))] * 2
+            + [pl.BlockSpec((128, COLS), lambda t, s: (0, jnp.maximum(t - 1, 0)))] * 4,
             scratch_shapes=[pltpu.VMEM((TOK, LW), BF)],
         ),
-        out_shape=[sds((256, HALF), BF)] * 2 + [sds((128, HALF), BF)] * 4,
-        compiler_params=params(),
+        out_shape=[sds((256, COLS), BF)] * 2 + [sds((128, 3 * COLS), BF)] * 4,
+        compiler_params=params(24),
         cost_estimate=cost(2 * TOK * D * LW, (LW * D + TOK * D) * 2),
     )(dest, att_dq, w_out)
 
 
 def input_kernel(dest_ref, *refs):
-    dq_ref, d_kv_ref, w_ref, near_in, far_in, y0_in, y1_in, y2_in, y3_in = refs[:9]
-    near_ref, y0_ref, left_ref, right_ref, x_ref, y1_ref, y2_ref, y3_ref, a_scr = refs[9:]
+    dq_ref, d_kv_ref, w_ref, near_in, far_in = refs[:5]
+    y_in, y_last = refs[5:9], refs[9:13]
+    near_ref, y0_ref, left_ref, right_ref, x_ref, y1_ref, y2_ref, y3_ref, a_scr = refs[13:]
     tile = pl.program_id(0)
 
     @pl.when(tile == 0)
@@ -262,24 +258,38 @@
         out = term if out is None else out + term
     out = out.astype(BF)
 
+    def total_of(parts, rows):
+        total = parts[0][rows, :].astype(F32)
+        for ref in parts[1:]:
+            total = total + ref[rows, :].astype(F32)
+        return total
+
     @pl.when(tile < 2)
     def _():
         near_ref[...] = out[:256]
         x_ref[:256] = out[256:]
-        total = y0_in[...].astype(F32)
-        for ref in (y1_in, y2_in, y3_in):
-            total = total + ref[...].astype(F32)
+        total = total_of(y_in, slice(0, 128))
         right_ref[...] = total[:64]
-        x_ref[256:] = total[64:].astype(BF)
-
-    @pl.when(tile >= 2)
-    def _():
-        total = near_in[...].astype(F32) + far_in[...].astype(F32)
-        left_ref[...] = total[:64]
-        y0_ref[:64], y0_ref[64:] = y_rows(out, 0)
-        for dy, ref in ((1, y1_ref), (2, y2_ref), (3, y3_ref)):
-            ref[:64], ref[64:128] = y_rows(out, dy)
-            ref[128:] = total[dy * 64 : (dy + 1) * 64].astype(BF)
+        x_ref[256:320] = total[64:].astype(BF)
+
+    for t in range(2):
+        @pl.when(tile == t)
+        def _():
+            x_ref[320:] = total_of(y_last, slice(64 + 32 * t, 96 + 32 * t)).astype(BF)
+
+    @pl.when(tile == 2)
+    def _():
+        right_ref[...] = total_of(y_last, slice(0, 64))
+
+    for t in range(2):
+        @pl.when(tile == 2 + t)
+        def _():
+            total = near_in[...].astype(F32) + far_in[...].astype(F32)
+            left_ref[...] = total[:64]
+            y0_ref[:64], y0_ref[64:] = y_rows(out, 0)
+            for dy, ref in ((1, y1_ref), (2, y2_ref), (3, y3_ref)):
+                ref[:64], ref[64:128] = y_rows(out, dy)
+                ref[128:] = total[dy * 64 + 32 * t : dy * 64 + 32 * t + 32].astype(BF)
 
 
 def input_product(dest, att_dq, d_kv, w3, mixed):
@@ -293,38 +303,54 @@
                 pl.BlockSpec((LH, TOK, 2 * E), lambda t, s: (0, 0, 0)),
                 pl.BlockSpec((3, COLS, LW), lambda t, s: (0, t, 0)),
             ]
-            + [right_tile(256)] * 2
-            + [left_tile(128)] * 4,
-            out_specs=[left_tile(256), right_tile(128), right_tile(64), left_tile(64), left_tile(320)]
-            + [right_tile(192)] * 3,
+            + [pl.BlockSpec((256, COLS), lambda t, s: (0, 0))] * 2
+            + [left_tile(128)] * 4
+            + [pl.BlockSpec((128, COLS), lambda t, s: (0, 2))] * 4,
+            out_specs=[
+                left_tile(256),
+                right_tile(128),
+                pl.BlockSpec((64, COLS), lambda t, s: (0, 0)),
+                pl.BlockSpec((64, COLS), lambda t, s: (0, jnp.minimum(t, 2))),
+                left_tile(352),
+            ]
+            + [right_tile(160)] * 3,
             scratch_shapes=[pltpu.VMEM((TOK, 3 * LW), BF)],
         ),
         out_shape=[
             sds((256, HALF), BF),
             sds((128, HALF), BF),
-            sds((64, HALF), F32),
-            sds((64, HALF), F32),
-            sds((320, HALF), BF),
+            sds((64, COLS), F32),
+            sds((64, 3 * COLS), F32),
+            sds((352, HALF), BF),
         ]
-        + [sds((192, HALF), BF)] * 3,
-        compiler_params=params(),
+        + [sds((160, HALF), BF)] * 3,
+        compiler_params=params(28),
         cost_estimate=cost(2 * TOK * D * 3 * LW, (3 * LW * D + 2 * TOK * D) * 2),
-    )(dest, att_dq, d_kv, w3, *mixed)
+    )(dest, att_dq, d_kv, w3, *mixed, *mixed[2:])
 
 
 def third_kernel(near_in, y0_in, left_in, right_in, x_in, y1_in, y2_in, y3_in, *refs):
     left_ref, right_ref, x_ref, y1_ref, y2_ref, y3_ref = refs
     y_in = (y1_in, y2_in, y3_in)
-    mixed_left = left_in[...]
-    for ref in y_in:
-        mixed_left = mixed_left + ref[128:].astype(F32)
-    mixed_left = mixed_left.astype(BF)
-    x_ref[64:] = (right_in[...] + x_in[256:].astype(F32)).astype(BF)
+    outs = ((1, y1_ref), (2, y2_ref), (3, y3_ref))
+    for t in range(2):
+        rows, cols = slice(32 * t, 32 * t + 32), slice(COLS * t, COLS * (t + 1))
+        mixed_left = left_in[rows, :]
+        for ref in y_in:
+            mixed_left = mixed_left + ref[128:, cols].astype(F32)
+        mixed_left = mixed_left.astype(BF)
+        last = (right_in[rows, 2 * COLS :] + x_in[320:, cols].astype(F32)).astype(BF)
+        x_ref[64 + 32 * t : 96 + 32 * t, COLS:] = last
+        for _, ref in outs:
+            ref[64 + 32 * t : 96 + 32 * t, :COLS] = mixed_left
+    x_ref[64:, :COLS] = (right_in[:, COLS : 2 * COLS] + x_in[256:320, COLS:].astype(F32)).astype(BF)
+    middle = (right_in[:, :COLS] + x_in[256:320, :COLS].astype(F32)).astype(BF)
+    for _, ref in outs:
+        ref[64:, COLS:] = middle
     total = near_in[...].astype(F32) + x_in[:256].astype(F32)
     left_ref[...] = total[:64]
-    for dy, ref in ((1, y1_ref), (2, y2_ref), (3, y3_ref)):
+    for dy, ref in outs:
         ref[:64] = total[dy * 64 : (dy + 1) * 64].astype(BF)
-        ref[64:] = mixed_left
     total = y0_in[...].astype(F32)
     for ref in y_in:
         total = total + ref[:128].astype(F32)
@@ -354,17 +380,17 @@
     y_ref[64:] = x_in[:64]
 
 
-def by_columns(kernel, inputs, outputs):
-    def tile(rows):
-        return pl.BlockSpec((rows, COLS), lambda t: (0, t))
+def by_columns(kernel, tiles, mib, inputs, outputs):
+    def tile(shape):
+        return pl.BlockSpec((shape[0], shape[1] // tiles), lambda t: (0, t))
 
     return pl.pallas_call(
         kernel,
-        grid=(2,),
-        in_specs=[tile(a.shape[0]) for a in inputs],
-        out_specs=[tile(rows) for rows, _ in outputs],
+        grid=(tiles,),
+        in_specs=[tile(a.shape) for a in inputs],
+        out_specs=[tile((rows, HALF)) for rows, _ in outputs],
         out_shape=[sds((rows, HALF), dtype) for rows, dtype in outputs],
-        compiler_params=params(),
+        compiler_params=params(mib),
         cost_estimate=cost(5e10, 4 << 20),
     )(*inputs)
 
@@ -405,7 +431,7 @@
             out_specs=pl.BlockSpec((TOK, HALF), lambda t, s: (0, 1 - t)),
         ),
         out_shape=sds((TOK, D), BF),
-        compiler_params=params(),
+        compiler_params=params(24),
         cost_estimate=cost(5e10, 4 * TOK * D),
     )(source, own, beside, *ys)
 
@@ -545,17 +571,19 @@
     near2, _, _ = lax.optimization_barrier((near2, late, g_mine))
     left3, right3, x3, *y3 = by_columns(
         third_kernel,
+        1,
+        56,
         (near2, y02, left2, right2, from_x2, *from_y2),
         [(64, F32), (64, F32), (128, BF), (128, BF), (128, BF), (128, BF)],
     )
     from_x3, from_y3 = exchange(x3, y3)
     left3, _ = lax.optimization_barrier((left3, early))
     x4, y4 = by_columns(
-        fourth_kernel, (left3, right3, x3, from_x3, y3[0], *from_y3), [(320, BF), (192, BF)]
+        fourth_kernel, 2, 16, (left3, right3, x3, from_x3, y3[0], *from_y3), [(320, BF), (192, BF)]
     )
     from_x4, from_y4 = exchange(x4, [y4] * 3)
     x4, late_sum = lax.optimization_barrier((x4, late_sum))
-    x5, y5 = by_columns(fifth_kernel, (x4, from_x4, y4, *from_y4), [(256, BF), (128, BF)])
+    x5, y5 = by_columns(fifth_kernel, 2, 16, (x4, from_x4, y4, *from_y4), [(256, BF), (128, BF)])
     early_other, _ = lax.optimization_barrier((early_other, x5))
     early_sum = with_x_hi(early_own, early_other)
     from_x5, from_y5 = exchange(x5, [y5] * 3)

time: 260 us -> 252 us (0.969)
  Pallas kernels: 84.2 us -> 70.6 us
  local copies, waits for them, and re-layouts: 14 us -> 19.4 us
    ppermute x13, waiting for transfers between devices: 41.1 us -> 33.8 us  [over_view(): return lax.ppermute(block, 'view', route)]
    unnamed x54 -> x58, local copies, waits for them, and re-layouts: 10 us -> 16.5 us
    reduce_scatter x2, waiting for transfers between devices: 12.7 us -> 18.1 us  [weight_sum(): lax.psum_scatter(terms, 'view', scatter_dimension=0, axis_index_groups=Z_...]
    pallas_call x4, Pallas kernels: 17.2 us -> 13 us  [the longest x1 7.01 us: project_kv(): pl.pallas_call(kv_kernel, grid=(2,), in_specs=[pl.BlockSpec((TOK, depth),...]
    pallas_call x1, Pallas kernels: 12 us -> 8.64 us  [input_product(): pl.pallas_call(input_kernel, grid_spec=pltpu.PrefetchScalarGridSpec(num_s...]
    pallas_call x1, Pallas kernels: 6.64 us -> 3.57 us  [mixed_product(): pl.pallas_call(mixed_kernel, grid_spec=pltpu.PrefetchScalarGridSpec(num_s...]
    pallas_call x2, Pallas kernels: 8.94 us -> 5.93 us  [place(): pl.pallas_call(functools.partial(place_kernel, first), grid_spec=pltpu.Pr...]
  transfers between devices with their start and end apart: 35 -> 35, of which waited for: 13 -> 14; matrix products, arithmetic and copies ran while one was open for 7% -> 7% of each run, Pallas kernels for 15% -> 13%
where the time goes in v3:
time: 252 us; the launch traced here: 251 us
  waiting for transfers between devices  81.1 us (32%)
  Pallas kernels  70.6 us (28%)
  starting transfers between devices  50.1 us (20%)
  local copies, waits for them, and re-layouts  19.4 us (8%)
  between operations  14.3 us (6%)
  matrix products  8.63 us (3%)
  other arithmetic  6.96 us (3%)
    ppermute x13, waiting for transfers between devices, over_view(): return lax.ppermute(block, 'view', route)  33.8 us
    ppermute x20, waiting for transfers between devices, over_head(): return lax.ppermute(block, 'head', head_route(*step))  29.1 us
    ppermute x20, starting transfers between devices, over_head(): return lax.ppermute(block, 'head', head_route(*step))  28.4 us
    ppermute x13, starting transfers between devices, over_view(): return lax.ppermute(block, 'view', route)  21.6 us
    pallas_call x1, Pallas kernels, attention(): pl.pallas_call(attention_kernel, grid=(LH,), in_specs=[head_block, head_b...  18.5 us
    reduce_scatter x2, waiting for transfers between devices, weight_sum(): lax.psum_scatter(terms, 'view', scatter_dimension=0, axis_index_groups=Z_...  18.1 us
    unnamed x58, local copies, waits for them, and re-layouts  16.5 us
    pallas_call x2, Pallas kernels, weight_terms(): pl.pallas_call(functools.partial(weight_kernel, plan, len(lhs_pairs), len...  13.5 us
  transfers between devices with their start and end apart: 35, of which 14 were waited for; matrix products, arithmetic and copies ran while one was open for 7% of the time, Pallas kernels for 13%

profile of v3, /device:TPU:0, one launch (start us, length us, event | category | flops | bytes accessed | tf_op | source)
XLA Modules:
  0.0 251.0 jit_solution(12653698713491245274)
XLA Ops:
  7.2 7.0 %shard_map.75.o_ref = bf16[3,512,256]{2,1,0:T(8,128)(2,1)} custom-call(bf16[512,3072]{1,0:T(8,128)(2,1)} %x_ref.4, bf16[3,3072,384]{2,1,0:T(8,128)(2,1)} %bitcast.44, bf16[3,3072,384]{2,1,0:T(8,128)(2,1)} %bitcast.45), custom_call_target="tpu_custom_call" | custom-call | flops 2415919104 | bytes 9437184 | tf_op jit(solution)/shard_map/pallas_call | solution.py:88
  16.2 4.7 %collective-permute-start = (bf16[3,512,256]{2,1,0:T(8,128)(2,1)}, bf16[3,512,256]{2,1,0:T(8,128)(2,1)}, u32[]{:S(2)}, u32[]{:S(2)}) collective-permute-start(bf16[3,512,256]{2,1,0:T(8,128)(2,1)} %shard_map.75.o_ref), channel_id=1, source_target_pairs={{0,112},{8,24},{16,0},{24,40},{32,16},{40,56},{48,32},{56,72},{64,... | collective-permute-start | bytes 2359304 | tf_op jit(solution)/shard_map/ppermute | solution.py:60
  20.9 4.4 %convolution_convert_fusion._.g_ref = bf16[512,384]{1,0:T(8,128)(2,1)} fusion(bf16[512,3072]{1,0:T(8,128)(2,1)} %x_ref.5, bf16[3072,384]{1,0:T(8,128)(2,1)S(1)} %copy-done.4), kind=kOutput, calls=%fused_computation.9 | convolution fusion | flops 1208156160 | bytes 5898240 | tf_op jit(solution)/shard_map/dot_general | solution.py:522
  25.3 3.8 %shard_map.76 = (bf16[8,192,512]{2,1,0:T(8,128)(2,1)}, bf16[8,192,512]{2,1,0:T(8,128)(2,1)}) custom-call(s32[1]{0:T(128)} %bitcast.16.core_ref, bf16[512,3072]{1,0:T(8,128)(2,1)} %x_ref.4, bf16[512,384]{1,0:T(8,128)(2,1)} %convolution_convert_fusion._.g_ref), custom_call_target="tpu_custom_call" | custom-call | flops 100663296 | bytes 6291456 | tf_op jit(solution)/shard_map/pallas_call | solution.py:450
  29.1 4.2 %fusion.5.q_ref = bf16[512,384]{1,0:T(8,128)(2,1)} fusion(bf16[512,3072]{1,0:T(8,128)(2,1)S(1)} %copy-done.18, bf16[3,3072,384]{2,1,0:T(8,128)(2,1)} %bitcast.46), kind=kOutput, calls=%fused_computation.8 | convolution fusion | flops 1208156160 | bytes 5898240 | tf_op jit(solution)/shard_map/dot_general | solution.py:521
  34.5 4.1 %collective-permute-done.b_ref = bf16[3,512,256]{2,1,0:T(8,128)(2,1)} collective-permute-done((bf16[3,512,256]{2,1,0:T(8,128)(2,1)}, bf16[3,512,256]{2,1,0:T(8,128)(2,1)}, u32[]{:S(2)}, u32[]{:S(2)}) %collective-permute-start) | collective-permute-done | bytes 786464 | tf_op jit(solution)/shard_map/ppermute | solution.py:60
  42.4 18.5 %shard_map.77 = (bf16[2,512,384]{2,1,0:T(8,128)(2,1)}, f32[3,512,256]{2,1,0:T(8,128)}, bf16[3,512,256]{2,1,0:T(8,128)(2,1)}, bf16[2,3,512,256]{3,2,1,0:T(8,128)(2,1)}, f32[3,512,256]{2,1,0:T(8,128)}) custom-call(bf16[512,384]{1,0:T(8,128)(2,1)} %fusion.5.q_ref, bf16[512,384]{1,0:T(8,128)(2,1)} %convolution_convert_fusion._.g_ref, ...), custom_call_target="tpu_custom_call" | custom-call | flops 12079595520 | bytes 12582912 | tf_op jit(solution)/shard_map/pallas_call | solution.py:155
  61.3 5.5 %collective-permute-start.5 = (bf16[3,512,256]{2,1,0:T(8,128)(2,1)}, bf16[3,512,256]{2,1,0:T(8,128)(2,1)}, u32[]{:S(2)}, u32[]{:S(2)}) collective-permute-start(bf16[3,512,256]{2,1,0:T(8,128)(2,1)} %get-tuple-element.60), channel_id=1, source_target_pairs={{0,112},{8,24},{16,0},{24,40},{32,16},{40,56},{48,32},{56,72},{64,... | collective-permute-start | bytes 2359304 | tf_op jit(solution)/shard_map/ppermute | solution.py:60
  66.8 3.1 %fusion.1 = bf16[3,512,256]{2,1,0:T(8,128)(2,1)} fusion(f32[3,512,256]{2,1,0:T(8,128)} %get-tuple-element.61, bf16[2,3,512,256]{3,2,1,0:T(8,128)(2,1)S(1)} %collective-permute-done.4), kind=kLoop, calls=%fused_computation.3 | loop fusion | flops 1179648 | bytes 3145728 | tf_op jit(solution)/shard_map/convert_element_type | solution.py:535
  69.9 3.2 %collective-permute-start.6 = (bf16[3,512,256]{2,1,0:T(8,128)(2,1)}, bf16[3,512,256]{2,1,0:T(8,128)(2,1)}, u32[]{:S(2)}, u32[]{:S(2)}) collective-permute-start(bf16[3,512,256]{2,1,0:T(8,128)(2,1)} %fusion.1), channel_id=1, source_target_pairs={{0,120},{8,16},{16,8},{24,32},{32,24},{40,48},{48,40},{56,64},{64,... | collective-permute-start | bytes 2359304 | tf_op jit(solution)/shard_map/ppermute | solution.py:60
  74.9 3.6 %shard_map.78 = (bf16[256,768]{1,0:T(8,128)(2,1)S(1)}, bf16[256,768]{1,0:T(8,128)(2,1)S(1)}, bf16[128,2304]{1,0:T(8,128)(2,1)S(1)}, bf16[128,2304]{1,0:T(8,128)(...) custom-call(s32[8]{0:T(128)S(1)} %stack.77.dest_ref, bf16[2,512,384]{2,1,0:T(8,128)(2,1)S(1)} %copy-done.1, ...), custom_call_target="tpu_custom_call" | custom-call | flops 1207959552 | bytes 5505024 | tf_op jit(solution)/shard_map/pallas_call | solution.py:222
  84.9 4.3 %collective-permute-done.6 = bf16[3,512,256]{2,1,0:T(8,128)(2,1)} collective-permute-done((bf16[3,512,256]{2,1,0:T(8,128)(2,1)}, bf16[3,512,256]{2,1,0:T(8,128)(2,1)}, u32[]{:S(2)}, u32[]{:S(2)}) %collective-permute-start.6) | collective-permute-done | bytes 786464 | tf_op jit(solution)/shard_map/ppermute | solution.py:60
  91.0 3.4 %collective-permute-done.7.refs_4_ = bf16[256,768]{1,0:T(8,128)(2,1)S(1)} collective-permute-done((bf16[256,768]{1,0:T(8,128)(2,1)S(1)}, bf16[256,768]{1,0:T(8,128)(2,1)S(1)}, u32[]{:S(2)}, u32[]{:S(2)}) %collective-permute-start.7) | collective-permute-done | bytes 393248 | tf_op jit(solution)/shard_map/ppermute | solution.py:64
  94.9 8.9 %collective-permute-done.9.refs_7_.refs_11_ = bf16[128,2304]{1,0:T(8,128)(2,1)S(1)} collective-permute-done((bf16[128,2304]{1,0:T(8,128)(2,1)S(1)}, bf16[128,2304]{1,0:T(8,128)(2,1)S(1)}, u32[]{:S(2)}, u32[]{:S(2)}) %collective-permute-start.9) | collective-permute-done | bytes 589856 | tf_op jit(solution)/shard_map/ppermute | solution.py:64
  106.8 8.6 %shard_map.79 = (bf16[256,1536]{1,0:T(8,128)(2,1)S(1)}, bf16[128,1536]{1,0:T(8,128)(2,1)S(1)}, f32[64,768]{1,0:T(8,128)S(1)}, f32[64,2304]{1,0:T(8,128)S(1)}, bf...) custom-call(s32[8]{0:T(128)S(1)} %stack.77.dest_ref, ...), custom_call_target="tpu_custom_call" | custom-call | flops 3623878656 | bytes 13369344 | tf_op jit(solution)/shard_map/pallas_call | solution.py:296
  125.3 3.6 %shard_map.81 = (bf16[8,192,512]{2,1,0:T(8,128)(2,1)}, bf16[8,192,512]{2,1,0:T(8,128)(2,1)}) custom-call(s32[1]{0:T(128)} %bitcast.16.core_ref, bf16[512,3072]{1,0:T(8,128)(2,1)} %x_ref.5, bf16[352,1536]{1,0:T(8,128)(2,1)} %copy-done.3), custom_call_target="tpu_custom_call" | custom-call | flops 100663296 | bytes 6291456 | tf_op jit(solution)/shard_map/pallas_call | solution.py:450
  130.1 6.5 %shard_map.80 = bf16[1536,768]{1,0:T(8,128)(2,1)} custom-call(bf16[2,4,192,512]{3,2,1,0:T(8,128)(2,1)} %bitcast.48, bf16[2,4,192,512]{3,2,1,0:T(8,128)(2,1)} %bitcast.50, bf16[3,512,256]{2,1,0:T(8,128)(2,1)} %copy-done.2, bf16[3,512,256]{2,1,0:T(8,128)(2,1)} %copy-done.27), custom_call_target="tpu_custom_call" | custom-call | flops 2415919104 | bytes 10485760 | tf_op jit(solution)/shard_map/pallas_call | solution.py:481
  136.8 8.2 %collective-permute-done.15.y2_in = bf16[160,1536]{1,0:T(8,128)(2,1)} collective-permute-done((bf16[160,1536]{1,0:T(8,128)(2,1)S(1)}, bf16[160,1536]{1,0:T(8,128)(2,1)}, u32[]{:S(2)}, u32[]{:S(2)}) %collective-permute-start.15) | collective-permute-done | bytes 491552 | tf_op jit(solution)/shard_map/ppermute | solution.py:64
  145.2 4.0 %shard_map.82 = (f32[64,1536]{1,0:T(8,128)}, f32[64,1536]{1,0:T(8,128)}, bf16[128,1536]{1,0:T(8,128)(2,1)}, bf16[128,1536]{1,0:T(8,128)(2,1)}, bf16[128,1536]{1,0:T(8,128)(2,1)}, /*index=5*/bf16[128,1536]{1,0:T(8,128)(2,1)}) custom-call(bf16[256,1536]{1,0:T(8,128)(2,1)} %copy-done.6, bf16[128,1536]{1,0:T(8,128)(2,1)} %copy-done.8, f32[64,768]{1,0:T(8,128)} %copy-done.15, ...), custom_call_target="tpu_custom_call" | custom-call | flops 49999998976 | bytes 4194304 | tf_op jit(solution)/shard_map/pallas_call | solution.py:387
  156.5 7.0 %shard_map.83 = bf16[1536,768]{1,0:T(8,128)(2,1)} custom-call(bf16[2,4,192,512]{3,2,1,0:T(8,128)(2,1)} %bitcast.49, bf16[2,4,192,512]{3,2,1,0:T(8,128)(2,1)} %bitcast.51, bf16[2,4,192,512]{3,2,1,0:T(8,128)(2,1)} %bitcast.52, bf16[2,4,192,512]{3,2,1,0:T(8,128)(2,1)} %bitcast.53, bf16[2,512,384]{2,1,0:T(8,128)(2,1)} %get-tuple-element.84.att_ref.refs_0_.refs_4_, ...), custom_call_target="tpu_custom_call" | custom-call | flops 2415919104 | bytes 10485760 | tf_op jit(solution)/shard_map/pallas_call | solution.py:481
  163.6 6.9 %collective-permute-done.22.y3_in = bf16[128,1536]{1,0:T(8,128)(2,1)S(1)} collective-permute-done((bf16[128,1536]{1,0:T(8,128)(2,1)}, bf16[128,1536]{1,0:T(8,128)(2,1)S(1)}, u32[]{:S(2)}, u32[]{:S(2)}) %collective-permute-start.22) | collective-permute-done | bytes 393248 | tf_op jit(solution)/shard_map/ppermute | solution.py:64
  185.4 18.1 %reduce-scatter.5.cloned.1.call-done = bf16[384,768]{1,0:T(8,128)(2,1)} async-done(((bf16[1536,768]{1,0:T(8,128)(2,1)}), bf16[384,768]{1,0:T(8,128)(2,1)}) %reduce-scatter.5.cloned.1.call-update) | async-done | bytes 589840 | tf_op jit(solution)/shard_map/reduce_scatter | solution.py:497
  217.4 3.6 %shard_map.85 = bf16[512,3072]{1,0:T(8,128)(2,1)} custom-call(s32[8]{0:T(128)S(1)} %stack.70.src_ref, bf16[320,1536]{1,0:T(8,128)(2,1)S(1)} %get-tuple-element.92.own_ref.x_own, bf16[320,1536]{1,0:T(8,128)(2,1)S(1)} %collective-permute-done.24.beside_ref.x_in, bf16[192,1536]{1,0:T(8,128)(2,1)S(1)} %get-tuple-element.93.y0_ref.y_own, ...), custom_call_target="tpu_custom_call" | custom-call | flops 49999998976 | bytes 6291456 | tf_op jit(solution)/shard_map/pallas_call | solution.py:425
  221.0 19.0 %collective-permute-done.32 = bf16[192,768]{1,0:T(8,128)(2,1)S(1)} collective-permute-done((bf16[192,768]{1,0:T(8,128)(2,1)S(1)}, bf16[192,768]{1,0:T(8,128)(2,1)S(1)}, u32[]{:S(2)}, u32[]{:S(2)}) %collective-permute-start.32) | collective-permute-done | bytes 294944 | tf_op jit(solution)/shard_map/ppermute | solution.py:60
  (132 shorter events, 72.6 us)
Async XLA Ops:
  7.2 174.7 %reduce-scatter.3.cloned.1.call-start = ((), (), s32[]{:S(2)}) async-start(), calls=%async_computation.2 | async-start | bytes 2949120 | tf_op jit(solution)/shard_map/reduce_scatter | solution.py:497
  14.2 25.1 %collective-permute-start.2 = (bf16[3,512,256]{2,1,0:T(8,128)(2,1)}, bf16[3,512,256]{2,1,0:T(8,128)(2,1)S(1)}, u32[]{:S(2)}, u32[]{:S(2)}) collective-permute-start(bf16[3,512,256]{2,1,0:T(8,128)(2,1)} %shard_map.75.o_ref), channel_id=1, source_target_pairs={{0,8},{8,0},{16,24},{24,16},{32,40},{40,32},{48,56},{56,48},{64,72... | collective-permute-start | bytes 2359304 | tf_op jit(solution)/shard_map/ppermute | solution.py:60
  14.2 20.3 %collective-permute-start.1 = (bf16[3,512,256]{2,1,0:T(8,128)(2,1)}, bf16[3,512,256]{2,1,0:T(8,128)(2,1)}, u32[]{:S(2)}, u32[]{:S(2)}) collective-permute-start(bf16[3,512,256]{2,1,0:T(8,128)(2,1)} %shard_map.75.o_ref), channel_id=1, source_target_pairs={{0,16},{8,120},{16,32},{24,8},{32,48},{40,24},{48,64},{56,40},{64,... | collective-permute-start | bytes 2359304 | tf_op jit(solution)/shard_map/ppermute | solution.py:60
  16.2 22.4 %collective-permute-start = (bf16[3,512,256]{2,1,0:T(8,128)(2,1)}, bf16[3,512,256]{2,1,0:T(8,128)(2,1)}, u32[]{:S(2)}, u32[]{:S(2)}) collective-permute-start(bf16[3,512,256]{2,1,0:T(8,128)(2,1)} %shard_map.75.o_ref), channel_id=1, source_target_pairs={{0,112},{8,24},{16,0},{24,40},{32,16},{40,56},{48,32},{56,72},{64,... | collective-permute-start | bytes 2359304 | tf_op jit(solution)/shard_map/ppermute | solution.py:60
  61.3 23.1 %collective-permute-start.5 = (bf16[3,512,256]{2,1,0:T(8,128)(2,1)}, bf16[3,512,256]{2,1,0:T(8,128)(2,1)}, u32[]{:S(2)}, u32[]{:S(2)}) collective-permute-start(bf16[3,512,256]{2,1,0:T(8,128)(2,1)} %get-tuple-element.60), channel_id=1, source_target_pairs={{0,112},{8,24},{16,0},{24,40},{32,16},{40,56},{48,32},{56,72},{64,... | collective-permute-start | bytes 2359304 | tf_op jit(solution)/shard_map/ppermute | solution.py:60
  69.9 19.4 %collective-permute-start.6 = (bf16[3,512,256]{2,1,0:T(8,128)(2,1)}, bf16[3,512,256]{2,1,0:T(8,128)(2,1)}, u32[]{:S(2)}, u32[]{:S(2)}) collective-permute-start(bf16[3,512,256]{2,1,0:T(8,128)(2,1)} %fusion.1), channel_id=1, source_target_pairs={{0,120},{8,16},{16,8},{24,32},{32,24},{40,48},{48,40},{56,64},{64,... | collective-permute-start | bytes 2359304 | tf_op jit(solution)/shard_map/ppermute | solution.py:60
  80.1 23.6 %collective-permute-start.9 = (bf16[128,2304]{1,0:T(8,128)(2,1)S(1)}, bf16[128,2304]{1,0:T(8,128)(2,1)S(1)}, u32[]{:S(2)}, u32[]{:S(2)}) collective-permute-start(bf16[128,2304]{1,0:T(8,128)(2,1)S(1)} %get-tuple-element.66), channel_id=1, source_target_pairs={{0,4},{1,5},{2,6},{3,7},{4,0},{5,1},{6,2},{7,3},{8,12},{9,13},{10,... | collective-permute-start | bytes 1769480 | tf_op jit(solution)/shard_map/ppermute | solution.py:64
  83.0 20.8 %collective-permute-start.10 = (bf16[128,2304]{1,0:T(8,128)(2,1)S(1)}, bf16[128,2304]{1,0:T(8,128)(2,1)S(1)}, u32[]{:S(2)}, u32[]{:S(2)}) collective-permute-start(bf16[128,2304]{1,0:T(8,128)(2,1)S(1)} %get-tuple-element.67), channel_id=1, source_target_pairs={{0,6},{1,7},{2,0},{3,1},{4,2},{5,3},{6,4},{7,5},{8,14},{9,15},{10,... | collective-permute-start | bytes 1769480 | tf_op jit(solution)/shard_map/ppermute | solution.py:64
  119.1 26.0 %collective-permute-start.13 = (bf16[352,1536]{1,0:T(8,128)(2,1)S(1)}, bf16[352,1536]{1,0:T(8,128)(2,1)}, u32[]{:S(2)}, u32[]{:S(2)}) collective-permute-start(bf16[352,1536]{1,0:T(8,128)(2,1)S(1)} %get-tuple-element.71._), channel_id=1, source_target_pairs={{0,1},{1,0},{2,3},{3,2},{4,5},{5,4},{6,7},{7,6},{8,9},{9,8},{10,11... | collective-permute-start | bytes 3244040 | tf_op jit(solution)/shard_map/ppermute | solution.py:64
  121.0 23.9 %collective-permute-start.15 = (bf16[160,1536]{1,0:T(8,128)(2,1)S(1)}, bf16[160,1536]{1,0:T(8,128)(2,1)}, u32[]{:S(2)}, u32[]{:S(2)}) collective-permute-start(bf16[160,1536]{1,0:T(8,128)(2,1)S(1)} %get-tuple-element.80), channel_id=1, source_target_pairs={{0,4},{1,5},{2,6},{3,7},{4,0},{5,1},{6,2},{7,3},{8,12},{9,13},{10,... | collective-permute-start | bytes 1474568 | tf_op jit(solution)/shard_map/ppermute | solution.py:64
  123.4 21.8 %collective-permute-start.16 = (bf16[160,1536]{1,0:T(8,128)(2,1)S(1)}, bf16[160,1536]{1,0:T(8,128)(2,1)}, u32[]{:S(2)}, u32[]{:S(2)}) collective-permute-start(bf16[160,1536]{1,0:T(8,128)(2,1)S(1)} %get-tuple-element.81), channel_id=1, source_target_pairs={{0,6},{1,7},{2,0},{3,1},{4,2},{5,3},{6,4},{7,5},{8,14},{9,15},{10,... | collective-permute-start | bytes 1474568 | tf_op jit(solution)/shard_map/ppermute | solution.py:64
  129.0 26.0 %collective-permute-start.18 = (bf16[2,512,384]{2,1,0:T(8,128)(2,1)S(1)}, bf16[2,512,384]{2,1,0:T(8,128)(2,1)}, u32[]{:S(2)}, u32[]{:S(2)}) collective-permute-start(bf16[2,512,384]{2,1,0:T(8,128)(2,1)S(1)} %copy-done.1), channel_id=1, source_target_pairs={{0,8},{8,0},{16,24},{24,16},{32,40},{40,32},{48,56},{56,48},{64,72... | collective-permute-start | bytes 2359304 | tf_op jit(solution)/shard_map/ppermute | solution.py:60
  136.6 66.8 %reduce-scatter.5.cloned.1.call-start = ((), (), s32[]{:S(2)}) async-start(), calls=%async_computation.3 | async-start | bytes 2949120 | tf_op jit(solution)/shard_map/reduce_scatter | solution.py:497
  136.7 18.7 %collective-permute-start.17 = (bf16[8,192,512]{2,1,0:T(8,128)(2,1)}, bf16[8,192,512]{2,1,0:T(8,128)(2,1)S(1)}, u32[]{:S(2)}, u32[]{:S(2)}) collective-permute-start(bf16[8,192,512]{2,1,0:T(8,128)(2,1)} %get-tuple-element.83), channel_id=1, source_target_pairs={{0,8},{8,0},{16,24},{24,16},{32,40},{40,32},{48,56},{56,48},{64,72... | collective-permute-start | bytes 4718600 | tf_op jit(solution)/shard_map/ppermute | solution.py:60
  176.6 33.1 %collective-permute-start.24 = (bf16[320,1536]{1,0:T(8,128)(2,1)S(1)}, bf16[320,1536]{1,0:T(8,128)(2,1)S(1)}, u32[]{:S(2)}, u32[]{:S(2)}) collective-permute-start(bf16[320,1536]{1,0:T(8,128)(2,1)S(1)} %get-tuple-element.92.own_ref.x_own), channel_id=1, source_target_pairs={{0,1},{1,0},{2,3},{3,2},{4,5},{5,4},{6,7},{7,6},{8,9},{9,8},{10,11... | collective-permute-start | bytes 2949128 | tf_op jit(solution)/shard_map/ppermute | solution.py:64
  178.1 30.6 %collective-permute-start.27 = (bf16[192,1536]{1,0:T(8,128)(2,1)S(1)}, bf16[192,1536]{1,0:T(8,128)(2,1)S(1)}, u32[]{:S(2)}, u32[]{:S(2)}) collective-permute-start(bf16[192,1536]{1,0:T(8,128)(2,1)S(1)} %get-tuple-element.93.y0_ref.y_own), channel_id=1, source_target_pairs={{0,6},{1,7},{2,0},{3,1},{4,2},{5,3},{6,4},{7,5},{8,14},{9,15},{10,... | collective-permute-start | bytes 1769480 | tf_op jit(solution)/shard_map/ppermute | solution.py:64
  180.7 28.0 %collective-permute-start.26 = (bf16[192,1536]{1,0:T(8,128)(2,1)S(1)}, bf16[192,1536]{1,0:T(8,128)(2,1)}, u32[]{:S(2)}, u32[]{:S(2)}) collective-permute-start(bf16[192,1536]{1,0:T(8,128)(2,1)S(1)} %get-tuple-element.93.y0_ref.y_own), channel_id=1, source_target_pairs={{0,4},{1,5},{2,6},{3,7},{4,0},{5,1},{6,2},{7,3},{8,12},{9,13},{10,... | collective-permute-start | bytes 1769480 | tf_op jit(solution)/shard_map/ppermute | solution.py:64
  181.8 27.8 %collective-permute-start.25 = (bf16[192,1536]{1,0:T(8,128)(2,1)S(1)}, bf16[192,1536]{1,0:T(8,128)(2,1)}, u32[]{:S(2)}, u32[]{:S(2)}) collective-permute-start(bf16[192,1536]{1,0:T(8,128)(2,1)S(1)} %get-tuple-element.93.y0_ref.y_own), channel_id=1, source_target_pairs={{0,2},{1,3},{2,4},{3,5},{4,6},{5,7},{6,0},{7,1},{8,10},{9,11},{10,... | collective-permute-start | bytes 1769480 | tf_op jit(solution)/shard_map/ppermute | solution.py:64
  182.8 24.7 %collective-permute-start.23 = (bf16[192,768]{1,0:T(8,128)(2,1)S(1)}, bf16[192,768]{1,0:T(8,128)(2,1)}, u32[]{:S(2)}, u32[]{:S(2)}) collective-permute-start(bf16[192,768]{1,0:T(8,128)(2,1)S(1)} %constant_dynamic-slice_fusion.1), channel_id=1, source_target_pairs={{0,64},{8,72},{16,80},{24,88},{32,96},{40,104},{48,112},{56,120},{... | collective-permute-start | bytes 884744 | tf_op jit(solution)/shard_map/ppermute | solution.py:60
  211.1 30.7 %collective-permute-start.31 = (bf16[128,1536]{1,0:T(8,128)(2,1)S(1)}, bf16[128,1536]{1,0:T(8,128)(2,1)S(1)}, u32[]{:S(2)}, u32[]{:S(2)}) collective-permute-start(bf16[128,1536]{1,0:T(8,128)(2,1)S(1)} %get-tuple-element.95.y0_ref), channel_id=1, source_target_pairs={{0,6},{1,7},{2,0},{3,1},{4,2},{5,3},{6,4},{7,5},{8,14},{9,15},{10,... | collective-permute-start | bytes 1179656 | tf_op jit(solution)/shard_map/ppermute | solution.py:64
  213.7 28.1 %collective-permute-start.30 = (bf16[128,1536]{1,0:T(8,128)(2,1)S(1)}, bf16[128,1536]{1,0:T(8,128)(2,1)S(1)}, u32[]{:S(2)}, u32[]{:S(2)}) collective-permute-start(bf16[128,1536]{1,0:T(8,128)(2,1)S(1)} %get-tuple-element.95.y0_ref), channel_id=1, source_target_pairs={{0,4},{1,5},{2,6},{3,7},{4,0},{5,1},{6,2},{7,3},{8,12},{9,13},{10,... | collective-permute-start | bytes 1179656 | tf_op jit(solution)/shard_map/ppermute | solution.py:64
  214.7 27.1 %collective-permute-start.29 = (bf16[128,1536]{1,0:T(8,128)(2,1)S(1)}, bf16[128,1536]{1,0:T(8,128)(2,1)S(1)}, u32[]{:S(2)}, u32[]{:S(2)}) collective-permute-start(bf16[128,1536]{1,0:T(8,128)(2,1)S(1)} %get-tuple-element.95.y0_ref), channel_id=1, source_target_pairs={{0,2},{1,3},{2,4},{3,5},{4,6},{5,7},{6,0},{7,1},{8,10},{9,11},{10,... | collective-permute-start | bytes 1179656 | tf_op jit(solution)/shard_map/ppermute | solution.py:64
  214.7 27.1 %collective-permute-start.28 = (bf16[256,1536]{1,0:T(8,128)(2,1)S(1)}, bf16[256,1536]{1,0:T(8,128)(2,1)S(1)}, u32[]{:S(2)}, u32[]{:S(2)}) collective-permute-start(bf16[256,1536]{1,0:T(8,128)(2,1)S(1)} %get-tuple-element.94.own_ref), channel_id=1, source_target_pairs={{0,1},{1,0},{2,3},{3,2},{4,5},{5,4},{6,7},{7,6},{8,9},{9,8},{10,11... | collective-permute-start | bytes 2359304 | tf_op jit(solution)/shard_map/ppermute | solution.py:64
  215.4 24.6 %collective-permute-start.32 = (bf16[192,768]{1,0:T(8,128)(2,1)S(1)}, bf16[192,768]{1,0:T(8,128)(2,1)S(1)}, u32[]{:S(2)}, u32[]{:S(2)}) collective-permute-start(bf16[192,768]{1,0:T(8,128)(2,1)S(1)} %constant_dynamic-slice_fusion), channel_id=1, source_target_pairs={{0,64},{8,72},{16,80},{24,88},{32,96},{40,104},{48,112},{56,120},{... | collective-permute-start | bytes 884744 | tf_op jit(solution)/shard_map/ppermute | solution.py:60
  (40 other events, 301.9 us)
Sparse Core Ops, SparseCore 0:
  136.7 32.0 reduce-scatter.2
  171.8 31.5 reduce-scatter.4

commit v4 on v3

--- a/solution.py
+++ b/solution.py
@@ -532,6 +532,7 @@
     mixed_near, mixed_far, mixed_y0, *mixed_y = mixed_product(dest, att_dq, w_out)
     mixed_x, mixed_y = exchange(mixed_far, mixed_y)
 
+    d_relay, _ = lax.optimization_barrier((d_relay, mixed_far))
     relay = (d_relay + back[0].astype(F32)).astype(BF)
     two = over_view(d_near, FAR)
     one = over_view(relay, BACK_ONE)

time: 252 us -> 250 us (level)
  starting transfers between devices: 50.1 us -> 47.1 us
    ppermute x13, waiting for transfers between devices: 33.8 us -> 42.6 us  [over_view(): return lax.ppermute(block, 'view', route)]
    ppermute x20, waiting for transfers between devices: 29.1 us -> 22.4 us  [over_head(): return lax.ppermute(block, 'head', head_route(*step))]
    ppermute x13, starting transfers between devices: 21.6 us -> 18.6 us  [over_view(): return lax.ppermute(block, 'view', route)]
  transfers between devices with their start and end apart: 35 -> 35, of which waited for: 14 -> 12; matrix products, arithmetic and copies ran while one was open for 7% -> 7% of each run, Pallas kernels for 13% -> 13%
where the time goes in v4:
time: 250 us; the launch traced here: 249 us
  waiting for transfers between devices  83 us (33%)
  Pallas kernels  70.4 us (28%)
  starting transfers between devices  47.1 us (19%)
  local copies, waits for them, and re-layouts  20.6 us (8%)
  between operations  14.3 us (6%)
  matrix products  8.67 us (3%)
  other arithmetic  5.11 us (2%)
    ppermute x13, waiting for transfers between devices, over_view(): return lax.ppermute(block, 'view', route)  42.6 us
    ppermute x20, starting transfers between devices, over_head(): return lax.ppermute(block, 'head', head_route(*step))  28.4 us
    ppermute x20, waiting for transfers between devices, over_head(): return lax.ppermute(block, 'head', head_route(*step))  22.4 us
    ppermute x13, starting transfers between devices, over_view(): return lax.ppermute(block, 'view', route)  18.6 us
    pallas_call x1, Pallas kernels, attention(): pl.pallas_call(attention_kernel, grid=(LH,), in_specs=[head_block, head_b...  18.5 us
    reduce_scatter x2, waiting for transfers between devices, weight_sum(): lax.psum_scatter(terms, 'view', scatter_dimension=0, axis_index_groups=Z_...  17.9 us
    unnamed x58, local copies, waits for them, and re-layouts  17.6 us
    pallas_call x2, Pallas kernels, weight_terms(): pl.pallas_call(functools.partial(weight_kernel, plan, len(lhs_pairs), len...  13.5 us
  transfers between devices with their start and end apart: 35, of which 12 were waited for; matrix products, arithmetic and copies ran while one was open for 7% of the time, Pallas kernels for 13%

profile of v4, /device:TPU:0, one launch (start us, length us, event | category | flops | bytes accessed | tf_op | source)
XLA Modules:
  0.0 249.1 jit_solution(17076048155027794995)
XLA Ops:
  7.2 7.0 %shard_map.75.o_ref = bf16[3,512,256]{2,1,0:T(8,128)(2,1)} custom-call(bf16[512,3072]{1,0:T(8,128)(2,1)} %x_ref.4, bf16[3,3072,384]{2,1,0:T(8,128)(2,1)} %bitcast.44, bf16[3,3072,384]{2,1,0:T(8,128)(2,1)} %bitcast.45), custom_call_target="tpu_custom_call" | custom-call | flops 2415919104 | bytes 9437184 | tf_op jit(solution)/shard_map/pallas_call | solution.py:88
  16.2 4.7 %collective-permute-start = (bf16[3,512,256]{2,1,0:T(8,128)(2,1)}, bf16[3,512,256]{2,1,0:T(8,128)(2,1)}, u32[]{:S(2)}, u32[]{:S(2)}) collective-permute-start(bf16[3,512,256]{2,1,0:T(8,128)(2,1)} %shard_map.75.o_ref), channel_id=1, source_target_pairs={{0,112},{8,24},{16,0},{24,40},{32,16},{40,56},{48,32},{56,72},{64,... | collective-permute-start | bytes 2359304 | tf_op jit(solution)/shard_map/ppermute | solution.py:60
  20.9 4.5 %convolution_convert_fusion._.g_ref = bf16[512,384]{1,0:T(8,128)(2,1)} fusion(bf16[512,3072]{1,0:T(8,128)(2,1)} %x_ref.5, bf16[3072,384]{1,0:T(8,128)(2,1)S(1)} %copy-done.5), kind=kOutput, calls=%fused_computation.9 | convolution fusion | flops 1208156160 | bytes 5898240 | tf_op jit(solution)/shard_map/dot_general | solution.py:522
  25.3 3.8 %shard_map.76 = (bf16[8,192,512]{2,1,0:T(8,128)(2,1)}, bf16[8,192,512]{2,1,0:T(8,128)(2,1)}) custom-call(s32[1]{0:T(128)} %bitcast.16.core_ref, bf16[512,3072]{1,0:T(8,128)(2,1)} %x_ref.4, bf16[512,384]{1,0:T(8,128)(2,1)} %convolution_convert_fusion._.g_ref), custom_call_target="tpu_custom_call" | custom-call | flops 100663296 | bytes 6291456 | tf_op jit(solution)/shard_map/pallas_call | solution.py:450
  29.2 4.2 %fusion.5.q_ref = bf16[512,384]{1,0:T(8,128)(2,1)} fusion(bf16[512,3072]{1,0:T(8,128)(2,1)S(1)} %copy-done.19, bf16[3,3072,384]{2,1,0:T(8,128)(2,1)} %bitcast.46), kind=kOutput, calls=%fused_computation.8 | convolution fusion | flops 1208156160 | bytes 5898240 | tf_op jit(solution)/shard_map/dot_general | solution.py:521
  34.5 4.1 %collective-permute-done.b_ref = bf16[3,512,256]{2,1,0:T(8,128)(2,1)} collective-permute-done((bf16[3,512,256]{2,1,0:T(8,128)(2,1)}, bf16[3,512,256]{2,1,0:T(8,128)(2,1)}, u32[]{:S(2)}, u32[]{:S(2)}) %collective-permute-start) | collective-permute-done | bytes 786464 | tf_op jit(solution)/shard_map/ppermute | solution.py:60
  42.4 18.5 %shard_map.77 = (bf16[2,512,384]{2,1,0:T(8,128)(2,1)}, f32[3,512,256]{2,1,0:T(8,128)}, bf16[3,512,256]{2,1,0:T(8,128)(2,1)}, bf16[2,3,512,256]{3,2,1,0:T(8,128)(2,1)}, f32[3,512,256]{2,1,0:T(8,128)}) custom-call(bf16[512,384]{1,0:T(8,128)(2,1)} %fusion.5.q_ref, bf16[512,384]{1,0:T(8,128)(2,1)} %convolution_convert_fusion._.g_ref, ...), custom_call_target="tpu_custom_call" | custom-call | flops 12079595520 | bytes 12582912 | tf_op jit(solution)/shard_map/pallas_call | solution.py:155
  61.3 5.7 %collective-permute-start.5 = (bf16[3,512,256]{2,1,0:T(8,128)(2,1)}, bf16[3,512,256]{2,1,0:T(8,128)(2,1)S(1)}, u32[]{:S(2)}, u32[]{:S(2)}) collective-permute-start(bf16[3,512,256]{2,1,0:T(8,128)(2,1)} %get-tuple-element.61), channel_id=1, source_target_pairs={{0,112},{8,24},{16,0},{24,40},{32,16},{40,56},{48,32},{56,72},{64,... | collective-permute-start | bytes 2359304 | tf_op jit(solution)/shard_map/ppermute | solution.py:60
  69.8 3.6 %shard_map.78 = (bf16[256,768]{1,0:T(8,128)(2,1)S(1)}, bf16[256,768]{1,0:T(8,128)(2,1)S(1)}, bf16[128,2304]{1,0:T(8,128)(2,1)S(1)}, bf16[128,2304]{1,0:T(8,128)(...) custom-call(s32[8]{0:T(128)S(1)} %stack.77.dest_ref, bf16[2,512,384]{2,1,0:T(8,128)(2,1)S(1)} %copy-done.1, ...), custom_call_target="tpu_custom_call" | custom-call | flops 1207959552 | bytes 5505024 | tf_op jit(solution)/shard_map/pallas_call | solution.py:222
  76.6 2.9 %collective-permute-start.9 = (bf16[128,2304]{1,0:T(8,128)(2,1)S(1)}, bf16[128,2304]{1,0:T(8,128)(2,1)S(1)}, u32[]{:S(2)}, u32[]{:S(2)}) collective-permute-start(bf16[128,2304]{1,0:T(8,128)(2,1)S(1)} %get-tuple-element.68), channel_id=1, source_target_pairs={{0,4},{1,5},{2,6},{3,7},{4,0},{5,1},{6,2},{7,3},{8,12},{9,13},{10,... | collective-permute-start | bytes 1769480 | tf_op jit(solution)/shard_map/ppermute | solution.py:64
  81.4 12.7 %collective-permute-done.6 = bf16[3,512,256]{2,1,0:T(8,128)(2,1)S(1)} collective-permute-done((bf16[3,512,256]{2,1,0:T(8,128)(2,1)S(1)}, bf16[3,512,256]{2,1,0:T(8,128)(2,1)S(1)}, u32[]{:S(2)}, u32[]{:S(2)}) %collective-permute-start.6) | collective-permute-done | bytes 786464 | tf_op jit(solution)/shard_map/ppermute | solution.py:60
  95.7 6.1 %collective-permute-done.9.refs_7_.refs_11_ = bf16[128,2304]{1,0:T(8,128)(2,1)S(1)} collective-permute-done((bf16[128,2304]{1,0:T(8,128)(2,1)S(1)}, bf16[128,2304]{1,0:T(8,128)(2,1)S(1)}, u32[]{:S(2)}, u32[]{:S(2)}) %collective-permute-start.9) | collective-permute-done | bytes 589856 | tf_op jit(solution)/shard_map/ppermute | solution.py:64
  101.9 3.0 %copy-done = bf16[3072,3,384]{2,0,1:T(8,128)(2,1)S(1)} copy-done((bf16[3072,3,384]{2,0,1:T(8,128)(2,1)S(1)}, bf16[3072,3,384]{2,0,1:T(8,128)(2,1)}, u32[]{:S(2)}) %copy-start) | copy-done | bytes 7077912
  104.9 8.6 %shard_map.79 = (bf16[256,1536]{1,0:T(8,128)(2,1)S(1)}, bf16[128,1536]{1,0:T(8,128)(2,1)S(1)}, f32[64,768]{1,0:T(8,128)S(1)}, f32[64,2304]{1,0:T(8,128)S(1)}, bf...) custom-call(s32[8]{0:T(128)S(1)} %stack.77.dest_ref, ...), custom_call_target="tpu_custom_call" | custom-call | flops 3623878656 | bytes 13369344 | tf_op jit(solution)/shard_map/pallas_call | solution.py:296
  123.3 3.6 %shard_map.81 = (bf16[8,192,512]{2,1,0:T(8,128)(2,1)}, bf16[8,192,512]{2,1,0:T(8,128)(2,1)}) custom-call(s32[1]{0:T(128)} %bitcast.16.core_ref, bf16[512,3072]{1,0:T(8,128)(2,1)} %x_ref.5, bf16[352,1536]{1,0:T(8,128)(2,1)} %copy-done.4), custom_call_target="tpu_custom_call" | custom-call | flops 100663296 | bytes 6291456 | tf_op jit(solution)/shard_map/pallas_call | solution.py:450
  128.2 6.5 %shard_map.80 = bf16[1536,768]{1,0:T(8,128)(2,1)} custom-call(bf16[2,4,192,512]{3,2,1,0:T(8,128)(2,1)} %bitcast.48, bf16[2,4,192,512]{3,2,1,0:T(8,128)(2,1)} %bitcast.50, bf16[3,512,256]{2,1,0:T(8,128)(2,1)} %copy-done.3, bf16[3,512,256]{2,1,0:T(8,128)(2,1)} %copy-done.27), custom_call_target="tpu_custom_call" | custom-call | flops 2415919104 | bytes 10485760 | tf_op jit(solution)/shard_map/pallas_call | solution.py:481
  134.8 8.2 %collective-permute-done.15.y2_in = bf16[160,1536]{1,0:T(8,128)(2,1)} collective-permute-done((bf16[160,1536]{1,0:T(8,128)(2,1)S(1)}, bf16[160,1536]{1,0:T(8,128)(2,1)}, u32[]{:S(2)}, u32[]{:S(2)}) %collective-permute-start.15) | collective-permute-done | bytes 491552 | tf_op jit(solution)/shard_map/ppermute | solution.py:64
  143.3 3.9 %shard_map.82 = (f32[64,1536]{1,0:T(8,128)}, f32[64,1536]{1,0:T(8,128)}, bf16[128,1536]{1,0:T(8,128)(2,1)}, bf16[128,1536]{1,0:T(8,128)(2,1)}, bf16[128,1536]{1,0:T(8,128)(2,1)}, /*index=5*/bf16[128,1536]{1,0:T(8,128)(2,1)}) custom-call(bf16[256,1536]{1,0:T(8,128)(2,1)} %copy-done.7, bf16[128,1536]{1,0:T(8,128)(2,1)} %copy-done.9, f32[64,768]{1,0:T(8,128)} %copy-done.16, ...), custom_call_target="tpu_custom_call" | custom-call | flops 49999998976 | bytes 4194304 | tf_op jit(solution)/shard_map/pallas_call | solution.py:387
  154.6 7.0 %shard_map.83 = bf16[1536,768]{1,0:T(8,128)(2,1)} custom-call(bf16[2,4,192,512]{3,2,1,0:T(8,128)(2,1)} %bitcast.49, bf16[2,4,192,512]{3,2,1,0:T(8,128)(2,1)} %bitcast.51, bf16[2,4,192,512]{3,2,1,0:T(8,128)(2,1)} %bitcast.52, bf16[2,4,192,512]{3,2,1,0:T(8,128)(2,1)} %bitcast.53, bf16[2,512,384]{2,1,0:T(8,128)(2,1)} %get-tuple-element.86.att_ref.refs_0_.refs_4_, ...), custom_call_target="tpu_custom_call" | custom-call | flops 2415919104 | bytes 10485760 | tf_op jit(solution)/shard_map/pallas_call | solution.py:481
  161.6 6.9 %collective-permute-done.22.y3_in = bf16[128,1536]{1,0:T(8,128)(2,1)S(1)} collective-permute-done((bf16[128,1536]{1,0:T(8,128)(2,1)}, bf16[128,1536]{1,0:T(8,128)(2,1)S(1)}, u32[]{:S(2)}, u32[]{:S(2)}) %collective-permute-start.22) | collective-permute-done | bytes 393248 | tf_op jit(solution)/shard_map/ppermute | solution.py:64
  183.4 17.9 %reduce-scatter.5.cloned.1.call-done = bf16[384,768]{1,0:T(8,128)(2,1)} async-done(((bf16[1536,768]{1,0:T(8,128)(2,1)}), bf16[384,768]{1,0:T(8,128)(2,1)}) %reduce-scatter.5.cloned.1.call-update) | async-done | bytes 589840 | tf_op jit(solution)/shard_map/reduce_scatter | solution.py:497
  202.3 3.4 %collective-permute-done.23 = bf16[192,768]{1,0:T(8,128)(2,1)} collective-permute-done((bf16[192,768]{1,0:T(8,128)(2,1)S(1)}, bf16[192,768]{1,0:T(8,128)(2,1)}, u32[]{:S(2)}, u32[]{:S(2)}) %collective-permute-start.23) | collective-permute-done | bytes 294944 | tf_op jit(solution)/shard_map/ppermute | solution.py:60
  215.4 3.6 %shard_map.85 = bf16[512,3072]{1,0:T(8,128)(2,1)} custom-call(s32[8]{0:T(128)S(1)} %stack.70.src_ref, bf16[320,1536]{1,0:T(8,128)(2,1)S(1)} %get-tuple-element.94.own_ref.x_own, bf16[320,1536]{1,0:T(8,128)(2,1)S(1)} %collective-permute-done.24.beside_ref.x_in, bf16[192,1536]{1,0:T(8,128)(2,1)S(1)} %get-tuple-element.95.y0_ref.y_own, ...), custom_call_target="tpu_custom_call" | custom-call | flops 49999998976 | bytes 6291456 | tf_op jit(solution)/shard_map/pallas_call | solution.py:425
  219.0 19.1 %collective-permute-done.32 = bf16[192,768]{1,0:T(8,128)(2,1)S(1)} collective-permute-done((bf16[192,768]{1,0:T(8,128)(2,1)S(1)}, bf16[192,768]{1,0:T(8,128)(2,1)S(1)}, u32[]{:S(2)}, u32[]{:S(2)}) %collective-permute-start.32) | collective-permute-done | bytes 294944 | tf_op jit(solution)/shard_map/ppermute | solution.py:60
  (132 shorter events, 65.4 us)
Async XLA Ops:
  7.2 172.7 %reduce-scatter.3.cloned.1.call-start = ((), (), s32[]{:S(2)}) async-start(), calls=%async_computation.2 | async-start | bytes 2949120 | tf_op jit(solution)/shard_map/reduce_scatter | solution.py:497
  14.2 25.1 %collective-permute-start.2 = (bf16[3,512,256]{2,1,0:T(8,128)(2,1)}, bf16[3,512,256]{2,1,0:T(8,128)(2,1)S(1)}, u32[]{:S(2)}, u32[]{:S(2)}) collective-permute-start(bf16[3,512,256]{2,1,0:T(8,128)(2,1)} %shard_map.75.o_ref), channel_id=1, source_target_pairs={{0,8},{8,0},{16,24},{24,16},{32,40},{40,32},{48,56},{56,48},{64,72... | collective-permute-start | bytes 2359304 | tf_op jit(solution)/shard_map/ppermute | solution.py:60
  14.2 20.3 %collective-permute-start.1 = (bf16[3,512,256]{2,1,0:T(8,128)(2,1)}, bf16[3,512,256]{2,1,0:T(8,128)(2,1)}, u32[]{:S(2)}, u32[]{:S(2)}) collective-permute-start(bf16[3,512,256]{2,1,0:T(8,128)(2,1)} %shard_map.75.o_ref), channel_id=1, source_target_pairs={{0,16},{8,120},{16,32},{24,8},{32,48},{40,24},{48,64},{56,40},{64,... | collective-permute-start | bytes 2359304 | tf_op jit(solution)/shard_map/ppermute | solution.py:60
  16.2 22.4 %collective-permute-start = (bf16[3,512,256]{2,1,0:T(8,128)(2,1)}, bf16[3,512,256]{2,1,0:T(8,128)(2,1)}, u32[]{:S(2)}, u32[]{:S(2)}) collective-permute-start(bf16[3,512,256]{2,1,0:T(8,128)(2,1)} %shard_map.75.o_ref), channel_id=1, source_target_pairs={{0,112},{8,24},{16,0},{24,40},{32,16},{40,56},{48,32},{56,72},{64,... | collective-permute-start | bytes 2359304 | tf_op jit(solution)/shard_map/ppermute | solution.py:60
  61.3 19.5 %collective-permute-start.5 = (bf16[3,512,256]{2,1,0:T(8,128)(2,1)}, bf16[3,512,256]{2,1,0:T(8,128)(2,1)S(1)}, u32[]{:S(2)}, u32[]{:S(2)}) collective-permute-start(bf16[3,512,256]{2,1,0:T(8,128)(2,1)} %get-tuple-element.61), channel_id=1, source_target_pairs={{0,112},{8,24},{16,0},{24,40},{32,16},{40,56},{48,32},{56,72},{64,... | collective-permute-start | bytes 2359304 | tf_op jit(solution)/shard_map/ppermute | solution.py:60
  74.8 19.3 %collective-permute-start.6 = (bf16[3,512,256]{2,1,0:T(8,128)(2,1)S(1)}, bf16[3,512,256]{2,1,0:T(8,128)(2,1)S(1)}, u32[]{:S(2)}, u32[]{:S(2)}) collective-permute-start(bf16[3,512,256]{2,1,0:T(8,128)(2,1)S(1)} %fusion.1), channel_id=1, source_target_pairs={{0,120},{8,16},{16,8},{24,32},{32,24},{40,48},{48,40},{56,64},{64,... | collective-permute-start | bytes 2359304 | tf_op jit(solution)/shard_map/ppermute | solution.py:60
  74.9 20.8 %collective-permute-start.8 = (bf16[128,2304]{1,0:T(8,128)(2,1)S(1)}, bf16[128,2304]{1,0:T(8,128)(2,1)S(1)}, u32[]{:S(2)}, u32[]{:S(2)}) collective-permute-start(bf16[128,2304]{1,0:T(8,128)(2,1)S(1)} %get-tuple-element.67), channel_id=1, source_target_pairs={{0,2},{1,3},{2,4},{3,5},{4,6},{5,7},{6,0},{7,1},{8,10},{9,11},{10,... | collective-permute-start | bytes 1769480 | tf_op jit(solution)/shard_map/ppermute | solution.py:64
  76.6 25.3 %collective-permute-start.9 = (bf16[128,2304]{1,0:T(8,128)(2,1)S(1)}, bf16[128,2304]{1,0:T(8,128)(2,1)S(1)}, u32[]{:S(2)}, u32[]{:S(2)}) collective-permute-start(bf16[128,2304]{1,0:T(8,128)(2,1)S(1)} %get-tuple-element.68), channel_id=1, source_target_pairs={{0,4},{1,5},{2,6},{3,7},{4,0},{5,1},{6,2},{7,3},{8,12},{9,13},{10,... | collective-permute-start | bytes 1769480 | tf_op jit(solution)/shard_map/ppermute | solution.py:64
  79.5 22.4 %collective-permute-start.10 = (bf16[128,2304]{1,0:T(8,128)(2,1)S(1)}, bf16[128,2304]{1,0:T(8,128)(2,1)S(1)}, u32[]{:S(2)}, u32[]{:S(2)}) collective-permute-start(bf16[128,2304]{1,0:T(8,128)(2,1)S(1)} %get-tuple-element.69), channel_id=1, source_target_pairs={{0,6},{1,7},{2,0},{3,1},{4,2},{5,3},{6,4},{7,5},{8,14},{9,15},{10,... | collective-permute-start | bytes 1769480 | tf_op jit(solution)/shard_map/ppermute | solution.py:64
  117.3 26.0 %collective-permute-start.13 = (bf16[352,1536]{1,0:T(8,128)(2,1)S(1)}, bf16[352,1536]{1,0:T(8,128)(2,1)}, u32[]{:S(2)}, u32[]{:S(2)}) collective-permute-start(bf16[352,1536]{1,0:T(8,128)(2,1)S(1)} %get-tuple-element.73._), channel_id=1, source_target_pairs={{0,1},{1,0},{2,3},{3,2},{4,5},{5,4},{6,7},{7,6},{8,9},{9,8},{10,11... | collective-permute-start | bytes 3244040 | tf_op jit(solution)/shard_map/ppermute | solution.py:64
  119.0 23.9 %collective-permute-start.15 = (bf16[160,1536]{1,0:T(8,128)(2,1)S(1)}, bf16[160,1536]{1,0:T(8,128)(2,1)}, u32[]{:S(2)}, u32[]{:S(2)}) collective-permute-start(bf16[160,1536]{1,0:T(8,128)(2,1)S(1)} %get-tuple-element.82), channel_id=1, source_target_pairs={{0,4},{1,5},{2,6},{3,7},{4,0},{5,1},{6,2},{7,3},{8,12},{9,13},{10,... | collective-permute-start | bytes 1474568 | tf_op jit(solution)/shard_map/ppermute | solution.py:64
  121.4 21.9 %collective-permute-start.16 = (bf16[160,1536]{1,0:T(8,128)(2,1)S(1)}, bf16[160,1536]{1,0:T(8,128)(2,1)}, u32[]{:S(2)}, u32[]{:S(2)}) collective-permute-start(bf16[160,1536]{1,0:T(8,128)(2,1)S(1)} %get-tuple-element.83), channel_id=1, source_target_pairs={{0,6},{1,7},{2,0},{3,1},{4,2},{5,3},{6,4},{7,5},{8,14},{9,15},{10,... | collective-permute-start | bytes 1474568 | tf_op jit(solution)/shard_map/ppermute | solution.py:64
  127.0 26.1 %collective-permute-start.18 = (bf16[2,512,384]{2,1,0:T(8,128)(2,1)S(1)}, bf16[2,512,384]{2,1,0:T(8,128)(2,1)}, u32[]{:S(2)}, u32[]{:S(2)}) collective-permute-start(bf16[2,512,384]{2,1,0:T(8,128)(2,1)S(1)} %copy-done.2), channel_id=1, source_target_pairs={{0,8},{8,0},{16,24},{24,16},{32,40},{40,32},{48,56},{56,48},{64,72... | collective-permute-start | bytes 2359304 | tf_op jit(solution)/shard_map/ppermute | solution.py:60
  134.6 66.7 %reduce-scatter.5.cloned.1.call-start = ((), (), s32[]{:S(2)}) async-start(), calls=%async_computation.3 | async-start | bytes 2949120 | tf_op jit(solution)/shard_map/reduce_scatter | solution.py:497
  174.6 33.1 %collective-permute-start.24 = (bf16[320,1536]{1,0:T(8,128)(2,1)S(1)}, bf16[320,1536]{1,0:T(8,128)(2,1)S(1)}, u32[]{:S(2)}, u32[]{:S(2)}) collective-permute-start(bf16[320,1536]{1,0:T(8,128)(2,1)S(1)} %get-tuple-element.94.own_ref.x_own), channel_id=1, source_target_pairs={{0,1},{1,0},{2,3},{3,2},{4,5},{5,4},{6,7},{7,6},{8,9},{9,8},{10,11... | collective-permute-start | bytes 2949128 | tf_op jit(solution)/shard_map/ppermute | solution.py:64
  176.1 30.7 %collective-permute-start.27 = (bf16[192,1536]{1,0:T(8,128)(2,1)S(1)}, bf16[192,1536]{1,0:T(8,128)(2,1)S(1)}, u32[]{:S(2)}, u32[]{:S(2)}) collective-permute-start(bf16[192,1536]{1,0:T(8,128)(2,1)S(1)} %get-tuple-element.95.y0_ref.y_own), channel_id=1, source_target_pairs={{0,6},{1,7},{2,0},{3,1},{4,2},{5,3},{6,4},{7,5},{8,14},{9,15},{10,... | collective-permute-start | bytes 1769480 | tf_op jit(solution)/shard_map/ppermute | solution.py:64
  178.7 28.1 %collective-permute-start.26 = (bf16[192,1536]{1,0:T(8,128)(2,1)S(1)}, bf16[192,1536]{1,0:T(8,128)(2,1)}, u32[]{:S(2)}, u32[]{:S(2)}) collective-permute-start(bf16[192,1536]{1,0:T(8,128)(2,1)S(1)} %get-tuple-element.95.y0_ref.y_own), channel_id=1, source_target_pairs={{0,4},{1,5},{2,6},{3,7},{4,0},{5,1},{6,2},{7,3},{8,12},{9,13},{10,... | collective-permute-start | bytes 1769480 | tf_op jit(solution)/shard_map/ppermute | solution.py:64
  179.9 27.8 %collective-permute-start.25 = (bf16[192,1536]{1,0:T(8,128)(2,1)S(1)}, bf16[192,1536]{1,0:T(8,128)(2,1)}, u32[]{:S(2)}, u32[]{:S(2)}) collective-permute-start(bf16[192,1536]{1,0:T(8,128)(2,1)S(1)} %get-tuple-element.95.y0_ref.y_own), channel_id=1, source_target_pairs={{0,2},{1,3},{2,4},{3,5},{4,6},{5,7},{6,0},{7,1},{8,10},{9,11},{10,... | collective-permute-start | bytes 1769480 | tf_op jit(solution)/shard_map/ppermute | solution.py:64
  180.9 24.9 %collective-permute-start.23 = (bf16[192,768]{1,0:T(8,128)(2,1)S(1)}, bf16[192,768]{1,0:T(8,128)(2,1)}, u32[]{:S(2)}, u32[]{:S(2)}) collective-permute-start(bf16[192,768]{1,0:T(8,128)(2,1)S(1)} %constant_dynamic-slice_fusion.1), channel_id=1, source_target_pairs={{0,64},{8,72},{16,80},{24,88},{32,96},{40,104},{48,112},{56,120},{... | collective-permute-start | bytes 884744 | tf_op jit(solution)/shard_map/ppermute | solution.py:60
  209.1 30.8 %collective-permute-start.31 = (bf16[128,1536]{1,0:T(8,128)(2,1)S(1)}, bf16[128,1536]{1,0:T(8,128)(2,1)S(1)}, u32[]{:S(2)}, u32[]{:S(2)}) collective-permute-start(bf16[128,1536]{1,0:T(8,128)(2,1)S(1)} %get-tuple-element.97.y0_ref), channel_id=1, source_target_pairs={{0,6},{1,7},{2,0},{3,1},{4,2},{5,3},{6,4},{7,5},{8,14},{9,15},{10,... | collective-permute-start | bytes 1179656 | tf_op jit(solution)/shard_map/ppermute | solution.py:64
  211.8 28.0 %collective-permute-start.30 = (bf16[128,1536]{1,0:T(8,128)(2,1)S(1)}, bf16[128,1536]{1,0:T(8,128)(2,1)S(1)}, u32[]{:S(2)}, u32[]{:S(2)}) collective-permute-start(bf16[128,1536]{1,0:T(8,128)(2,1)S(1)} %get-tuple-element.97.y0_ref), channel_id=1, source_target_pairs={{0,4},{1,5},{2,6},{3,7},{4,0},{5,1},{6,2},{7,3},{8,12},{9,13},{10,... | collective-permute-start | bytes 1179656 | tf_op jit(solution)/shard_map/ppermute | solution.py:64
  212.9 26.9 %collective-permute-start.29 = (bf16[128,1536]{1,0:T(8,128)(2,1)S(1)}, bf16[128,1536]{1,0:T(8,128)(2,1)S(1)}, u32[]{:S(2)}, u32[]{:S(2)}) collective-permute-start(bf16[128,1536]{1,0:T(8,128)(2,1)S(1)} %get-tuple-element.97.y0_ref), channel_id=1, source_target_pairs={{0,2},{1,3},{2,4},{3,5},{4,6},{5,7},{6,0},{7,1},{8,10},{9,11},{10,... | collective-permute-start | bytes 1179656 | tf_op jit(solution)/shard_map/ppermute | solution.py:64
  213.0 26.9 %collective-permute-start.28 = (bf16[256,1536]{1,0:T(8,128)(2,1)S(1)}, bf16[256,1536]{1,0:T(8,128)(2,1)S(1)}, u32[]{:S(2)}, u32[]{:S(2)}) collective-permute-start(bf16[256,1536]{1,0:T(8,128)(2,1)S(1)} %get-tuple-element.96.own_ref), channel_id=1, source_target_pairs={{0,1},{1,0},{2,3},{3,2},{4,5},{5,4},{6,7},{7,6},{8,9},{9,8},{10,11... | collective-permute-start | bytes 2359304 | tf_op jit(solution)/shard_map/ppermute | solution.py:64
  213.5 24.6 %collective-permute-start.32 = (bf16[192,768]{1,0:T(8,128)(2,1)S(1)}, bf16[192,768]{1,0:T(8,128)(2,1)S(1)}, u32[]{:S(2)}, u32[]{:S(2)}) collective-permute-start(bf16[192,768]{1,0:T(8,128)(2,1)S(1)} %constant_dynamic-slice_fusion), channel_id=1, source_target_pairs={{0,64},{8,72},{16,80},{24,88},{32,96},{40,104},{48,112},{56,120},{... | collective-permute-start | bytes 884744 | tf_op jit(solution)/shard_map/ppermute | solution.py:60
  (40 other events, 303.2 us)
Sparse Core Ops, SparseCore 0:
  134.8 31.8 reduce-scatter.2
  169.7 31.6 reduce-scatter.4
